TPU v7x, 32 devices: a whole 2x2x4 slice. The times are simulated.
32 devices in a mesh: row: 4 (over z), col: 8 (over y, x, core).
Axes of the slice: x: 2, y: 2, z: 4, core: 2. Of those that a mesh axis runs over, the one named last changes fastest.
Arguments:
- hidden_in: bfloat16 [8192, 1536], P(('row', 'col')), may hold values from -6 to 6
- routes: int32 [2, 8192, 4], P(None, ('row', 'col')), may hold values from 0 to 31, all different within a row
- norm_attn: bfloat16 [2, 1536], replicated, may hold values from 0.099609375 to 1.8984375
- w_qkv: bfloat16 [2, 1536, 2048], P(None, 'row', 'col'), may hold values from -0.15625 to 0.15625
- w_out: bfloat16 [2, 1536, 1536], P(None, 'row', 'col'), may hold values from -2.5 to 2.5
- norm_moe: bfloat16 [2, 1536], replicated, may hold values from 0.099609375 to 1.8984375
- w_router: bfloat16 [2, 1536, 32], P(None, 'row'), may hold values from -0.078125 to 0.078125
- w_gate: bfloat16 [2, 32, 1536, 768], P(None, 'col', None, 'row'), may hold values from -0.15625 to 0.15625
- w_up: bfloat16 [2, 32, 1536, 768], P(None, 'col', None, 'row'), may hold values from -0.15625 to 0.15625
- w_down: bfloat16 [2, 32, 768, 1536], P(None, 'col', 'row'), may hold values from -0.4375 to 0.4375
- cotangent: bfloat16 [8192, 1536], P(('row', 'col')), may hold values from -6 to 6
Outputs:
- block_out: float32 [8192, 1536], P(('row', 'col'))
- grad_in: float32 [8192, 1536], P(('row', 'col'))
- grad_norm_attn: float32 [2, 1536], P(None, ('row', 'col'))
- grad_qkv: float32 [2, 1536, 2048], P(None, 'row', 'col')
- grad_out: float32 [2, 1536, 1536], P(None, 'row', 'col')
- grad_norm_moe: float32 [2, 1536], P(None, ('row', 'col'))
- grad_router: float32 [2, 1536, 32], P(None, ('row', 'col'))
- grad_gate: float32 [2, 32, 1536, 768], P(None, 'col', None, 'row')
- grad_up: float32 [2, 32, 1536, 768], P(None, 'col', None, 'row')
- grad_down: float32 [2, 32, 768, 1536], P(None, 'col', 'row')
All inputs are finite; a program needn't handle non-finite values.
Results may differ from a plain program's by a relative error of at most 0.025.
Values may be sent and summed in bfloat16 or wider, within the bound.
A program may use at most 448 MiB of HBM per device.

v0:
```python
import jax
import jax.numpy as jnp
from jax import lax
from jax.sharding import PartitionSpec as P

QUERY_HEADS = 12
KEY_VALUE_HEADS = 2
HEAD_SIZE = 128
E = 32
TOPK = 4
BLOCK = 256
QUERY_FEATURES = 1536
CAP = 36


eps_norm = 1e-06
rope_base = 1000000.0
masked_score = -1e30
highest = lax.Precision.HIGHEST
wide_type = jnp.float32
narrow_type = jnp.bfloat16


def rms_parts(values, gain_vec):
    inverse = lax.rsqrt(jnp.mean(values * values, axis=-1, keepdims=True) + eps_norm)
    return (values * inverse * gain_vec, inverse)


def rms_backward(values, inverse, gain_vec, incoming):
    scaled = incoming * gain_vec
    inner_mean = jnp.mean(scaled * values, axis=-1, keepdims=True)
    grad_values = inverse * scaled - values * (inverse * inverse * inverse) * inner_mean
    grad_gain = jnp.sum(incoming * values * inverse, axis=0)
    return (grad_values, grad_gain)


def rope_angles(positions, half_dim):
    frequency = rope_base ** (-jnp.arange(half_dim, dtype=jnp.float32) / half_dim)
    angles = positions.astype(jnp.float32)[:, None] * frequency[None, :]
    return (jnp.cos(angles), jnp.sin(angles))


def rotate_heads(values, cosine_table, sine_table_rows, direction):
    half_dim = values.shape[-1] // 2
    first_half = values[..., :half_dim]
    second_half = values[..., half_dim:]
    cos_rows = cosine_table[:, None, :]
    sin_rows = direction * sine_table_rows[:, None, :]
    return jnp.concatenate(
        [
            first_half * cos_rows - second_half * sin_rows,
            second_half * cos_rows + first_half * sin_rows,
        ],
        axis=-1,
    )


def slot_table(route_rows):
    groups = route_rows.shape[0]
    onehot = (route_rows[..., None] == jnp.arange(E, dtype=jnp.int32)).astype(jnp.int32)
    flat_pairs = onehot.reshape(groups, -1, E)
    before = jnp.cumsum(flat_pairs, axis=1) - flat_pairs
    slot_number = jnp.sum(before * flat_pairs, axis=-1).reshape(route_rows.shape)
    usable = slot_number < CAP
    target = route_rows * CAP + jnp.minimum(slot_number, CAP - 1)
    return (target, usable)


def slot_owner(target, usable):
    pair_ids = jnp.arange(target.size, dtype=jnp.int32)
    slot_ids = jnp.arange(E * CAP, dtype=jnp.int32)
    matches = (target.reshape(-1)[None, :] == slot_ids[:, None]) & usable.reshape(-1)[None, :]
    occupied = jnp.any(matches, axis=1)
    owner_pair = jnp.sum(jnp.where(matches, pair_ids[None, :], 0), axis=1)
    return (owner_pair, occupied)


def to_full(gathered, row_count, col_count):
    height = gathered.shape[1]
    breadth = gathered.shape[2]
    return (
        gathered.reshape(row_count, col_count, height, breadth)
        .transpose(0, 2, 1, 3)
        .reshape(row_count * height, col_count * breadth)
    )


def to_blocks(full_matrix, row_count, col_count):
    height = full_matrix.shape[0] // row_count
    breadth = full_matrix.shape[1] // col_count
    return (
        full_matrix.reshape(row_count, height, col_count, breadth)
        .transpose(0, 2, 1, 3)
        .reshape(row_count * col_count, height, breadth)
    )


def fetch_dense(qkv_block, out_block, row_count, col_count):
    gathered = (
        lax.all_gather(qkv_block[None], ("row", "col"), axis=0, tiled=True),
        lax.all_gather(out_block[None], ("row", "col"), axis=0, tiled=True),
    )
    return (to_full(gathered[0], row_count, col_count), to_full(gathered[1], row_count, col_count))


def fetch_experts(gate_block, up_block, down_block, router_block):
    return (
        lax.all_gather(gate_block, "row", axis=2, tiled=True),
        lax.all_gather(up_block, "row", axis=2, tiled=True),
        lax.all_gather(down_block, "row", axis=1, tiled=True),
        lax.all_gather(router_block, "row", axis=0, tiled=True),
    )


def fetch_keys(kv_local):
    return lax.all_gather(kv_local, "col", axis=0, tiled=True)


def move_slots(buffer_rows):
    return lax.all_to_all(buffer_rows, "col", split_axis=0, concat_axis=0, tiled=True)


def glu_backward(grad_act, gate_val, up_val):
    sigmoid_gate = jax.nn.sigmoid(gate_val)
    silu_gate = gate_val * sigmoid_gate
    slope = sigmoid_gate * (1.0 + gate_val * (1.0 - sigmoid_gate))
    return (
        (grad_act * up_val * slope).astype(narrow_type),
        (grad_act * silu_gate).astype(narrow_type),
    )


def attend_forward(queries_b, key_value_full, allowed, score_scale):
    token_rows = queries_b.shape[0]
    query_group_width = QUERY_HEADS // KEY_VALUE_HEADS
    head_outputs = []
    log_sums = []
    for key_value_index in range(KEY_VALUE_HEADS):
        head_start = key_value_index * query_group_width
        query_part = queries_b[:, head_start : head_start + query_group_width, :]
        key_part = key_value_full[
            :, key_value_index * HEAD_SIZE : (key_value_index + 1) * HEAD_SIZE
        ]
        value_portion = key_value_full[
            :,
            (KEY_VALUE_HEADS + key_value_index)
            * HEAD_SIZE : (KEY_VALUE_HEADS + key_value_index + 1)
            * HEAD_SIZE,
        ]
        scores = (
            jnp.einsum("tgd,sd->gts", query_part, key_part, preferred_element_type=wide_type)
            * score_scale
        )
        scores = jnp.where(allowed[None], scores, masked_score)
        peak_score = jnp.max(scores, axis=-1, keepdims=True)
        exponent = jnp.exp(scores - peak_score)
        row_total = jnp.sum(exponent, axis=-1, keepdims=True)
        weights_soft = (exponent / row_total).astype(narrow_type)
        head_outputs.append(
            jnp.einsum("gts,sd->tgd", weights_soft, value_portion, preferred_element_type=wide_type)
        )
        log_sums.append(peak_score + jnp.log(row_total))
    attended = (
        jnp.concatenate(head_outputs, axis=1)
        .reshape(token_rows, QUERY_FEATURES)
        .astype(narrow_type)
    )
    return (attended, jnp.stack(log_sums))


def attend_backward(queries_b, key_value_full, allowed, score_scale, log_sums, grad_out_b):
    token_rows = queries_b.shape[0]
    query_group_width = QUERY_HEADS // KEY_VALUE_HEADS
    grad_heads = grad_out_b.reshape(token_rows, QUERY_HEADS, HEAD_SIZE)
    query_grads = []
    key_grads = []
    value_grads = []
    for key_value_index in range(KEY_VALUE_HEADS):
        head_start = key_value_index * query_group_width
        query_part = queries_b[:, head_start : head_start + query_group_width, :]
        grad_part = grad_heads[:, head_start : head_start + query_group_width, :]
        key_part = key_value_full[
            :, key_value_index * HEAD_SIZE : (key_value_index + 1) * HEAD_SIZE
        ]
        value_portion = key_value_full[
            :,
            (KEY_VALUE_HEADS + key_value_index)
            * HEAD_SIZE : (KEY_VALUE_HEADS + key_value_index + 1)
            * HEAD_SIZE,
        ]
        scores = (
            jnp.einsum("tgd,sd->gts", query_part, key_part, preferred_element_type=wide_type)
            * score_scale
        )
        weights_soft = jnp.where(allowed[None], jnp.exp(scores - log_sums[key_value_index]), 0.0)
        grad_weights = jnp.einsum(
            "tgd,sd->gts", grad_part, value_portion, preferred_element_type=wide_type
        )
        inner_sum = jnp.sum(weights_soft * grad_weights, axis=-1, keepdims=True)
        grad_scores = (weights_soft * (grad_weights - inner_sum)).astype(narrow_type)
        query_grads.append(
            jnp.einsum("gts,sd->tgd", grad_scores, key_part, preferred_element_type=wide_type)
            * score_scale
        )
        key_grads.append(
            jnp.einsum("gts,tgd->sd", grad_scores, query_part, preferred_element_type=wide_type)
            * score_scale
        )
        value_grads.append(
            jnp.einsum(
                "gts,tgd->sd",
                weights_soft.astype(narrow_type),
                grad_part,
                preferred_element_type=wide_type,
            )
        )
    return (jnp.concatenate(query_grads, axis=1), jnp.concatenate(key_grads + value_grads, axis=1))


def body(
    hidden_in, routes, norm_attn, w_qkv, w_out, norm_moe, w_router, w_gate, w_up, w_down, cotangent
):
    row_count = lax.axis_size("row")
    col_count = lax.axis_size("col")
    device_count = row_count * col_count
    col_index = lax.axis_index("col")
    layer_count = w_qkv.shape[0]
    token_rows = hidden_in.shape[0]
    model_width = hidden_in.shape[1]
    local_experts = w_gate.shape[1]
    seq_rows = token_rows * col_count
    key_value_width = KEY_VALUE_HEADS * HEAD_SIZE
    positions = col_index * token_rows + jnp.arange(token_rows, dtype=jnp.int32)
    cosine_table, sine_table_rows = rope_angles(positions, HEAD_SIZE // 2)
    key_block = jnp.arange(seq_rows, dtype=jnp.int32) // BLOCK
    allowed = key_block[None, :] <= (positions // BLOCK)[:, None]
    score_scale = HEAD_SIZE ** (-0.5)
    hidden = hidden_in.astype(wide_type)
    saved = []
    for layer_index in range(layer_count):
        layer_state = {}
        gain_attn = norm_attn[layer_index].astype(wide_type)
        gain_moe = norm_moe[layer_index].astype(wide_type)
        dense = fetch_dense(w_qkv[layer_index], w_out[layer_index], row_count, col_count)
        normed, inverse_attn = rms_parts(hidden, gain_attn)
        normed_b = normed.astype(narrow_type)
        projected_rows = jnp.dot(normed_b, dense[0], preferred_element_type=wide_type)
        queries_b = rotate_heads(
            projected_rows[:, :QUERY_FEATURES].reshape(token_rows, QUERY_HEADS, HEAD_SIZE),
            cosine_table,
            sine_table_rows,
            1.0,
        ).astype(narrow_type)
        keys_b = (
            rotate_heads(
                projected_rows[:, QUERY_FEATURES : QUERY_FEATURES + key_value_width].reshape(
                    token_rows, KEY_VALUE_HEADS, HEAD_SIZE
                ),
                cosine_table,
                sine_table_rows,
                1.0,
            )
            .reshape(token_rows, key_value_width)
            .astype(narrow_type)
        )
        kv_local = jnp.concatenate(
            [keys_b, projected_rows[:, QUERY_FEATURES + key_value_width :].astype(narrow_type)],
            axis=1,
        )
        key_value_full = fetch_keys(kv_local)
        attended_b, log_sums = attend_forward(queries_b, key_value_full, allowed, score_scale)
        attn_proj = jnp.dot(attended_b, dense[1], preferred_element_type=wide_type)
        hidden_mid = hidden + attn_proj
        experts_full = fetch_experts(
            w_gate[layer_index], w_up[layer_index], w_down[layer_index], w_router[layer_index]
        )
        router_mat = experts_full[3]
        normed_moe, inverse_moe = rms_parts(hidden_mid, gain_moe)
        normed_moe_b = normed_moe.astype(narrow_type)
        logits = jnp.dot(normed_moe_b, router_mat, preferred_element_type=wide_type)
        route_rows = routes[layer_index]
        gate_weights = jax.nn.softmax(jnp.take_along_axis(logits, route_rows, axis=1), axis=-1)
        target, usable = slot_table(route_rows[None])
        target = target[0]
        usable = usable[0]
        owner_pair, occupied = slot_owner(target, usable)
        slot_token = owner_pair // TOPK
        buffer_in = jnp.where(
            occupied[:, None], normed_moe_b[slot_token], jnp.zeros((), narrow_type)
        ).reshape(E, CAP, model_width)
        received = move_slots(buffer_in).reshape(col_count, local_experts, CAP, model_width)
        gate_val = jnp.einsum(
            "ijcd,jdf->ijcf", received, experts_full[0], preferred_element_type=wide_type
        )
        up_val = jnp.einsum(
            "ijcd,jdf->ijcf", received, experts_full[1], preferred_element_type=wide_type
        )
        activated_b = (jax.nn.silu(gate_val) * up_val).astype(narrow_type)
        expert_res = jnp.einsum(
            "ijcf,jfd->ijcd", activated_b, experts_full[2], preferred_element_type=wide_type
        ).astype(narrow_type)
        returned = move_slots(
            expert_res.reshape(col_count * local_experts, CAP, model_width)
        ).reshape(E * CAP, model_width)
        pair_gate = jnp.where(usable, gate_weights, 0.0)
        pair_rows = (
            returned[target.reshape(-1)].reshape(token_rows, TOPK, model_width).astype(wide_type)
        )
        hidden_next = hidden_mid + jnp.sum(pair_gate[..., None] * pair_rows, axis=1)
        layer_state["hidden"] = hidden
        layer_state["normed"] = normed_b
        layer_state["inverse_attn"] = inverse_attn
        layer_state["queries"] = queries_b
        layer_state["kv_local"] = kv_local
        layer_state["log_sums"] = log_sums
        layer_state["attended"] = attended_b
        layer_state["slices_attn"] = None
        layer_state["slices_out"] = None
        layer_state["hidden_mid"] = hidden_mid
        layer_state["inverse_moe"] = inverse_moe
        layer_state["normed_moe"] = normed_moe_b
        layer_state["gate_weights"] = gate_weights
        layer_state["usable"] = usable
        layer_state["target"] = target
        layer_state["pair_gate"] = pair_gate
        layer_state["owner_pair"] = owner_pair
        layer_state["occupied"] = occupied
        layer_state["slot_token"] = slot_token
        layer_state["buffer"] = buffer_in
        layer_state["pair_rows"] = pair_rows
        layer_state["gate_val"] = gate_val
        layer_state["up_val"] = up_val
        layer_state["activated"] = activated_b
        saved.append(layer_state)
        hidden = hidden_next
    incoming = cotangent.astype(wide_type)
    dense_results = [None] * layer_count
    small_results = [None] * layer_count
    expert_results = [None] * layer_count
    for layer_index in reversed(range(layer_count)):
        layer_state = saved[layer_index]
        gain_attn = norm_attn[layer_index].astype(wide_type)
        gain_moe = norm_moe[layer_index].astype(wide_type)
        dense = fetch_dense(w_qkv[layer_index], w_out[layer_index], row_count, col_count)
        key_value_full = fetch_keys(layer_state["kv_local"])
        slot_inputs = move_slots(layer_state["buffer"]).reshape(
            col_count, local_experts, CAP, model_width
        )
        experts_full = fetch_experts(
            w_gate[layer_index], w_up[layer_index], w_down[layer_index], w_router[layer_index]
        )
        gate_full, up_full, down_full, router_mat = experts_full
        route_rows = routes[layer_index]
        gate_weights = layer_state["gate_weights"]
        usable = layer_state["usable"]
        target = layer_state["target"]
        gate_val = layer_state["gate_val"]
        up_val = layer_state["up_val"]
        activated_b = layer_state["activated"]
        grad_pair = jnp.where(
            usable, jnp.sum(incoming[:, None, :] * layer_state["pair_rows"], axis=-1), 0.0
        )
        grad_picked = gate_weights * (
            grad_pair - jnp.sum(gate_weights * grad_pair, axis=-1, keepdims=True)
        )
        expert_ids = jnp.arange(E, dtype=jnp.int32)
        grad_logits = jnp.sum(
            jnp.where(route_rows[..., None] == expert_ids, grad_picked[..., None], 0.0), axis=1
        )
        slot_gate = jnp.where(
            layer_state["occupied"],
            layer_state["pair_gate"].reshape(-1)[layer_state["owner_pair"]],
            0.0,
        )
        grad_buffer = (
            (slot_gate[:, None] * incoming[layer_state["slot_token"]])
            .astype(narrow_type)
            .reshape(E, CAP, model_width)
        )
        grad_received = move_slots(grad_buffer).reshape(col_count, local_experts, CAP, model_width)
        grad_act = jnp.einsum(
            "ijcd,jfd->ijcf", grad_received, down_full, preferred_element_type=wide_type
        )
        grad_gate_b, grad_up_b = glu_backward(grad_act, gate_val, up_val)
        first_term = jnp.einsum(
            "ijcf,jdf->ijcd", grad_gate_b, gate_full, preferred_element_type=wide_type
        )
        grad_slots_b = (
            first_term
            + jnp.einsum("ijcf,jdf->ijcd", grad_up_b, up_full, preferred_element_type=wide_type)
        ).astype(narrow_type)
        gate_partial = jnp.einsum(
            "ijcd,ijcf->jdf", slot_inputs, grad_gate_b, preferred_element_type=wide_type
        )
        up_partial = jnp.einsum(
            "ijcd,ijcf->jdf", slot_inputs, grad_up_b, preferred_element_type=wide_type
        )
        down_partial = jnp.einsum(
            "ijcf,ijcd->jfd", activated_b, grad_received, preferred_element_type=wide_type
        )
        expert_results[layer_index] = (
            lax.psum_scatter(
                gate_partial.astype(jnp.bfloat16), "row", scatter_dimension=2, tiled=True
            ).astype(jnp.float32),
            lax.psum_scatter(
                up_partial.astype(jnp.bfloat16), "row", scatter_dimension=2, tiled=True
            ).astype(jnp.float32),
            lax.psum_scatter(
                down_partial.astype(jnp.bfloat16), "row", scatter_dimension=1, tiled=True
            ).astype(jnp.float32),
        )
        grad_returned = move_slots(
            grad_slots_b.reshape(col_count * local_experts, CAP, model_width)
        ).reshape(E * CAP, model_width)
        pair_grads = (
            grad_returned[target.reshape(-1)]
            .reshape(token_rows, TOPK, model_width)
            .astype(wide_type)
        )
        grad_normed_moe = jnp.sum(jnp.where(usable[..., None], pair_grads, 0.0), axis=1)
        grad_normed_moe = grad_normed_moe + jnp.einsum(
            "te,de->td", grad_logits, router_mat.astype(wide_type), precision=highest
        )
        grad_router = jnp.einsum(
            "td,te->de", layer_state["normed_moe"].astype(wide_type), grad_logits, precision=highest
        )
        grad_mid_norm, grad_gain_moe = rms_backward(
            layer_state["hidden_mid"], layer_state["inverse_moe"], gain_moe, grad_normed_moe
        )
        grad_mid = incoming + grad_mid_norm
        grad_attn_b = grad_mid.astype(narrow_type)
        grad_out_w = jnp.einsum(
            "ta,td->ad", layer_state["attended"], grad_attn_b, preferred_element_type=wide_type
        )
        grad_attended_b = jnp.einsum(
            "td,ad->ta", grad_attn_b, dense[1], preferred_element_type=wide_type
        ).astype(narrow_type)
        grad_queries, grad_kv_full = attend_backward(
            layer_state["queries"],
            key_value_full,
            allowed,
            score_scale,
            layer_state["log_sums"],
            grad_attended_b,
        )
        key_value_gradient = (
            lax.psum_scatter(
                grad_kv_full.astype(jnp.bfloat16), "col", scatter_dimension=0, tiled=True
            )
            .astype(jnp.float32)
            .astype(narrow_type)
        )
        key_value_gradient = lax.optimization_barrier(key_value_gradient).astype(wide_type)
        grad_queries = lax.optimization_barrier(grad_queries.astype(narrow_type)).astype(wide_type)
        grad_queries = rotate_heads(grad_queries, cosine_table, sine_table_rows, -1.0).reshape(
            token_rows, QUERY_FEATURES
        )
        grad_keys = rotate_heads(
            key_value_gradient[:, :key_value_width].reshape(token_rows, KEY_VALUE_HEADS, HEAD_SIZE),
            cosine_table,
            sine_table_rows,
            -1.0,
        ).reshape(token_rows, key_value_width)
        grad_projected = jnp.concatenate(
            [grad_queries, grad_keys, key_value_gradient[:, key_value_width:]], axis=1
        ).astype(narrow_type)
        grad_qkv_full = jnp.einsum(
            "td,tq->dq", layer_state["normed"], grad_projected, preferred_element_type=wide_type
        )
        grad_normed = jnp.einsum(
            "tq,dq->td", grad_projected, dense[0], preferred_element_type=wide_type
        )
        reduced = (
            lax.psum_scatter(
                to_blocks(grad_qkv_full, row_count, col_count),
                ("row", "col"),
                scatter_dimension=0,
                tiled=True,
            ),
            lax.psum_scatter(
                to_blocks(grad_out_w, row_count, col_count),
                ("row", "col"),
                scatter_dimension=0,
                tiled=True,
            ),
        )
        dense_results[layer_index] = (reduced[0][0], reduced[1][0])
        grad_hidden_norm, grad_gain_attn = rms_backward(
            layer_state["hidden"], layer_state["inverse_attn"], gain_attn, grad_normed
        )
        incoming = grad_mid + grad_hidden_norm
        small_sums = (
            lax.psum_scatter(
                grad_router.reshape(device_count, -1, E),
                ("row", "col"),
                scatter_dimension=0,
                tiled=True,
            ),
            lax.psum_scatter(
                grad_gain_attn.reshape(device_count, -1),
                ("row", "col"),
                scatter_dimension=0,
                tiled=True,
            ),
            lax.psum_scatter(
                grad_gain_moe.reshape(device_count, -1),
                ("row", "col"),
                scatter_dimension=0,
                tiled=True,
            ),
        )
        small_results[layer_index] = (small_sums[0][0], small_sums[1][0], small_sums[2][0])
    grad_qkv = jnp.stack([dense_results[index][0] for index in range(layer_count)])
    grad_out = jnp.stack([dense_results[index][1] for index in range(layer_count)])
    grad_router_all = jnp.stack([small_results[index][0] for index in range(layer_count)])
    grad_norm_attn = jnp.stack([small_results[index][1] for index in range(layer_count)])
    grad_norm_moe = jnp.stack([small_results[index][2] for index in range(layer_count)])
    grad_gate = jnp.stack([expert_results[index][0] for index in range(layer_count)])
    grad_up = jnp.stack([expert_results[index][1] for index in range(layer_count)])
    grad_down = jnp.stack([expert_results[index][2] for index in range(layer_count)])
    return (
        hidden,
        incoming,
        grad_norm_attn,
        grad_qkv,
        grad_out,
        grad_norm_moe,
        grad_router_all,
        grad_gate,
        grad_up,
        grad_down,
    )


def solution(mesh):
    in_specs = (
        P(("row", "col"), None),
        P(None, ("row", "col"), None),
        P(),
        P(None, "row", "col"),
        P(None, "row", "col"),
        P(),
        P(None, "row", None),
        P(None, "col", None, "row"),
        P(None, "col", None, "row"),
        P(None, "col", "row", None),
        P(("row", "col"), None),
    )
    out_specs = (
        P(("row", "col"), None),
        P(("row", "col"), None),
        P(None, ("row", "col")),
        P(None, "row", "col"),
        P(None, "row", "col"),
        P(None, ("row", "col")),
        P(None, ("row", "col"), None),
        P(None, "col", None, "row"),
        P(None, "col", None, "row"),
        P(None, "col", "row", None),
    )
    return jax.shard_map(body, mesh=mesh, in_specs=in_specs, out_specs=out_specs, check_vma=False)
```

profile of v0, /device:TPU:30, one launch (start us, length us, event | category | flops | bytes accessed | tf_op | source)
XLA Modules:
  0.0 3843.2 jit_solution(11772514578033616109)
XLA Ops:
  15.5 64.0 %all-gather.21.cloned.1.call-done = bf16[32,384,256]{2,1,0:T(8,128)(2,1)} async-done(((bf16[1,384,256]{2,1,0:T(8,128)(2,1)}), bf16[32,384,256]{2,1,0:T(8,128)(2,1)}) %all-gather.21.cloned.1.call-update) | async-done | bytes 6291472 | tf_op jit(solution)/shard_map/all_gather | solution.py:100
  116.4 9.0 reduce-window.14
  129.9 15.7 all-gather.25.cloned.1.call-done
  182.9 16.8 fusion.24
  242.9 99.4 %all-gather.33.cloned.1.call-done = bf16[1,4,1536,768]{2,1,0,3:T(4,128)(2,1)} async-done(((bf16[1,4,1536,192]{2,1,0,3:T(4,128)(2,1)}), bf16[1,4,1536,768]{2,1,0,3:T(4,128)(2,1)}) %all-gather.33.cloned.1.call-update) | async-done | bytes 9437200 | tf_op jit(solution)/shard_map/all_gather | solution.py:108
  342.4 15.6 copy.305
  358.0 150.8 %all-gather.35.cloned.1.call-done = bf16[1,4,1536,768]{2,1,0,3:T(4,128)(2,1)} async-done(((bf16[1,4,1536,192]{2,1,0,3:T(4,128)(2,1)}), bf16[1,4,1536,768]{2,1,0,3:T(4,128)(2,1)}) %all-gather.35.cloned.1.call-update) | async-done | bytes 9437200 | tf_op jit(solution)/shard_map/all_gather | solution.py:109
  508.8 15.6 copy.308
  542.5 132.7 %all-gather.37.cloned.1.call-done = bf16[1,4,768,1536]{3,2,1,0:T(8,128)(2,1)} async-done(((bf16[1,4,192,1536]{3,2,1,0:T(8,128)(2,1)}), bf16[1,4,768,1536]{3,2,1,0:T(8,128)(2,1)}) %all-gather.37.cloned.1.call-update) | async-done | bytes 9437200 | tf_op jit(solution)/shard_map/all_gather | solution.py:110
  690.6 13.3 all-gather
  703.9 56.5 %all-gather.27.cloned.1.call-done = bf16[32,384,256]{2,1,0:T(8,128)(2,1)} async-done(((bf16[1,384,256]{2,1,0:T(8,128)(2,1)}), bf16[32,384,256]{2,1,0:T(8,128)(2,1)}) %all-gather.27.cloned.1.call-update) | async-done | bytes 6291472 | tf_op jit(solution)/shard_map/all_gather | solution.py:100
  826.3 9.0 reduce-window.16
  862.6 9.2 fusion.22
  938.0 16.3 all-gather.4
  978.8 46.1 %all-gather.39.cloned.1.call-done = bf16[1,4,1536,768]{2,1,0,3:T(4,128)(2,1)} async-done(((bf16[1,4,1536,192]{2,1,0,3:T(4,128)(2,1)}), bf16[1,4,1536,768]{2,1,0,3:T(4,128)(2,1)}) %all-gather.39.cloned.1.call-update) | async-done | bytes 9437200 | tf_op jit(solution)/shard_map/all_gather | solution.py:108
  1024.9 15.7 copy.326
  1040.6 150.8 %all-gather.41.cloned.1.call-done = bf16[1,4,1536,768]{2,1,0,3:T(4,128)(2,1)} async-done(((bf16[1,4,1536,192]{2,1,0,3:T(4,128)(2,1)}), bf16[1,4,1536,768]{2,1,0,3:T(4,128)(2,1)}) %all-gather.41.cloned.1.call-update) | async-done | bytes 9437200 | tf_op jit(solution)/shard_map/all_gather | solution.py:109
  1191.5 15.6 copy.329
  1207.1 10.5 fusion.42
  1224.9 133.0 %all-gather.43.cloned.1.call-done = bf16[1,4,768,1536]{3,2,1,0:T(8,128)(2,1)} async-done(((bf16[1,4,192,1536]{3,2,1,0:T(8,128)(2,1)}), bf16[1,4,768,1536]{3,2,1,0:T(8,128)(2,1)}) %all-gather.43.cloned.1.call-update) | async-done | bytes 9437200 | tf_op jit(solution)/shard_map/all_gather | solution.py:110
  1357.9 13.9 fusion.90
  1386.6 10.7 fusion.40
  1397.3 11.8 fusion.104
  1413.5 17.1 all-to-all-done.3
  1444.7 9.7 gather_fusion.3
  1454.5 27.2 all-to-all-done.5
  1487.3 9.7 gather_fusion.6
  1503.7 8.9 select_reduce_fusion.1
  1519.2 10.1 multiply_reduce_fusion.1
  1564.5 19.6 fusion.9
  1584.1 20.7 fusion.11
  1635.9 21.9 reduce-scatter.15.cloned.1.call-done
  1683.6 49.0 %all_to_all.42 = bf16[32,36,1536]{2,1,0:T(8,128)(2,1)} all-to-all(bf16[32,36,1536]{2,1,0:T(8,128)(2,1)S(1)} %multiply_convert_fusion), channel_id=1, replica_groups=mesh['row'=4,'col'=8] {'col'}, dimensions={0} | all-to-all | bytes 7077888 | tf_op jit(solution)/shard_map/all_to_all | solution.py:120
  1732.6 12.8 fusion.87
  1745.4 11.5 fusion.28
  1756.8 12.5 fusion.107
  1785.7 39.2 %all-to-all-done.7 = bf16[32,36,1536]{2,1,0:T(8,128)(2,1)} async-done(((bf16[32,36,1536]{2,1,0:T(8,128)(2,1)}), bf16[32,36,1536]{2,1,0:T(8,128)(2,1)}, u32[]{:S(2)}, u32[]{:S(2)}) %all-to-all-start.7) | async-done | bytes 3538976 | tf_op jit(solution)/shard_map/all_to_all | solution.py:120
  1830.5 9.7 gather_fusion.9
  1884.3 19.2 fusion.3
  1903.5 20.7 fusion.5
  1958.7 9.7 bitcast_convert_fusion
  1970.0 9.7 bitcast_convert_fusion.1
  1981.2 9.6 bitcast_convert_fusion.2
  1992.3 9.6 bitcast_convert_fusion.3
  2003.5 9.6 bitcast_convert_fusion.4
  2014.7 9.7 bitcast_convert_fusion.5
  2032.5 15.5 copy.508
  2048.0 10.0 bitcast_bitcast_fusion
  2058.0 13.5 copy.388
  2094.1 15.6 copy.507
  2109.8 10.0 bitcast_bitcast_fusion.1
  2119.7 13.1 copy.387
  2133.6 107.8 %reduce-scatter.27.cloned.1.call-done = f32[1,48,32]{1,2,0:T(8,128)} async-done(((f32[32,48,32]{1,2,0:T(8,128)}), f32[1,48,32]{1,2,0:T(8,128)}) %reduce-scatter.27.cloned.1.call-update) | async-done | bytes 6160 | tf_op jit(solution)/shard_map/reduce_scatter | solution.py:493
  2249.0 41.5 %all-reduce.4 = (f32[32,48]{1,0:T(8,128)S(1)}, f32[32,48]{1,0:T(8,128)S(1)}, f32[32,48]{1,0:T(8,128)S(1)}, f32[32,48]{1,0:T(8,128)S(1)}) all-reduce(f32[32,48]{1,0:T(8,128)S(1)} %reshape.1052, f32[32,48]{1,0:T(8,128)S(1)} %reshape.1051, f32[32,48]{1,0:T(8,128)S(1)} %reshape.1060, ...), channel_id=13, replica_groups=mesh['row'=4,'col'=8] {'row','col'}, use_global_device_ids=true, to_apply=%region_49.51.clone | all-reduce | flops 6144 | bytes 49152
  2294.7 88.1 %reduce-scatter.25.cloned.1.call-done = f32[1,384,192]{1,2,0:T(8,128)} async-done(((f32[32,384,192]{1,2,0:T(8,128)}), f32[1,384,192]{1,2,0:T(8,128)}) %reduce-scatter.25.cloned.1.call-update) | async-done | bytes 294928 | tf_op jit(solution)/shard_map/reduce_scatter | solution.py:480
  2382.8 141.9 %reduce-scatter.23.cloned.1.call-done = f32[1,384,192]{1,2,0:T(8,128)} async-done(((f32[32,384,192]{1,2,0:T(8,128)}), f32[1,384,192]{1,2,0:T(8,128)}) %reduce-scatter.23.cloned.1.call-update) | async-done | bytes 294928 | tf_op jit(solution)/shard_map/reduce_scatter | solution.py:480
  2526.6 162.6 %reduce-scatter.41.cloned.1.call-done = bf16[4,192,1536]{2,1,0:T(8,128)(2,1)} async-done(((bf16[4,768,1536]{2,1,0:T(8,128)(2,1)}), bf16[4,192,1536]{2,1,0:T(8,128)(2,1)}) %reduce-scatter.41.cloned.1.call-update) | async-done | bytes 2359312 | tf_op jit(solution)/shard_map/reduce_scatter | solution.py:408
  2689.2 164.4 %reduce-scatter.39.cloned.1.call-done = bf16[4,192,1536]{2,1,0:T(8,128)(2,1)} async-done(((bf16[4,768,1536]{2,1,0:T(8,128)(2,1)}), bf16[4,192,1536]{2,1,0:T(8,128)(2,1)}) %reduce-scatter.39.cloned.1.call-update) | async-done | bytes 2359312 | tf_op jit(solution)/shard_map/reduce_scatter | solution.py:408
  2860.3 157.8 %reduce-scatter.37.cloned.1.call-done = bf16[4,1536,192]{1,2,0:T(8,128)(2,1)} async-done(((bf16[4,1536,768]{1,2,0:T(8,128)(2,1)}), bf16[4,1536,192]{1,2,0:T(8,128)(2,1)}) %reduce-scatter.37.cloned.1.call-update) | async-done | bytes 2359312 | tf_op jit(solution)/shard_map/reduce_scatter | solution.py:405
  3018.1 164.5 %reduce-scatter.35.cloned.1.call-done = bf16[4,1536,192]{1,2,0:T(8,128)(2,1)} async-done(((bf16[4,1536,768]{1,2,0:T(8,128)(2,1)}), bf16[4,1536,192]{1,2,0:T(8,128)(2,1)}) %reduce-scatter.35.cloned.1.call-update) | async-done | bytes 2359312 | tf_op jit(solution)/shard_map/reduce_scatter | solution.py:405
  3189.3 158.4 %reduce-scatter.33.cloned.1.call-done = bf16[4,1536,192]{1,2,0:T(8,128)(2,1)} async-done(((bf16[4,1536,768]{1,2,0:T(8,128)(2,1)}), bf16[4,1536,192]{1,2,0:T(8,128)(2,1)}) %reduce-scatter.33.cloned.1.call-update) | async-done | bytes 2359312 | tf_op jit(solution)/shard_map/reduce_scatter | solution.py:402
  3347.7 164.4 %reduce-scatter.31.cloned.1.call-done = bf16[4,1536,192]{1,2,0:T(8,128)(2,1)} async-done(((bf16[4,1536,768]{1,2,0:T(8,128)(2,1)}), bf16[4,1536,192]{1,2,0:T(8,128)(2,1)}) %reduce-scatter.31.cloned.1.call-update) | async-done | bytes 2359312 | tf_op jit(solution)/shard_map/reduce_scatter | solution.py:402
  3518.8 153.9 %reduce-scatter.21.cloned.1.call-done = f32[1,384,256]{2,1,0:T(8,128)} async-done(((f32[32,384,256]{2,1,0:T(8,128)}), f32[1,384,256]{2,1,0:T(8,128)}) %reduce-scatter.21.cloned.1.call-update) | async-done | bytes 393232 | tf_op jit(solution)/shard_map/reduce_scatter | solution.py:474
  3672.7 161.7 %reduce-scatter.19.cloned.1.call-done = f32[1,384,256]{2,1,0:T(8,128)} async-done(((f32[32,384,256]{2,1,0:T(8,128)}), f32[1,384,256]{2,1,0:T(8,128)}) %reduce-scatter.19.cloned.1.call-update) | async-done | bytes 393232 | tf_op jit(solution)/shard_map/reduce_scatter | solution.py:474
  (660 shorter events, 672.6 us)
Async XLA Ops:
  7.2 72.3 %all-gather.21.cloned.1.call-start = ((), (), s32[]{:S(2)}) async-start(), calls=%async_computation.22 | async-start | bytes 6488064 | tf_op jit(solution)/shard_map/all_gather | solution.py:100
  9.0 136.5 %all-gather.25.cloned.1.call-start = ((), (), s32[]{:S(2)}) async-start(), calls=%async_computation.24 | async-start | bytes 4866048 | tf_op jit(solution)/shard_map/all_gather | solution.py:101
  10.8 165.2 %all-gather.23.cloned.1.call-start = ((), (), s32[]{:S(2)}) async-start(), calls=%async_computation.23 | async-start | bytes 2359296 | tf_op jit(solution)/shard_map/all_gather | solution.py:116
  12.3 76.4 %copy-start.92 = (f32[1536]{0:T(1024)}, f32[1536]{0:T(1024)S(1)}, u32[]{:S(2)}) copy-start(f32[1536]{0:T(1024)S(1)} %get-tuple-element.36) | copy-start | bytes 18436
  14.3 74.4 %copy-start.126 = (f32[256]{0:T(256)}, f32[256]{0:T(256)S(1)}, u32[]{:S(2)}) copy-start(f32[256]{0:T(256)S(1)} %get-tuple-element.107) | copy-start | bytes 3076
  15.5 149.0 %copy-start.20 = (f32[256,64]{1,0:T(8,128)}, f32[256,64]{1,0:T(8,128)S(1)}, u32[]{:S(2)}) copy-start(f32[256,64]{1,0:T(8,128)S(1)} %get-tuple-element.105) | copy-start | bytes 196612
  15.5 149.0 %copy-start.40 = (f32[256,64]{1,0:T(8,128)}, f32[256,64]{1,0:T(8,128)S(1)}, u32[]{:S(2)}) copy-start(f32[256,64]{1,0:T(8,128)S(1)} %get-tuple-element.104) | copy-start | bytes 196612
  94.4 247.9 %all-gather.33.cloned.1.call-start = ((), (), s32[]{:S(2)}) async-start(), calls=%async_computation.42 | async-start | bytes 11796480 | tf_op jit(solution)/shard_map/all_gather | solution.py:108
  102.2 406.5 %all-gather.35.cloned.1.call-start = ((), (), s32[]{:S(2)}) async-start(), calls=%async_computation.43 | async-start | bytes 11796480 | tf_op jit(solution)/shard_map/all_gather | solution.py:109
  109.8 565.4 %all-gather.37.cloned.1.call-start = ((), (), s32[]{:S(2)}) async-start(), calls=%async_computation.44 | async-start | bytes 11796480 | tf_op jit(solution)/shard_map/all_gather | solution.py:110
  114.6 14.6 copy-start.121
  114.7 645.7 %all-gather.27.cloned.1.call-start = ((), (), s32[]{:S(2)}) async-start(), calls=%async_computation.25 | async-start | bytes 6488064 | tf_op jit(solution)/shard_map/all_gather | solution.py:100
  116.2 665.5 %copy-start.24 = (s32[1,256,4]{2,1,0:T(8,128)}, s32[1,256,4]{2,1,0:T(8,128)S(1)}, u32[]{:S(2)}) copy-start(s32[1,256,4]{2,1,0:T(8,128)S(1)} %copy.483) | copy-start | bytes 12292
  127.7 81.4 %copy-start.10 = (pred[256,2048]{0,1:T(8,128)(4,1)}, pred[256,2048]{0,1:T(8,128)(4,1)S(1)}, u32[]{:S(2)}) copy-start(pred[256,2048]{0,1:T(8,128)(4,1)S(1)} %broadcast_compare_fusion) | copy-start | bytes 1572868
  128.6 103.5 %copy-start.102 = (pred[32,36]{1,0:T(8,128)(4,1)}, pred[32,36]{1,0:T(8,128)(4,1)S(1)}, u32[]{:S(2)}) copy-start(pred[32,36]{1,0:T(8,128)(4,1)S(1)} %broadcast_in_dim.226) | copy-start | bytes 3460
  129.3 91.4 %copy-start.98 = (s32[2048]{0:T(1024)}, s32[2048]{0:T(1024)S(1)}, u32[]{:S(2)}) copy-start(s32[2048]{0:T(1024)S(1)} %get-tuple-element.133) | copy-start | bytes 24580
  129.9 90.1 %copy-start.87 = (f32[1536]{0:T(1024)}, f32[1536]{0:T(1024)S(1)}, u32[]{:S(2)}) copy-start(f32[1536]{0:T(1024)S(1)} %get-tuple-element.34) | copy-start | bytes 18436
  166.9 16.0 copy-start.26
  166.9 16.0 copy-start.27
  182.9 26.3 copy-start.128
  204.4 13.4 slice-start
  236.4 287.9 %all-to-all-start = ((bf16[32,36,1536]{2,1,0:T(8,128)(2,1)}), bf16[32,36,1536]{2,1,0:T(8,128)(2,1)}, u32[]{:S(2)}, u32[]{:S(2)}) async-start(bf16[32,36,1536]{2,1,0:T(8,128)(2,1)} %broadcast_select_fusion.1), calls=%async_computation | async-start | bytes 7864320 | tf_op jit(solution)/shard_map/all_to_all | solution.py:120
  242.2 595.9 %all-gather.31.cloned.1.call-start = ((), (), s32[]{:S(2)}) async-start(), calls=%async_computation.27 | async-start | bytes 4866048 | tf_op jit(solution)/shard_map/all_gather | solution.py:101
  542.5 139.9 %copy-start.142 = (bf16[8,4,36,768]{3,2,0,1:T(8,128)(2,1)}, bf16[8,4,36,768]{3,2,0,1:T(8,128)(2,1)S(1)}, u32[]{:S(2)}) copy-start(bf16[8,4,36,768]{3,2,0,1:T(8,128)(2,1)S(1)} %get-tuple-element.119) | copy-start | bytes 5308420
  684.6 98.0 %all-to-all-start.1 = ((bf16[32,36,1536]{2,1,0:T(8,128)(2,1)}), bf16[32,36,1536]{2,1,0:T(8,128)(2,1)}, u32[]{:S(2)}, u32[]{:S(2)}) async-start(bf16[32,36,1536]{2,1,0:T(8,128)(2,1)} %bitcast.678), calls=%async_computation.1 | async-start | bytes 7864320 | tf_op jit(solution)/shard_map/all_to_all | solution.py:120
  689.5 173.1 %all-gather.29.cloned.1.call-start = ((), (), s32[]{:S(2)}) async-start(), calls=%async_computation.26 | async-start | bytes 2359296 | tf_op jit(solution)/shard_map/all_gather | solution.py:116
  689.7 92.0 %copy-start.75 = (pred[256,4]{1,0:T(8,128)(4,1)}, pred[256,4]{1,0:T(8,128)(4,1)S(1)}, u32[]{:S(2)}) copy-start(pred[256,4]{1,0:T(8,128)(4,1)S(1)} %lt.89) | copy-start | bytes 3076
  703.9 68.2 %copy-start.73 = (bf16[1,1536,32]{1,2,0:T(8,128)(2,1)}, bf16[1,1536,32]{1,2,0:T(8,128)(2,1)S(1)}, u32[]{:S(2)}) copy-start(bf16[1,1536,32]{1,2,0:T(8,128)(2,1)S(1)} %all-gather) | copy-start | bytes 294916
  703.9 82.6 %copy-start.104 = (s32[1024]{0:T(1024)}, s32[1024]{0:T(1024)S(1)}, u32[]{:S(2)}) copy-start(s32[1024]{0:T(1024)S(1)} %broadcast_clamp_fusion.1) | copy-start | bytes 12292
  806.5 91.9 %copy-start.17 = (f32[256,1536]{1,0:T(8,128)}, f32[256,1536]{1,0:T(8,128)S(1)}, u32[]{:S(2)}) copy-start(f32[256,1536]{1,0:T(8,128)S(1)} %get-tuple-element.48) | copy-start | bytes 4718596
  815.0 209.9 %all-gather.39.cloned.1.call-start = ((), (), s32[]{:S(2)}) async-start(), calls=%async_computation.45 | async-start | bytes 11796480 | tf_op jit(solution)/shard_map/all_gather | solution.py:108
  820.0 371.5 %all-gather.41.cloned.1.call-start = ((), (), s32[]{:S(2)}) async-start(), calls=%async_computation.46 | async-start | bytes 11796480 | tf_op jit(solution)/shard_map/all_gather | solution.py:109
  825.4 532.5 %all-gather.43.cloned.1.call-start = ((), (), s32[]{:S(2)}) async-start(), calls=%async_computation.47 | async-start | bytes 11796480 | tf_op jit(solution)/shard_map/all_gather | solution.py:110
  871.9 18.0 copy-start.133
  885.1 13.4 slice-start.4
  917.2 57.1 %all-to-all-start.2 = ((bf16[32,36,1536]{2,1,0:T(8,128)(2,1)}), bf16[32,36,1536]{2,1,0:T(8,128)(2,1)}, u32[]{:S(2)}, u32[]{:S(2)}) async-start(bf16[32,36,1536]{2,1,0:T(8,128)(2,1)} %broadcast_select_fusion), calls=%async_computation.2 | async-start | bytes 7864320 | tf_op jit(solution)/shard_map/all_to_all | solution.py:120
  974.3 383.5 %all-to-all-start.4 = ((bf16[32,36,1536]{2,1,0:T(8,128)(2,1)}), bf16[32,36,1536]{2,1,0:T(8,128)(2,1)}, u32[]{:S(2)}, u32[]{:S(2)}) async-start(bf16[32,36,1536]{2,1,0:T(8,128)(2,1)} %multiply_convert_fusion.1), calls=%async_computation.4 | async-start | bytes 7864320 | tf_op jit(solution)/shard_map/all_to_all | solution.py:120
  1381.6 49.0 %all-to-all-start.3 = ((bf16[32,36,1536]{2,1,0:T(8,128)(2,1)}), bf16[32,36,1536]{2,1,0:T(8,128)(2,1)}, u32[]{:S(2)}, u32[]{:S(2)}) async-start(bf16[32,36,1536]{2,1,0:T(8,128)(2,1)} %bitcast.681), calls=%async_computation.3 | async-start | bytes 7864320 | tf_op jit(solution)/shard_map/all_to_all | solution.py:120
  1430.6 51.0 %all-to-all-start.5 = ((bf16[32,36,1536]{2,1,0:T(8,128)(2,1)}), bf16[32,36,1536]{2,1,0:T(8,128)(2,1)}, u32[]{:S(2)}, u32[]{:S(2)}) async-start(bf16[32,36,1536]{2,1,0:T(8,128)(2,1)} %bitcast.679), calls=%async_computation.5 | async-start | bytes 7864320 | tf_op jit(solution)/shard_map/all_to_all | solution.py:120
  1437.5 220.3 %reduce-scatter.15.cloned.1.call-start = ((), (), s32[]{:S(2)}) async-start(), calls=%async_computation.28 | async-start | bytes 2359296 | tf_op jit(solution)/shard_map/reduce_scatter | solution.py:447
  1633.2 26.8 copy-start.18
  1633.2 26.8 copy-start.95
  1633.2 26.8 copy-start.123
  1635.9 29.7 copy-start.42
  1745.4 11.5 copy-start.57
  1773.8 51.0 %all-to-all-start.7 = ((bf16[32,36,1536]{2,1,0:T(8,128)(2,1)}), bf16[32,36,1536]{2,1,0:T(8,128)(2,1)}, u32[]{:S(2)}, u32[]{:S(2)}) async-start(bf16[32,36,1536]{2,1,0:T(8,128)(2,1)} %bitcast.680), calls=%async_computation.8 | async-start | bytes 7864320 | tf_op jit(solution)/shard_map/all_to_all | solution.py:120
  1780.8 304.7 %reduce-scatter.17.cloned.1.call-start = ((), (), s32[]{:S(2)}) async-start(), calls=%async_computation.29 | async-start | bytes 2359296 | tf_op jit(solution)/shard_map/reduce_scatter | solution.py:447
  1785.4 45.1 %copy-start.105 = (s32[1024]{0:T(1024)S(1)}, s32[1024]{0:T(1024)}, u32[]{:S(2)}) copy-start(s32[1024]{0:T(1024)} %copy-done.104) | copy-start | bytes 12292
  1847.1 12.5 slice-start.2
  1935.6 198.1 %reduce-scatter.29.cloned.1.call-start = ((), (), s32[]{:S(2)}) async-start(), calls=%async_computation.35 | async-start | bytes 540672 | tf_op jit(solution)/shard_map/reduce_scatter | solution.py:493
  1940.5 301.0 %reduce-scatter.27.cloned.1.call-start = ((), (), s32[]{:S(2)}) async-start(), calls=%async_computation.34 | async-start | bytes 540672 | tf_op jit(solution)/shard_map/reduce_scatter | solution.py:493
  1943.9 438.9 %reduce-scatter.25.cloned.1.call-start = ((), (), s32[]{:S(2)}) async-start(), calls=%async_computation.33 | async-start | bytes 9732096 | tf_op jit(solution)/shard_map/reduce_scatter | solution.py:480
  1950.4 574.3 %reduce-scatter.23.cloned.1.call-start = ((), (), s32[]{:S(2)}) async-start(), calls=%async_computation.32 | async-start | bytes 9732096 | tf_op jit(solution)/shard_map/reduce_scatter | solution.py:480
  1957.0 732.2 %reduce-scatter.41.cloned.1.call-start = ((), (), s32[]{:S(2)}) async-start(), calls=%async_computation.41 | async-start | bytes 11796480 | tf_op jit(solution)/shard_map/reduce_scatter | solution.py:408
  1968.5 885.1 %reduce-scatter.39.cloned.1.call-start = ((), (), s32[]{:S(2)}) async-start(), calls=%async_computation.40 | async-start | bytes 11796480 | tf_op jit(solution)/shard_map/reduce_scatter | solution.py:408
  1979.7 1038.4 %reduce-scatter.37.cloned.1.call-start = ((), (), s32[]{:S(2)}) async-start(), calls=%async_computation.39 | async-start | bytes 11796480 | tf_op jit(solution)/shard_map/reduce_scatter | solution.py:405
  1990.8 1191.8 %reduce-scatter.35.cloned.1.call-start = ((), (), s32[]{:S(2)}) async-start(), calls=%async_computation.38 | async-start | bytes 11796480 | tf_op jit(solution)/shard_map/reduce_scatter | solution.py:405
  2002.0 1345.7 %reduce-scatter.33.cloned.1.call-start = ((), (), s32[]{:S(2)}) async-start(), calls=%async_computation.37 | async-start | bytes 11796480 | tf_op jit(solution)/shard_map/reduce_scatter | solution.py:402
  2013.1 1498.9 %reduce-scatter.31.cloned.1.call-start = ((), (), s32[]{:S(2)}) async-start(), calls=%async_computation.36 | async-start | bytes 11796480 | tf_op jit(solution)/shard_map/reduce_scatter | solution.py:402
  2024.4 1648.3 %reduce-scatter.21.cloned.1.call-start = ((), (), s32[]{:S(2)}) async-start(), calls=%async_computation.31 | async-start | bytes 12976128 | tf_op jit(solution)/shard_map/reduce_scatter | solution.py:474
  2071.5 1762.9 %reduce-scatter.19.cloned.1.call-start = ((), (), s32[]{:S(2)}) async-start(), calls=%async_computation.30 | async-start | bytes 12976128 | tf_op jit(solution)/shard_map/reduce_scatter | solution.py:474
  2132.8 110.0 %copy-start.111 = (f32[1536]{0:T(1024)S(1)}, f32[1536]{0:T(1024)}, u32[]{:S(2)}) copy-start(f32[1536]{0:T(1024)} %get-tuple-element.13) | copy-start | bytes 18436
  2242.9 48.8 %copy-start.35 = (f32[256,1536]{1,0:T(8,128)S(1)}, f32[256,1536]{1,0:T(8,128)}, u32[]{:S(2)}) copy-start(f32[256,1536]{1,0:T(8,128)} %copy-done.34) | copy-start | bytes 4718596
  2242.9 48.8 %copy-start.140 = (f32[256]{0:T(256)S(1)}, f32[256]{0:T(256)}, u32[]{:S(2)}) copy-start(f32[256]{0:T(256)} %get-tuple-element.106) | copy-start | bytes 3076
  (120 other events, 568.6 us)
Sparse Core Ops, SparseCore 0:
  11.4 67.9 all-gather.20
  83.0 62.5 all-gather.24
  148.0 27.9 all-gather.22
  177.4 164.8 all-gather.32
  343.8 164.9 all-gather.34
  510.2 164.9 all-gather.36
  678.0 82.3 all-gather.26
  763.3 63.8 all-gather.30
  829.0 27.9 all-gather.28
  858.4 166.4 all-gather.38
  1026.5 164.9 all-gather.40
  1192.9 164.9 all-gather.42
  1616.2 41.6 reduce-scatter.14
  1935.7 41.2 reduce-scatter.16
  1979.6 129.1 reduce-scatter.28
  2111.6 129.8 reduce-scatter.26
  2247.8 134.9 reduce-scatter.24
  2390.1 134.5 reduce-scatter.22
  2527.1 162.0 reduce-scatter.40
  2691.4 162.1 reduce-scatter.38
  2855.9 162.1 reduce-scatter.36
  3020.4 162.1 reduce-scatter.34
  3185.5 162.1 reduce-scatter.32
  3349.9 162.1 reduce-scatter.30
  3518.1 154.5 reduce-scatter.20
  3679.6 154.7 reduce-scatter.18
where the time goes:
time: 3860 us; the launch traced here: 3840 us
  waiting for transfers between devices  2590 us (67%)
  local copies, waits for them, and re-layouts  447 us (12%)
  matrix products  435 us (11%)
  other arithmetic  191 us (5%)
  blocking collectives  120 us (3%)
  starting transfers between devices  43 us (1%)
    reduce_scatter x2, waiting for transfers between devices, body(): lax.psum_scatter(down_partial.astype(jnp.bfloat16), 'row', scatter_dimens...  327 us
    reduce_scatter x2, waiting for transfers between devices, body(): lax.psum_scatter(gate_partial.astype(jnp.bfloat16), 'row', scatter_dimens...  323 us
    reduce_scatter x2, waiting for transfers between devices, body(): lax.psum_scatter(up_partial.astype(jnp.bfloat16), 'row', scatter_dimensio...  322 us
    reduce_scatter x2, waiting for transfers between devices, body(): lax.psum_scatter(to_blocks(grad_qkv_full, row_count, col_count), ('row',...  316 us
    all_gather x2, waiting for transfers between devices, fetch_experts(): lax.all_gather(up_block, 'row', axis=2, tiled=True)  302 us
    all_gather x2, waiting for transfers between devices, fetch_experts(): lax.all_gather(down_block, 'row', axis=1, tiled=True)  266 us
    reduce_scatter x2, waiting for transfers between devices, body(): lax.psum_scatter(to_blocks(grad_out_w, row_count, col_count), ('row', 'co...  230 us
    all_gather x2, waiting for transfers between devices, fetch_experts(): lax.all_gather(gate_block, 'row', axis=2, tiled=True)  145 us
  transfers between devices with their start and end apart: 33, of which 25 were waited for; matrix products, arithmetic and copies ran while one was open for 18% of the time, Pallas kernels for 0%

commit v1 on v0

v1 whole, which is shorter than its diff:
```python
import functools

import jax
import jax.numpy as jnp
from jax import lax
from jax.experimental import pallas as pl
from jax.experimental.pallas import tpu as pltpu
from jax.sharding import PartitionSpec as P

QUERY_HEADS = 12
KEY_VALUE_HEADS = 2
HEAD_SIZE = 128
E = 32
TOPK = 4
BLOCK = 256
QUERY_FEATURES = 1536
CAP = 36


eps_norm = 1e-06
rope_base = 1000000.0
masked_score = -1e30
highest = lax.Precision.HIGHEST
wide_type = jnp.float32
narrow_type = jnp.bfloat16


def rms_parts(values, gain_vec):
    inverse = lax.rsqrt(jnp.mean(values * values, axis=-1, keepdims=True) + eps_norm)
    return (values * inverse * gain_vec, inverse)


def rms_backward(values, inverse, gain_vec, incoming):
    scaled = incoming * gain_vec
    inner_mean = jnp.mean(scaled * values, axis=-1, keepdims=True)
    grad_values = inverse * scaled - values * (inverse * inverse * inverse) * inner_mean
    grad_gain = jnp.sum(incoming * values * inverse, axis=0)
    return (grad_values, grad_gain)


def rope_angles(positions, half_dim):
    frequency = rope_base ** (-jnp.arange(half_dim, dtype=jnp.float32) / half_dim)
    angles = positions.astype(jnp.float32)[:, None] * frequency[None, :]
    return (jnp.cos(angles), jnp.sin(angles))


def rotate_heads(values, cosine_table, sine_table_rows, direction):
    half_dim = values.shape[-1] // 2
    first_half = values[..., :half_dim]
    second_half = values[..., half_dim:]
    cos_rows = cosine_table[:, None, :]
    sin_rows = direction * sine_table_rows[:, None, :]
    return jnp.concatenate(
        [
            first_half * cos_rows - second_half * sin_rows,
            second_half * cos_rows + first_half * sin_rows,
        ],
        axis=-1,
    )


def to_full(gathered, row_count, col_count):
    height = gathered.shape[1]
    breadth = gathered.shape[2]
    return (
        gathered.reshape(row_count, col_count, height, breadth)
        .transpose(0, 2, 1, 3)
        .reshape(row_count * height, col_count * breadth)
    )


def fetch_keys(kv_local):
    return lax.all_gather(kv_local, "col", axis=0, tiled=True)


def split_rows(total, most):
    best = 16
    for step in range(16, most + 1, 16):
        if total % step == 0:
            best = step
    return best


def over_blocks(total, block, step):
    def run(index, carry):
        step(pl.ds(pl.multiple_of(index * block, block), block))
        return carry

    lax.fori_loop(0, total // block, run, 0)


def over_chunks(chunks, width, step):
    def run(index, carry):
        step(index, pl.ds(pl.multiple_of(index * width, width), width))
        return carry

    lax.fori_loop(0, chunks, run, 0)


def dot_nt(left, right):
    return lax.dot_general(
        left, right, (((1,), (1,)), ((), ())), preferred_element_type=jnp.float32
    )


def dot_nn(left, right):
    return jnp.dot(left, right, preferred_element_type=jnp.float32)


class Peers:
    def __init__(self, count, place, device_of):
        self.count = count
        self.place = place
        self.device_of = device_of

    def ahead(self, step):
        return lax.rem(self.place + step, self.count)

    def behind(self, step):
        return lax.rem(self.place + self.count - step, self.count)


def expert_peers(col_count, copies, group_rows):
    row_index = lax.axis_index("row")
    share = lax.rem(row_index, copies)
    rows = Peers(
        group_rows, row_index // copies, lambda place: {"row": share + copies * place}
    )
    cols = Peers(col_count, lax.axis_index("col"), lambda place: {"col": place})
    return rows, cols


def greet(groups):
    barrier = pltpu.get_barrier_semaphore()
    total = 0
    for peers in groups:
        for step in range(1, peers.count):
            pl.semaphore_signal(
                barrier,
                inc=1,
                device_id=peers.device_of(peers.ahead(step)),
                device_id_type=pl.DeviceIdType.MESH,
            )
            total += 1
    pl.semaphore_wait(barrier, total)


class Exchange:
    def __init__(self, peers, send_sems, recv_sems, source, target):
        self.peers = peers
        self.send_sems = send_sems
        self.recv_sems = recv_sems
        self.source = source
        self.target = target

    def out(self, step, index, chunk):
        place = self.peers.ahead(step)
        return pltpu.make_async_remote_copy(
            src_ref=self.source(place, chunk),
            dst_ref=self.target(self.peers.place, step, chunk),
            send_sem=self.send_sems.at[index, step - 1],
            recv_sem=self.recv_sems.at[index, step - 1],
            device_id=self.peers.device_of(place),
            device_id_type=pl.DeviceIdType.MESH,
        )

    def start(self, index, chunk):
        for step in range(1, self.peers.count):
            self.out(step, index, chunk).start()

    def wait_send(self, index, chunk):
        for step in range(1, self.peers.count):
            self.out(step, index, chunk).wait_send()

    def wait_recv(self, index, chunk):
        for step in range(1, self.peers.count):
            landed = self.target(self.peers.behind(step), step, chunk)
            pltpu.make_async_remote_copy(
                src_ref=landed,
                dst_ref=landed,
                send_sem=self.send_sems.at[index, step - 1],
                recv_sem=self.recv_sems.at[index, step - 1],
                device_id=self.peers.device_of(self.peers.behind(step)),
                device_id_type=pl.DeviceIdType.MESH,
            ).wait_recv()


def slot_block(shape, slot_axis, slot_rows):
    slots = lax.broadcasted_iota(jnp.int32, shape, slot_axis)
    block = lax.broadcasted_iota(jnp.int32, shape, 1 - slot_axis)
    return (slots >= block * slot_rows) & (slots < (block + 1) * slot_rows)


def moe_forward_kernel(
    dims,
    own_ref,
    place_ref,
    place_t_ref,
    member_ref,
    router_ref,
    gate_ref,
    up_ref,
    down_ref,
    sum_ref,
    gates_ref,
    slots_out,
    returned_out,
    tokens,
    send,
    slots,
    gate_val,
    up_val,
    act,
    returned,
    mix_t,
    landed,
    row_send,
    row_recv,
    there_send,
    there_recv,
    back_send,
    back_recv,
    home_send,
    home_recv,
    local_sem,
):
    group_rows, col_count, copies, token_rows, slot_rows, chunks, width = dims
    all_tokens = group_rows * token_rows
    all_slots = col_count * slot_rows
    slot_step = split_rows(all_slots, 320)
    rows, cols = expert_peers(col_count, copies, group_rows)

    def token_part(place):
        return pl.ds(pl.multiple_of(place * token_rows, token_rows), token_rows)

    def slot_part(place):
        return pl.ds(pl.multiple_of(place * slot_rows, slot_rows), slot_rows)

    gather = Exchange(
        rows,
        row_send,
        row_recv,
        lambda place, chunk: own_ref.at[:, chunk],
        lambda place, step, chunk: tokens.at[token_part(place), chunk],
    )
    there = Exchange(
        cols,
        there_send,
        there_recv,
        lambda place, chunk: send.at[slot_part(place), chunk],
        lambda place, step, chunk: slots.at[slot_part(place), chunk],
    )
    back = Exchange(
        cols,
        back_send,
        back_recv,
        lambda place, chunk: send.at[slot_part(place), chunk],
        lambda place, step, chunk: returned.at[slot_part(place), chunk],
    )
    home = Exchange(
        rows,
        home_send,
        home_recv,
        lambda place, chunk: tokens.at[token_part(place), chunk],
        lambda place, step, chunk: landed.at[step - 1, :, chunk],
    )
    greet((rows, cols))
    over_chunks(chunks, width, gather.start)
    tokens[token_part(rows.place), :] = own_ref[...]

    def dispatch(index, chunk):
        gather.wait_recv(index, chunk)

        def rows_of(part):
            send[part, chunk] = dot_nn(place_ref[part, :], tokens[:, chunk]).astype(jnp.bfloat16)

        over_blocks(all_slots, slot_step, rows_of)
        there.start(index, chunk)
        slots[slot_part(cols.place), chunk] = send[slot_part(cols.place), chunk]

    over_chunks(chunks, width, dispatch)

    def gating(part):
        member = member_ref[part, :] > 0
        logits = jnp.where(member, dot_nt(tokens[part, :], router_ref[...]), masked_score)
        peak = jnp.max(logits, axis=-1, keepdims=True)
        exponent = jnp.where(member, jnp.exp(logits - peak), 0.0)
        gates = exponent / jnp.sum(exponent, axis=-1, keepdims=True)
        gates_ref[part, :] = gates
        pick = slot_block((gates.shape[1], all_slots), 1, slot_rows).astype(jnp.bfloat16)
        spread = dot_nn(gates.astype(jnp.bfloat16), pick)
        mix_t[part, :] = (place_t_ref[part, :].astype(jnp.float32) * spread).astype(jnp.bfloat16)

    over_blocks(all_tokens, token_rows, gating)

    def project(index, chunk):
        there.wait_recv(index, chunk)

        def rows_of(part):
            gate_part = dot_nt(slots[part, chunk], gate_ref[:, chunk])
            up_part = dot_nt(slots[part, chunk], up_ref[:, chunk])

            @pl.when(index == 0)
            def _():
                gate_val[part, :] = gate_part
                up_val[part, :] = up_part

            @pl.when(index > 0)
            def _():
                gate_val[part, :] += gate_part
                up_val[part, :] += up_part

        over_blocks(all_slots, slot_step, rows_of)

    over_chunks(chunks, width, project)
    keep_slots = pltpu.make_async_copy(slots, slots_out, local_sem.at[0])
    keep_slots.start()

    def activate(part):
        value = gate_val[part, :]
        act[part, :] = (value * jax.nn.sigmoid(value) * up_val[part, :]).astype(jnp.bfloat16)

    over_blocks(all_slots, slot_step, activate)

    def give_back(index, chunk):
        there.wait_send(index, chunk)

        def rows_of(part):
            send[part, chunk] = dot_nn(act[part, :], down_ref[:, chunk]).astype(jnp.bfloat16)

        over_blocks(all_slots, slot_step, rows_of)
        back.start(index, chunk)
        returned[slot_part(cols.place), chunk] = send[slot_part(cols.place), chunk]

    over_chunks(chunks, width, give_back)

    def combine(index, chunk):
        back.wait_recv(index, chunk)

        def rows_of(part):
            tokens[part, chunk] = dot_nn(mix_t[part, :], returned[:, chunk]).astype(jnp.bfloat16)

        over_blocks(all_tokens, token_rows, rows_of)
        home.start(index, chunk)

    over_chunks(chunks, width, combine)
    keep_returned = pltpu.make_async_copy(returned, returned_out, local_sem.at[1])
    keep_returned.start()

    def finish(index, chunk):
        home.wait_recv(index, chunk)
        total = tokens[token_part(rows.place), chunk].astype(jnp.float32)
        for step in range(1, group_rows):
            total = total + landed[step - 1, :, chunk].astype(jnp.float32)
        sum_ref[:, chunk] = total

    over_chunks(chunks, width, finish)

    def drain(index, chunk):
        gather.wait_send(index, chunk)
        back.wait_send(index, chunk)
        home.wait_send(index, chunk)

    over_chunks(chunks, width, drain)
    keep_slots.wait()
    keep_returned.wait()


def moe_backward_kernel(
    dims,
    own_ref,
    place_ref,
    place_t_ref,
    gates_ref,
    slots_ref,
    returned_ref,
    gate_ref,
    up_ref,
    down_ref,
    sum_ref,
    pair_ref,
    act_out,
    grad_gate_out,
    grad_up_out,
    received_out,
    tokens,
    send,
    slope,
    silu,
    act,
    weight,
    inner,
    received,
    grad_act,
    grad_gate,
    grad_up,
    returned,
    landed,
    pair_send,
    pair_landed,
    row_send,
    row_recv,
    there_send,
    there_recv,
    back_send,
    back_recv,
    home_send,
    home_recv,
    pair_send_sem,
    pair_recv_sem,
    local_sem,
):
    group_rows, col_count, copies, token_rows, slot_rows, chunks, width = dims
    all_tokens = group_rows * token_rows
    all_slots = col_count * slot_rows
    slot_step = split_rows(all_slots, 320)
    rows, cols = expert_peers(col_count, copies, group_rows)

    def token_part(place):
        return pl.ds(pl.multiple_of(place * token_rows, token_rows), token_rows)

    def slot_part(place):
        return pl.ds(pl.multiple_of(place * slot_rows, slot_rows), slot_rows)

    gather = Exchange(
        rows,
        row_send,
        row_recv,
        lambda place, chunk: own_ref.at[:, chunk],
        lambda place, step, chunk: tokens.at[token_part(place), chunk],
    )
    there = Exchange(
        cols,
        there_send,
        there_recv,
        lambda place, chunk: send.at[slot_part(place), chunk],
        lambda place, step, chunk: received.at[slot_part(place), chunk],
    )
    back = Exchange(
        cols,
        back_send,
        back_recv,
        lambda place, chunk: send.at[slot_part(place), chunk],
        lambda place, step, chunk: returned.at[slot_part(place), chunk],
    )
    home = Exchange(
        rows,
        home_send,
        home_recv,
        lambda place, chunk: tokens.at[token_part(place), chunk],
        lambda place, step, chunk: landed.at[step - 1, :, chunk],
    )
    pair = Exchange(
        rows,
        pair_send_sem,
        pair_recv_sem,
        lambda place, chunk: pair_send.at[token_part(place), :],
        lambda place, step, chunk: pair_landed.at[step - 1],
    )
    greet((rows, cols))
    over_chunks(chunks, width, gather.start)
    tokens[token_part(rows.place), :] = own_ref[...]

    def recompute(part):
        gate_val = dot_nt(slots_ref[part, :], gate_ref[...])
        up_val = dot_nt(slots_ref[part, :], up_ref[...])
        sigmoid = jax.nn.sigmoid(gate_val)
        value = gate_val * sigmoid
        act[part, :] = (value * up_val).astype(jnp.bfloat16)
        silu[part, :] = value
        slope[part, :] = up_val * sigmoid * (1.0 + gate_val * (1.0 - sigmoid))
        picked = dot_nn(place_ref[part, :], gates_ref[...].astype(jnp.bfloat16))
        block = lax.broadcasted_iota(jnp.int32, picked.shape, 1)
        slot = lax.broadcasted_iota(jnp.int32, picked.shape, 0) + part.start
        in_block = (slot >= block * slot_rows) & (slot < (block + 1) * slot_rows)
        weight[part, :] = jnp.sum(jnp.where(in_block, picked, 0.0), axis=1, keepdims=True)

    over_blocks(all_slots, slot_step, recompute)

    def dispatch(index, chunk):
        gather.wait_recv(index, chunk)

        def rows_of(part):
            grad = dot_nn(place_ref[part, :], tokens[:, chunk])
            share = jnp.sum(
                grad * returned_ref[part, chunk].astype(jnp.float32), axis=1, keepdims=True
            )
            send[part, chunk] = (weight[part, :] * grad).astype(jnp.bfloat16)

            @pl.when(index == 0)
            def _():
                inner[part, :] = share

            @pl.when(index > 0)
            def _():
                inner[part, :] += share

        over_blocks(all_slots, slot_step, rows_of)
        there.start(index, chunk)
        received[slot_part(cols.place), chunk] = send[slot_part(cols.place), chunk]

    over_chunks(chunks, width, dispatch)

    def pairs(part):
        picked = slot_block((all_slots, pair_send.shape[1]), 0, slot_rows)
        spread = jnp.where(picked, inner[...], 0.0)
        high = spread.astype(jnp.bfloat16)
        low = (spread - high.astype(jnp.float32)).astype(jnp.bfloat16)
        pair_send[part, :] = dot_nn(place_t_ref[part, :], high) + dot_nn(place_t_ref[part, :], low)

    over_blocks(all_tokens, token_rows, pairs)
    pair.start(0, None)

    def project(index, chunk):
        there.wait_recv(index, chunk)

        def rows_of(part):
            grad = dot_nt(received[part, chunk], down_ref[:, chunk])

            @pl.when(index == 0)
            def _():
                grad_act[part, :] = grad

            @pl.when(index > 0)
            def _():
                grad_act[part, :] += grad

        over_blocks(all_slots, slot_step, rows_of)

    over_chunks(chunks, width, project)

    def slopes(part):
        grad = grad_act[part, :]
        grad_gate[part, :] = (grad * slope[part, :]).astype(jnp.bfloat16)
        grad_up[part, :] = (grad * silu[part, :]).astype(jnp.bfloat16)

    over_blocks(all_slots, slot_step, slopes)
    kept = [
        pltpu.make_async_copy(source, target, local_sem.at[number])
        for number, (source, target) in enumerate(
            (
                (act, act_out),
                (grad_gate, grad_gate_out),
                (grad_up, grad_up_out),
                (received, received_out),
            )
        )
    ]
    for copy in kept:
        copy.start()

    def give_back(index, chunk):
        there.wait_send(index, chunk)

        def rows_of(part):
            send[part, chunk] = (
                dot_nn(grad_gate[part, :], gate_ref[:, chunk])
                + dot_nn(grad_up[part, :], up_ref[:, chunk])
            ).astype(jnp.bfloat16)

        over_blocks(all_slots, slot_step, rows_of)
        back.start(index, chunk)
        returned[slot_part(cols.place), chunk] = send[slot_part(cols.place), chunk]

    over_chunks(chunks, width, give_back)

    def combine(index, chunk):
        back.wait_recv(index, chunk)

        def rows_of(part):
            tokens[part, chunk] = dot_nn(place_t_ref[part, :], returned[:, chunk]).astype(
                jnp.bfloat16
            )

        over_blocks(all_tokens, token_rows, rows_of)
        home.start(index, chunk)

    over_chunks(chunks, width, combine)
    pair.wait_recv(0, None)
    pair_total = pair_send[token_part(rows.place), :]
    pair_ref[0] = pair_total
    for step in range(1, group_rows):
        pair_ref[step] = pair_landed[step - 1]

    def finish(index, chunk):
        home.wait_recv(index, chunk)
        total = tokens[token_part(rows.place), chunk].astype(jnp.float32)
        for step in range(1, group_rows):
            total = total + landed[step - 1, :, chunk].astype(jnp.float32)
        sum_ref[:, chunk] = total

    over_chunks(chunks, width, finish)

    def drain(index, chunk):
        gather.wait_send(index, chunk)
        back.wait_send(index, chunk)
        home.wait_send(index, chunk)

    over_chunks(chunks, width, drain)
    pair.wait_send(0, None)
    for copy in kept:
        copy.wait()


vmem_most = 60 * 1024 * 1024


def exchange_sems(chunks, count):
    return [pltpu.SemaphoreType.DMA((chunks, max(count - 1, 1))) for _ in range(2)]


def moe_forward(dims, own, place, place_t, member, router, gate, up, down):
    group_rows, col_count, copies, token_rows, slot_rows, chunks, width = dims
    all_tokens, all_slots = group_rows * token_rows, col_count * slot_rows
    model_width, hidden = own.shape[1], gate.shape[0]
    vmem = pl.BlockSpec(memory_space=pltpu.VMEM)
    outside = pl.BlockSpec(memory_space=pl.ANY)
    slot_array = pltpu.VMEM((all_slots, model_width), jnp.bfloat16)
    flops = 2 * all_slots * model_width * (3 * hidden + 2 * all_tokens)
    return pl.pallas_call(
        functools.partial(moe_forward_kernel, dims),
        out_shape=(
            jax.ShapeDtypeStruct((token_rows, model_width), jnp.float32),
            jax.ShapeDtypeStruct((all_tokens, member.shape[1]), jnp.float32),
            jax.ShapeDtypeStruct((all_slots, model_width), jnp.bfloat16),
            jax.ShapeDtypeStruct((all_slots, model_width), jnp.bfloat16),
        ),
        in_specs=[vmem] * 8,
        out_specs=(vmem, vmem, outside, outside),
        scratch_shapes=[
            pltpu.VMEM((all_tokens, model_width), jnp.bfloat16),
            slot_array,
            slot_array,
            pltpu.VMEM((all_slots, hidden), jnp.float32),
            pltpu.VMEM((all_slots, hidden), jnp.float32),
            pltpu.VMEM((all_slots, hidden), jnp.bfloat16),
            slot_array,
            pltpu.VMEM((all_tokens, all_slots), jnp.bfloat16),
            pltpu.VMEM((group_rows - 1, token_rows, model_width), jnp.bfloat16),
            *exchange_sems(chunks, group_rows),
            *exchange_sems(chunks, col_count),
            *exchange_sems(chunks, col_count),
            *exchange_sems(chunks, group_rows),
            pltpu.SemaphoreType.DMA((2,)),
        ],
        compiler_params=pltpu.CompilerParams(
            collective_id=1, has_side_effects=True, vmem_limit_bytes=vmem_most
        ),
        cost_estimate=pl.CostEstimate(
            flops=flops, bytes_accessed=40 * 1024 * 1024, transcendentals=all_slots * hidden
        ),
        name="moe_forward",
    )(own, place, place_t, member, router, gate, up, down)


def moe_backward(dims, own, place, place_t, gates, slots, returned, gate, up, down):
    group_rows, col_count, copies, token_rows, slot_rows, chunks, width = dims
    all_tokens, all_slots = group_rows * token_rows, col_count * slot_rows
    model_width, hidden = own.shape[1], gate.shape[0]
    vmem = pl.BlockSpec(memory_space=pltpu.VMEM)
    outside = pl.BlockSpec(memory_space=pl.ANY)
    slot_array = pltpu.VMEM((all_slots, model_width), jnp.bfloat16)
    hidden_wide = pltpu.VMEM((all_slots, hidden), jnp.float32)
    hidden_narrow = pltpu.VMEM((all_slots, hidden), jnp.bfloat16)
    flops = 2 * all_slots * model_width * (6 * hidden + 2 * all_tokens)
    return pl.pallas_call(
        functools.partial(moe_backward_kernel, dims),
        out_shape=(
            jax.ShapeDtypeStruct((token_rows, model_width), jnp.float32),
            jax.ShapeDtypeStruct((group_rows, token_rows, 128), jnp.float32),
            jax.ShapeDtypeStruct((all_slots, hidden), jnp.bfloat16),
            jax.ShapeDtypeStruct((all_slots, hidden), jnp.bfloat16),
            jax.ShapeDtypeStruct((all_slots, hidden), jnp.bfloat16),
            jax.ShapeDtypeStruct((all_slots, model_width), jnp.bfloat16),
        ),
        in_specs=[vmem] * 9,
        out_specs=(vmem, vmem, outside, outside, outside, outside),
        scratch_shapes=[
            pltpu.VMEM((all_tokens, model_width), jnp.bfloat16),
            slot_array,
            hidden_wide,
            hidden_wide,
            hidden_narrow,
            pltpu.VMEM((all_slots, 1), jnp.float32),
            pltpu.VMEM((all_slots, 1), jnp.float32),
            slot_array,
            hidden_wide,
            hidden_narrow,
            hidden_narrow,
            slot_array,
            pltpu.VMEM((group_rows - 1, token_rows, model_width), jnp.bfloat16),
            pltpu.VMEM((all_tokens, 128), jnp.float32),
            pltpu.VMEM((group_rows - 1, token_rows, 128), jnp.float32),
            *exchange_sems(chunks, group_rows),
            *exchange_sems(chunks, col_count),
            *exchange_sems(chunks, col_count),
            *exchange_sems(chunks, group_rows),
            *exchange_sems(1, group_rows),
            pltpu.SemaphoreType.DMA((4,)),
        ],
        compiler_params=pltpu.CompilerParams(
            collective_id=2, has_side_effects=True, vmem_limit_bytes=vmem_most
        ),
        cost_estimate=pl.CostEstimate(
            flops=flops, bytes_accessed=50 * 1024 * 1024, transcendentals=all_slots * hidden
        ),
        name="moe_backward",
    )(own, place, place_t, gates, slots, returned, gate, up, down)


def col_pairs():
    col_index = lax.axis_index("col")
    return col_index // 2, lax.rem(col_index, 2)


def send_to(source, target, sems, number, device):
    send_sems, recv_sems = sems
    return pltpu.make_async_remote_copy(
        src_ref=source,
        dst_ref=target,
        send_sem=send_sems.at[number],
        recv_sem=recv_sems.at[number],
        device_id=device,
        device_id_type=pl.DeviceIdType.MESH,
    )


def dense_peers(row_count, pair_count):
    row_index = lax.axis_index("row")
    pair, side = col_pairs()
    rows = Peers(row_count, row_index, lambda place: {"row": place})
    pairs = Peers(pair_count, pair, lambda place: {"col": place * 2 + side})
    sides = Peers(2, side, lambda place: {"col": pair * 2 + place})
    return rows, pairs, sides


def reduce_dense_kernel(
    dims,
    normed_ref,
    grad_proj_ref,
    grad_mid_ref,
    attended_ref,
    small_ref,
    qkv_ref,
    out_ref,
    small_out_ref,
    *scratch,
):
    row_count, pair_count = dims
    kinds = 3
    buffers = [scratch[6 * kind : 6 * kind + 6] for kind in range(kinds)]
    sems = scratch[6 * kinds :]
    side_sems = [(sems[6 * kind], sems[6 * kind + 1]) for kind in range(kinds)]
    pair_sems = [(sems[6 * kind + 2], sems[6 * kind + 3]) for kind in range(kinds)]
    row_sems = [(sems[6 * kind + 4], sems[6 * kind + 5]) for kind in range(kinds)]
    rows, pairs, sides = dense_peers(row_count, pair_count)
    other = 1 - sides.place

    def block(kind, row, pair, side):
        col = pair * 2 + side
        if kind == 0:
            return dot_nn(normed_ref[row], grad_proj_ref[col])
        if kind == 1:
            return dot_nn(grad_mid_ref[col], attended_ref[row])
        return small_ref[col, row].astype(jnp.float32)

    greet((rows, pairs, sides))
    outputs = (qkv_ref, out_ref, small_out_ref)

    def side_copy(kind, pair):
        side_send, side_recv = buffers[kind][0], buffers[kind][1]
        return send_to(
            side_send.at[pair],
            side_recv.at[pair],
            side_sems[kind],
            pair,
            sides.device_of(other),
        )

    def pair_copy(kind, step, row):
        place = pairs.ahead(step)
        half, pair_recv = buffers[kind][2], buffers[kind][3]
        return send_to(
            half.at[place, row],
            pair_recv.at[step - 1, row],
            pair_sems[kind],
            (step - 1) * row_count + row,
            pairs.device_of(place),
        )

    def row_copy(kind, step):
        place = rows.ahead(step)
        whole, row_recv = buffers[kind][4], buffers[kind][5]
        return send_to(
            whole.at[place],
            row_recv.at[step - 1],
            row_sems[kind],
            step - 1,
            rows.device_of(place),
        )

    def first(step, carry):
        pair = lax.rem(pairs.place + step, pair_count)
        for kind in range(kinds):
            for row in range(row_count):
                buffers[kind][0][pair, row] = block(kind, row, pair, other).astype(jnp.bfloat16)
            side_copy(kind, pair).start()
        return carry

    lax.fori_loop(1, pair_count + 1, first, 0)

    def second(step, carry):
        pair = lax.rem(pairs.place + step, pair_count)
        for kind in range(kinds):
            side_copy(kind, pair).wait_recv()
            side_recv, half = buffers[kind][1], buffers[kind][2]
            for row in range(row_count):
                total = block(kind, row, pair, sides.place)
                total = total + side_recv[pair, row].astype(jnp.float32)
                half[pair, row] = total.astype(jnp.bfloat16)

                @pl.when(step < pair_count)
                def _():
                    pair_copy(kind, step, row).start()

        return carry

    lax.fori_loop(1, pair_count + 1, second, 0)

    def third(step, carry):
        row = lax.rem(rows.place + step, row_count)
        for kind in range(kinds):
            half, pair_recv, whole = buffers[kind][2], buffers[kind][3], buffers[kind][4]
            total = half[pairs.place, row].astype(jnp.float32)
            for ahead in range(1, pair_count):
                pair_copy(kind, ahead, row).wait_recv()
                total = total + pair_recv[ahead - 1, row].astype(jnp.float32)

            whole[row] = total.astype(jnp.bfloat16)

            @pl.when(step < row_count)
            def _():
                row_copy(kind, step).start()

        return carry

    lax.fori_loop(1, row_count + 1, third, 0)
    for kind in range(kinds):
        whole, row_recv = buffers[kind][4], buffers[kind][5]
        total = whole[rows.place].astype(jnp.float32)
        for step in range(1, row_count):
            row_copy(kind, step).wait_recv()
            total = total + row_recv[step - 1].astype(jnp.float32)
        outputs[kind][...] = total

    def drain_sides(pair, carry):
        for kind in range(kinds):
            side_copy(kind, pair).wait_send()
        return carry

    lax.fori_loop(0, pair_count, drain_sides, 0)

    def drain_pairs(step, carry):
        for kind in range(kinds):
            for row in range(row_count):
                pair_copy(kind, step, row).wait_send()
        return carry

    lax.fori_loop(1, pair_count, drain_pairs, 0)
    for kind in range(kinds):
        for step in range(1, row_count):
            row_copy(kind, step).wait_send()


def reduce_dense(row_count, col_count, normed, grad_projected, grad_mid_b, attended, small):
    token_rows, model_width = normed.shape
    qkv_width, out_rows = grad_projected.shape[1], attended.shape[1]
    pair_count = col_count // 2
    shapes = (
        (model_width // row_count, qkv_width // col_count),
        (model_width // col_count, out_rows // row_count),
        small.shape[2:],
    )
    vmem = pl.BlockSpec(memory_space=pltpu.VMEM)
    scratch = []
    sems = []
    for height, breadth in shapes:
        for lead in (
            (pair_count, row_count),
            (pair_count, row_count),
            (pair_count, row_count),
            (max(pair_count - 1, 1), row_count),
            (row_count,),
            (max(row_count - 1, 1),),
        ):
            scratch.append(pltpu.VMEM((*lead, height, breadth), jnp.bfloat16))
        for count in (pair_count, max(pair_count - 1, 1) * row_count, max(row_count - 1, 1)):
            sems.extend([pltpu.SemaphoreType.DMA((count,))] * 2)
    return pl.pallas_call(
        functools.partial(reduce_dense_kernel, (row_count, pair_count)),
        out_shape=tuple(jax.ShapeDtypeStruct(shape, jnp.float32) for shape in shapes),
        in_specs=[vmem] * 5,
        out_specs=(vmem,) * 3,
        scratch_shapes=scratch + sems,
        compiler_params=pltpu.CompilerParams(
            collective_id=3, has_side_effects=True, vmem_limit_bytes=vmem_most
        ),
        cost_estimate=pl.CostEstimate(
            flops=2 * token_rows * model_width * (qkv_width + out_rows),
            bytes_accessed=8 * 1024 * 1024,
            transcendentals=0,
        ),
        name="reduce_dense",
    )(
        normed.T.reshape(row_count, -1, token_rows),
        grad_projected.reshape(token_rows, col_count, -1).transpose(1, 0, 2),
        grad_mid_b.T.reshape(col_count, -1, token_rows),
        attended.reshape(token_rows, row_count, -1).transpose(1, 0, 2),
        small,
    )


def gather_dense_kernel(dims, qkv_ref, out_ref, qkv_full, out_full, *sems):
    row_count, pair_count = dims
    rows, pairs, sides = dense_peers(row_count, pair_count)
    other = 1 - sides.place
    kinds = 2
    own_blocks = (qkv_ref, out_ref)
    height, breadth = qkv_ref.shape
    out_height = out_ref.shape[0]
    row_sems = [(sems[6 * kind], sems[6 * kind + 1]) for kind in range(kinds)]
    pair_sems = [(sems[6 * kind + 2], sems[6 * kind + 3]) for kind in range(kinds)]
    side_sems = [(sems[6 * kind + 4], sems[6 * kind + 5]) for kind in range(kinds)]
    local_sems = sems[6 * kinds]

    def spot(kind, row, pair, side):
        col = pair * 2 + side
        if kind == 0:
            return qkv_full.at[
                pl.ds(pl.multiple_of(row * height, height), height),
                pl.ds(pl.multiple_of(col * breadth, breadth), breadth),
            ]
        return out_full.at[row, pl.ds(pl.multiple_of(col * out_height, out_height), out_height), :]

    def row_copy(kind, step):
        target = spot(kind, rows.place, pairs.place, sides.place)
        return send_to(
            own_blocks[kind], target, row_sems[kind], step - 1, rows.device_of(rows.ahead(step))
        )

    def row_landed(kind, step):
        landed = spot(kind, rows.behind(step), pairs.place, sides.place)
        return send_to(
            landed, landed, row_sems[kind], step - 1, rows.device_of(rows.behind(step))
        )

    def pair_copy(kind, step, row, number):
        block = spot(kind, row, pairs.place, sides.place)
        return send_to(
            block if number else own_blocks[kind],
            block,
            pair_sems[kind],
            (step - 1) * row_count + number,
            pairs.device_of(pairs.ahead(step)),
        )

    def pair_landed(kind, step, number):
        row = rows.behind(number)
        landed = spot(kind, row, pairs.behind(step), sides.place)
        return send_to(
            landed,
            landed,
            pair_sems[kind],
            (step - 1) * row_count + number,
            pairs.device_of(pairs.behind(step)),
        )

    def side_copy(kind, step, number):
        block = spot(kind, rows.behind(number), pairs.behind(step), sides.place)
        source = own_blocks[kind] if step == 0 and number == 0 else block
        return send_to(
            source,
            block,
            side_sems[kind],
            step * row_count + number,
            sides.device_of(other),
        )

    def side_landed(kind, step, number):
        landed = spot(kind, rows.behind(number), pairs.behind(step), other)
        return send_to(
            landed,
            landed,
            side_sems[kind],
            step * row_count + number,
            sides.device_of(other),
        )

    greet((rows, pairs, sides))
    own_copies = []
    for kind in range(kinds):
        copy = pltpu.make_async_copy(
            own_blocks[kind],
            spot(kind, rows.place, pairs.place, sides.place),
            local_sems.at[kind],
        )
        copy.start()
        own_copies.append(copy)
    for kind in range(kinds):
        for step in range(1, row_count):
            row_copy(kind, step).start()
        for step in range(1, pair_count):
            pair_copy(kind, step, rows.place, 0).start()
        side_copy(kind, 0, 0).start()
    for kind in range(kinds):
        for number in range(1, row_count):
            row_landed(kind, number).wait_recv()
            for step in range(1, pair_count):
                pair_copy(kind, step, rows.behind(number), number).start()
            side_copy(kind, 0, number).start()
    for kind in range(kinds):
        for number in range(row_count):
            for step in range(1, pair_count):
                pair_landed(kind, step, number).wait_recv()
                side_copy(kind, step, number).start()
    for kind in range(kinds):
        for step in range(pair_count):
            for number in range(row_count):
                side_landed(kind, step, number).wait_recv()
    for kind in range(kinds):
        own_copies[kind].wait()
        for step in range(1, row_count):
            row_copy(kind, step).wait_send()
        for number in range(row_count):
            for step in range(1, pair_count):
                pair_copy(kind, step, rows.behind(number), number).wait_send()
            for step in range(pair_count):
                side_copy(kind, step, number).wait_send()


def gather_dense(row_count, col_count, qkv_block, out_block):
    height, breadth = qkv_block.shape
    out_height, out_breadth = out_block.shape
    pair_count = col_count // 2
    outside = pl.BlockSpec(memory_space=pl.ANY)
    sems = []
    for _ in range(2):
        for count in (
            max(row_count - 1, 1),
            max(pair_count - 1, 1) * row_count,
            pair_count * row_count,
        ):
            sems.extend([pltpu.SemaphoreType.DMA((count,))] * 2)
    return pl.pallas_call(
        functools.partial(gather_dense_kernel, (row_count, pair_count)),
        out_shape=(
            jax.ShapeDtypeStruct((row_count * height, col_count * breadth), qkv_block.dtype),
            jax.ShapeDtypeStruct((row_count, col_count * out_height, out_breadth), out_block.dtype),
        ),
        in_specs=[outside] * 2,
        out_specs=(outside,) * 2,
        scratch_shapes=sems + [pltpu.SemaphoreType.DMA((2,))],
        compiler_params=pltpu.CompilerParams(collective_id=4, has_side_effects=True),
        name="gather_dense",
    )(qkv_block, out_block)


def attend_forward_kernel(score_scale, q_ref, kv_ref, value_t_ref, out_ref, lse_ref):
    token_rows = q_ref.shape[0]
    group = QUERY_HEADS // KEY_VALUE_HEADS
    position = lax.axis_index("col") * token_rows + lax.broadcasted_iota(
        jnp.int32, (1, token_rows), 1
    )
    seen = (position // BLOCK + 1) * BLOCK

    def head(index, carry):
        kv_head = index // group
        lanes = pl.ds(pl.multiple_of(index * HEAD_SIZE, HEAD_SIZE), HEAD_SIZE)
        kv_lanes = pl.ds(pl.multiple_of(kv_head * HEAD_SIZE, HEAD_SIZE), HEAD_SIZE)
        scores = dot_nt(kv_ref[:, kv_lanes], q_ref[:, lanes]) * score_scale
        key = lax.broadcasted_iota(jnp.int32, scores.shape, 0)
        scores = jnp.where(key < seen, scores, masked_score)
        peak = jnp.max(scores, axis=0, keepdims=True)
        exponent = jnp.exp(scores - peak)
        total = jnp.sum(exponent, axis=0, keepdims=True)
        attended = dot_nn(value_t_ref[kv_lanes, :], exponent.astype(jnp.bfloat16)) / total
        out_ref[:, lanes] = attended.T.astype(jnp.bfloat16)
        lse_ref[index] = peak + jnp.log(total)
        return carry

    lax.fori_loop(0, QUERY_HEADS, head, 0)


def attend_forward(queries_b, key_value_full, value_t, score_scale):
    token_rows = queries_b.shape[0]
    seq_rows = key_value_full.shape[0]
    vmem = pl.BlockSpec(memory_space=pltpu.VMEM)
    return pl.pallas_call(
        functools.partial(attend_forward_kernel, score_scale),
        out_shape=(
            jax.ShapeDtypeStruct(queries_b.shape, jnp.bfloat16),
            jax.ShapeDtypeStruct((QUERY_HEADS, 1, token_rows), jnp.float32),
        ),
        in_specs=[vmem] * 3,
        out_specs=(vmem, vmem),
        compiler_params=pltpu.CompilerParams(vmem_limit_bytes=vmem_most),
        cost_estimate=pl.CostEstimate(
            flops=4 * token_rows * seq_rows * QUERY_FEATURES,
            bytes_accessed=6 * 1024 * 1024,
            transcendentals=token_rows * seq_rows * QUERY_HEADS,
        ),
        name="attend_forward",
    )(queries_b, key_value_full, value_t)


def attend_backward_kernel(
    score_scale,
    q_ref,
    kv_ref,
    key_t_ref,
    lse_ref,
    inner_ref,
    grad_ref,
    grad_q_ref,
    grad_kv_ref,
    key_sum,
    value_sum,
):
    token_rows = q_ref.shape[0]
    group = QUERY_HEADS // KEY_VALUE_HEADS
    position = lax.axis_index("col") * token_rows + lax.broadcasted_iota(
        jnp.int32, (1, token_rows), 1
    )
    seen = (position // BLOCK + 1) * BLOCK
    for kv_head in range(KEY_VALUE_HEADS):
        kv_lanes = slice(kv_head * HEAD_SIZE, (kv_head + 1) * HEAD_SIZE)
        value_lanes = slice(
            (KEY_VALUE_HEADS + kv_head) * HEAD_SIZE, (KEY_VALUE_HEADS + kv_head + 1) * HEAD_SIZE
        )
        key_sum[...] = jnp.zeros_like(key_sum)
        value_sum[...] = jnp.zeros_like(value_sum)

        def head(step, carry, kv_lanes=kv_lanes, value_lanes=value_lanes, kv_head=kv_head):
            index = kv_head * group + step
            lanes = pl.ds(pl.multiple_of(index * HEAD_SIZE, HEAD_SIZE), HEAD_SIZE)
            query = q_ref[:, lanes]
            grad = grad_ref[:, lanes]
            scores = dot_nt(kv_ref[:, kv_lanes], query) * score_scale
            key = lax.broadcasted_iota(jnp.int32, scores.shape, 0)
            soft = jnp.where(key < seen, jnp.exp(scores - lse_ref[index]), 0.0)
            grad_soft = dot_nt(kv_ref[:, value_lanes], grad)
            grad_scores = (soft * (grad_soft - inner_ref[index])).astype(jnp.bfloat16)
            value_sum[...] += dot_nn(soft.astype(jnp.bfloat16), grad)
            key_sum[...] += dot_nn(grad_scores, query)
            grad_q = dot_nn(key_t_ref[kv_lanes, :], grad_scores) * score_scale
            grad_q_ref[:, lanes] = grad_q.T.astype(jnp.bfloat16)
            return carry

        lax.fori_loop(0, group, head, 0)
        grad_kv_ref[:, kv_lanes] = (key_sum[...] * score_scale).astype(jnp.bfloat16)
        grad_kv_ref[:, value_lanes] = value_sum[...].astype(jnp.bfloat16)


def attend_backward(queries_b, key_value_full, key_t, score_scale, log_sums, inner, grad_out_b):
    token_rows = queries_b.shape[0]
    seq_rows = key_value_full.shape[0]
    vmem = pl.BlockSpec(memory_space=pltpu.VMEM)
    return pl.pallas_call(
        functools.partial(attend_backward_kernel, score_scale),
        out_shape=(
            jax.ShapeDtypeStruct(queries_b.shape, jnp.bfloat16),
            jax.ShapeDtypeStruct(key_value_full.shape, jnp.bfloat16),
        ),
        in_specs=[vmem] * 6,
        out_specs=(vmem, vmem),
        scratch_shapes=[pltpu.VMEM((seq_rows, HEAD_SIZE), jnp.float32)] * 2,
        compiler_params=pltpu.CompilerParams(vmem_limit_bytes=vmem_most),
        cost_estimate=pl.CostEstimate(
            flops=10 * token_rows * seq_rows * QUERY_FEATURES,
            bytes_accessed=10 * 1024 * 1024,
            transcendentals=token_rows * seq_rows * QUERY_HEADS,
        ),
        name="attend_backward",
    )(queries_b, key_value_full, key_t, log_sums, inner, grad_out_b)


def layer_routing(route_rows, dims, expert_pick):
    group_rows, col_count, copies, token_rows, slot_rows, chunks, width = dims
    expert_ids = jnp.arange(E, dtype=jnp.int32)
    member = jnp.any(route_rows[..., None] == expert_ids, axis=2)
    earlier = (
        jnp.arange(token_rows)[None, :] < jnp.arange(token_rows)[:, None]
    ).astype(narrow_type)
    before = jnp.einsum(
        "ts,gse->gte", earlier, member.astype(narrow_type), preferred_element_type=wide_type
    )
    slot_number = jnp.where(member, before, -1.0).reshape(group_rows * token_rows, E)
    slot_number = place_first(slot_number, group_rows, expert_pick)
    mine = slot_number[:, :col_count]
    token_group = jnp.arange(group_rows * token_rows, dtype=jnp.int32) // token_rows
    slot_group = jnp.arange(slot_rows, dtype=jnp.int32) // CAP
    slot_index = (jnp.arange(slot_rows, dtype=jnp.int32) % CAP).astype(wide_type)
    same_group = slot_group[:, None] == token_group[None, :]
    place = same_group[None] & (mine.T[:, None, :] == slot_index[None, :, None])
    place = place.astype(narrow_type).reshape(col_count * slot_rows, -1)
    return ((slot_number >= 0).astype(wide_type), place, place.T)


def place_first(values, group_rows, expert_pick):
    tokens = values.shape[0]
    rolled = jnp.roll(values.reshape(tokens, -1, group_rows), -expert_pick, axis=2)
    return rolled.transpose(0, 2, 1).reshape(tokens, E)


def place_back(values, group_rows, expert_pick):
    tokens = values.shape[0]
    rolled = values.reshape(tokens, group_rows, -1).transpose(0, 2, 1)
    return jnp.roll(rolled, expert_pick, axis=2).reshape(tokens, E)


def body(
    hidden_in, routes, norm_attn, w_qkv, w_out, norm_moe, w_router, w_gate, w_up, w_down, cotangent
):
    row_count = lax.axis_size("row")
    col_count = lax.axis_size("col")
    device_count = row_count * col_count
    row_index = lax.axis_index("row")
    col_index = lax.axis_index("col")
    layer_count = w_qkv.shape[0]
    token_rows = hidden_in.shape[0]
    model_width = hidden_in.shape[1]
    local_experts = w_gate.shape[1]
    slice_width = w_gate.shape[3]
    expert_width = slice_width * row_count
    copies = row_count // local_experts
    expert_pick = row_index // copies
    if copies > 1:
        token_rows_of = [[s + copies * i for i in range(local_experts)] for s in range(copies)]
    else:
        token_rows_of = None
    slot_rows = -(-local_experts * CAP // 16) * 16
    chunks = model_width // 384
    dims = (
        local_experts,
        col_count,
        copies,
        token_rows,
        slot_rows,
        chunks,
        model_width // chunks,
    )
    key_value_width = KEY_VALUE_HEADS * HEAD_SIZE
    positions = col_index * token_rows + jnp.arange(token_rows, dtype=jnp.int32)
    cosine_table, sine_table_rows = rope_angles(positions, HEAD_SIZE // 2)
    score_scale = HEAD_SIZE ** (-0.5)

    def own_tokens(rows):
        return lax.dynamic_slice_in_dim(rows, expert_pick * token_rows, token_rows, axis=0)

    def move_weights(block):
        spread = jnp.repeat(block, copies, axis=0) if copies > 1 else block
        return lax.all_to_all(spread, "row", split_axis=0, concat_axis=0, tiled=True).reshape(
            expert_width, model_width
        )

    def move_grads(full):
        spread = full.astype(narrow_type).reshape(row_count, slice_width, model_width)
        got = lax.all_to_all(spread, "row", split_axis=0, concat_axis=0, tiled=True)
        got = got.astype(wide_type)
        if copies > 1:
            got = jnp.sum(
                got.reshape(local_experts, copies, slice_width, model_width), axis=1
            )
        return got

    router_t = lax.all_gather(w_router.transpose(0, 2, 1), "row", axis=2, tiled=True)
    routers = [place_first(router_t[index].T, local_experts, expert_pick).T for index in range(layer_count)]
    routes_all = lax.all_gather(routes, "row", axis=0, axis_index_groups=token_rows_of)
    hidden = hidden_in.astype(wide_type)
    saved = []
    for layer_index in range(layer_count):
        layer_state = {}
        gain_attn = norm_attn[layer_index].astype(wide_type)
        gain_moe = norm_moe[layer_index].astype(wide_type)
        if layer_index == 0:
            qkv_full, out_full = gather_dense(
                row_count, col_count, w_qkv[layer_index], w_out[layer_index].T
            )
            out_full = out_full.transpose(0, 2, 1).reshape(QUERY_FEATURES, model_width)
        else:
            qkv_full = to_full(
                lax.all_gather(w_qkv[layer_index][None], ("row", "col"), axis=0, tiled=True),
                row_count,
                col_count,
            )
            out_full = to_full(
                lax.all_gather(w_out[layer_index][None], ("row", "col"), axis=0, tiled=True),
                row_count,
                col_count,
            )
        dense = (qkv_full, out_full)
        gate_full = move_weights(w_gate[layer_index].transpose(0, 2, 1))
        up_full = move_weights(w_up[layer_index].transpose(0, 2, 1))
        down_full = move_weights(w_down[layer_index])
        normed, inverse_attn = rms_parts(hidden, gain_attn)
        normed_b = normed.astype(narrow_type)
        projected_rows = jnp.dot(normed_b, dense[0], preferred_element_type=wide_type)
        queries_b = rotate_heads(
            projected_rows[:, :QUERY_FEATURES].reshape(token_rows, QUERY_HEADS, HEAD_SIZE),
            cosine_table,
            sine_table_rows,
            1.0,
        ).astype(narrow_type)
        keys_b = (
            rotate_heads(
                projected_rows[:, QUERY_FEATURES : QUERY_FEATURES + key_value_width].reshape(
                    token_rows, KEY_VALUE_HEADS, HEAD_SIZE
                ),
                cosine_table,
                sine_table_rows,
                1.0,
            )
            .reshape(token_rows, key_value_width)
            .astype(narrow_type)
        )
        kv_local = jnp.concatenate(
            [keys_b, projected_rows[:, QUERY_FEATURES + key_value_width :].astype(narrow_type)],
            axis=1,
        )
        key_value_full = fetch_keys(kv_local)
        key_value_t = key_value_full.T
        attended_b, log_sums = attend_forward(
            queries_b.reshape(token_rows, QUERY_FEATURES),
            key_value_full,
            key_value_t[key_value_width:],
            score_scale,
        )
        attn_proj = jnp.dot(attended_b, dense[1], preferred_element_type=wide_type)
        hidden_mid = hidden + attn_proj
        normed_moe, inverse_moe = rms_parts(hidden_mid, gain_moe)
        normed_moe_b = normed_moe.astype(narrow_type)
        member, place, place_t = layer_routing(routes_all[:, layer_index], dims, expert_pick)
        mixed, gates, slot_inputs, returned = moe_forward(
            dims,
            normed_moe_b,
            place,
            place_t,
            member,
            routers[layer_index],
            gate_full,
            up_full,
            down_full,
        )
        hidden_next = hidden_mid + mixed
        layer_state["dense"] = dense
        layer_state["experts"] = (gate_full, up_full, down_full)
        layer_state["hidden"] = hidden
        layer_state["normed"] = normed_b
        layer_state["inverse_attn"] = inverse_attn
        layer_state["queries"] = queries_b
        layer_state["key_value"] = (key_value_full, key_value_t[:key_value_width])
        layer_state["log_sums"] = log_sums
        layer_state["attended"] = attended_b
        layer_state["hidden_mid"] = hidden_mid
        layer_state["inverse_moe"] = inverse_moe
        layer_state["normed_moe"] = normed_moe_b
        layer_state["gates"] = gates
        layer_state["place"] = (place, place_t)
        layer_state["slot_inputs"] = slot_inputs
        layer_state["returned"] = returned
        saved.append(layer_state)
        hidden = hidden_next
    incoming = cotangent.astype(wide_type)
    dense_results = [None] * layer_count
    small_results = [None] * layer_count
    expert_results = [None] * layer_count
    for layer_index in reversed(range(layer_count)):
        layer_state = saved[layer_index]
        gain_attn = norm_attn[layer_index].astype(wide_type)
        gain_moe = norm_moe[layer_index].astype(wide_type)
        dense = layer_state["dense"]
        gate_full, up_full, down_full = layer_state["experts"]
        key_value_full, key_t = layer_state["key_value"]
        slot_inputs = layer_state["slot_inputs"]
        place, place_t = layer_state["place"]
        (
            grad_tokens,
            grad_pair,
            activated_b,
            grad_gate_b,
            grad_up_b,
            grad_received,
        ) = moe_backward(
            dims,
            incoming.astype(narrow_type),
            place,
            place_t,
            layer_state["gates"],
            slot_inputs,
            layer_state["returned"],
            gate_full,
            up_full,
            down_full,
        )
        gates = place_back(own_tokens(layer_state["gates"]), local_experts, expert_pick)
        places = (expert_pick - jnp.arange(local_experts)) % local_experts
        grad_pair = jnp.take(grad_pair[:, :, :col_count], places, axis=0)
        grad_pair = grad_pair.transpose(1, 2, 0).reshape(token_rows, E)
        expert_results[layer_index] = (
            move_grads(
                jnp.einsum(
                    "cf,cd->fd", grad_gate_b, slot_inputs, preferred_element_type=wide_type
                )
            ).transpose(0, 2, 1),
            move_grads(
                jnp.einsum("cf,cd->fd", grad_up_b, slot_inputs, preferred_element_type=wide_type)
            ).transpose(0, 2, 1),
            move_grads(
                jnp.einsum(
                    "cf,cd->fd", activated_b, grad_received, preferred_element_type=wide_type
                )
            ),
        )
        grad_logits = gates * (grad_pair - jnp.sum(gates * grad_pair, axis=-1, keepdims=True))
        grad_logits_high = grad_logits.astype(narrow_type)
        grad_normed_moe = grad_tokens + jnp.dot(
            grad_logits_high, router_t[layer_index], preferred_element_type=wide_type
        )
        grad_router = jnp.einsum(
            "td,te->de",
            layer_state["normed_moe"],
            grad_logits_high,
            preferred_element_type=wide_type,
        )
        grad_mid_norm, grad_gain_moe = rms_backward(
            layer_state["hidden_mid"], layer_state["inverse_moe"], gain_moe, grad_normed_moe
        )
        grad_mid = incoming + grad_mid_norm
        grad_attn_b = grad_mid.astype(narrow_type)
        grad_attended_b = jnp.einsum(
            "td,ad->ta", grad_attn_b, dense[1], preferred_element_type=wide_type
        ).astype(narrow_type)
        inner = jnp.sum(
            (grad_attended_b.astype(wide_type) * layer_state["attended"].astype(wide_type)).reshape(
                token_rows, QUERY_HEADS, HEAD_SIZE
            ),
            axis=-1,
        ).T[:, None, :]
        grad_queries, grad_kv_full = attend_backward(
            layer_state["queries"].reshape(token_rows, QUERY_FEATURES),
            key_value_full,
            key_t,
            score_scale,
            layer_state["log_sums"],
            inner,
            grad_attended_b,
        )
        grad_queries = grad_queries.reshape(token_rows, QUERY_HEADS, HEAD_SIZE).astype(wide_type)
        key_value_gradient = lax.psum_scatter(
            grad_kv_full, "col", scatter_dimension=0, tiled=True
        ).astype(wide_type)
        grad_queries = rotate_heads(grad_queries, cosine_table, sine_table_rows, -1.0).reshape(
            token_rows, QUERY_FEATURES
        )
        grad_keys = rotate_heads(
            key_value_gradient[:, :key_value_width].reshape(token_rows, KEY_VALUE_HEADS, HEAD_SIZE),
            cosine_table,
            sine_table_rows,
            -1.0,
        ).reshape(token_rows, key_value_width)
        grad_projected = jnp.concatenate(
            [grad_queries, grad_keys, key_value_gradient[:, key_value_width:]], axis=1
        ).astype(narrow_type)
        grad_normed = jnp.einsum(
            "tq,dq->td", grad_projected, dense[0], preferred_element_type=wide_type
        )
        grad_hidden_norm, grad_gain_attn = rms_backward(
            layer_state["hidden"], layer_state["inverse_attn"], gain_attn, grad_normed
        )
        incoming = grad_mid + grad_hidden_norm
        small = jnp.concatenate(
            [grad_router, grad_gain_attn[:, None], grad_gain_moe[:, None]], axis=1
        ).astype(narrow_type)
        small = small.reshape(device_count, -1)
        small_size = small.shape[1]
        small_rows = -(-small_size // 2048) * 16
        small = jnp.pad(small, ((0, 0), (0, small_rows * 128 - small_size)))
        small = small.reshape(row_count, col_count, small_rows, 128).transpose(1, 0, 2, 3)
        grad_qkv_block, grad_out_block, small = reduce_dense(
            row_count,
            col_count,
            layer_state["normed"],
            grad_projected,
            grad_attn_b,
            layer_state["attended"],
            small,
        )
        dense_results[layer_index] = (grad_qkv_block, grad_out_block.T)
        small_results[layer_index] = small.reshape(-1)[:small_size].reshape(-1, E + 2)
    small = jnp.stack(small_results)
    grad_router_all = small[:, :, :E]
    grad_norm_attn = small[:, :, E]
    grad_norm_moe = small[:, :, E + 1]
    grad_qkv = jnp.stack([dense_results[index][0] for index in range(layer_count)])
    grad_out = jnp.stack([dense_results[index][1] for index in range(layer_count)])
    grad_gate = jnp.stack([expert_results[index][0] for index in range(layer_count)])
    grad_up = jnp.stack([expert_results[index][1] for index in range(layer_count)])
    grad_down = jnp.stack([expert_results[index][2] for index in range(layer_count)])
    return (
        hidden,
        incoming,
        grad_norm_attn,
        grad_qkv,
        grad_out,
        grad_norm_moe,
        grad_router_all,
        grad_gate,
        grad_up,
        grad_down,
    )


def solution(mesh):
    in_specs = (
        P(("row", "col"), None),
        P(None, ("row", "col"), None),
        P(),
        P(None, "row", "col"),
        P(None, "row", "col"),
        P(),
        P(None, "row", None),
        P(None, "col", None, "row"),
        P(None, "col", None, "row"),
        P(None, "col", "row", None),
        P(("row", "col"), None),
    )
    out_specs = (
        P(("row", "col"), None),
        P(("row", "col"), None),
        P(None, ("row", "col")),
        P(None, "row", "col"),
        P(None, "row", "col"),
        P(None, ("row", "col")),
        P(None, ("row", "col"), None),
        P(None, "col", None, "row"),
        P(None, "col", None, "row"),
        P(None, "col", "row", None),
    )
    return jax.shard_map(body, mesh=mesh, in_specs=in_specs, out_specs=out_specs, check_vma=False)
```

time: 3860 us -> 1770 us (0.46)
  waiting for transfers between devices: 2590 us -> 114 us
  Pallas kernels: 0 us -> 1110 us
  matrix products: 435 us -> 82.9 us
  local copies, waits for them, and re-layouts: 447 us -> 160 us
  other arithmetic: 191 us -> 70.7 us
    reduce_scatter x14 -> x2, waiting for transfers between devices: 1650 us -> 8.11 us  [body(): lax.psum_scatter(grad_kv_full, 'col', scatter_dimension=0, tiled=True)]
    pallas_call x0 -> x11, Pallas kernels: none -> 1110 us  [the longest x2 400 us: moe_backward(): pl.pallas_call(functools.partial(moe_backward_kernel, dims), out_shape=(j...]
    all_gather x10 -> x2, waiting for transfers between devices: 849 us -> 0.01 us  [the longest x1 0.01 us: body(): lax.all_gather(w_qkv[layer_index][None], ('row', 'col'), axis=0, tiled=True)]
    dot_general x52 -> x12, matrix products: 408 us -> 47.9 us  [the longest x2 14.4 us: body(): jnp.einsum('cf,cd->fd', grad_up_b, slot_inputs, preferred_element_type=wi...]
    gather x22 -> x2, local copies, waits for them, and re-layouts: 112 us -> 5.07 us  [body(): grad_pair = jnp.take(grad_pair[:, :, :col_count], places, axis=0)]
    all_gather x2, blocking collectives: 29.6 us -> 133 us  [the longest x1 82.4 us: body(): lax.all_gather(routes, 'row', axis=0, axis_index_groups=token_rows_of)]
    unnamed x330 -> x158, local copies, waits for them, and re-layouts: 100 us -> 14.5 us
    all_gather x4 -> x2, local copies, waits for them, and re-layouts: 62.5 us -> 7.96 us  [fetch_keys(): return lax.all_gather(kv_local, 'col', axis=0, tiled=True)]
  transfers between devices with their start and end apart: 33 -> 18, of which waited for: 25 -> 6; matrix products, arithmetic and copies ran while one was open for 18% -> 16% of each run, Pallas kernels for 0% -> 39%
where the time goes in v1:
time: 1770 us; the launch traced here: 1760 us
  Pallas kernels  1110 us (63%)
  local copies, waits for them, and re-layouts  160 us (9%)
  blocking collectives  133 us (8%)
  waiting for transfers between devices  114 us (6%)
  matrix products  82.9 us (5%)
  starting transfers between devices  75.5 us (4%)
  other arithmetic  70.7 us (4%)
    pallas_call x2, Pallas kernels, moe_backward(): pl.pallas_call(functools.partial(moe_backward_kernel, dims), out_shape=(j...  400 us
    pallas_call x2, Pallas kernels, moe_forward(): pl.pallas_call(functools.partial(moe_forward_kernel, dims), out_shape=(ja...  362 us
    pallas_call x2, Pallas kernels, reduce_dense(): pl.pallas_call(functools.partial(reduce_dense_kernel, (row_count, pair_co...  193 us
    all_to_all x6, waiting for transfers between devices, move_weights(): lax.all_to_all(spread, 'row', split_axis=0, concat_axis=0, tiled=True)  87.3 us
    all_gather x1, blocking collectives, body(): lax.all_gather(routes, 'row', axis=0, axis_index_groups=token_rows_of)  82.4 us
    pallas_call x1, Pallas kernels, gather_dense(): pl.pallas_call(functools.partial(gather_dense_kernel, (row_count, pair_co...  65.5 us
    all_gather x1, blocking collectives, body(): lax.all_gather(w_router.transpose(0, 2, 1), 'row', axis=2, tiled=True)  51 us
    pallas_call x2, Pallas kernels, attend_backward(): pl.pallas_call(functools.partial(attend_backward_kernel, score_scale), ou...  48.9 us
  transfers between devices with their start and end apart: 18, of which 6 were waited for; matrix products, arithmetic and copies ran while one was open for 16% of the time, Pallas kernels for 39%

profile of v1, /device:TPU:30, one launch (start us, length us, event | category | flops | bytes accessed | tf_op | source)
XLA Modules:
  0.0 1761.6 jit_solution(11926415258552258291)
XLA Ops:
  12.5 65.5 %gather_dense.1 = (bf16[1536,2048]{1,0:T(8,128)(2,1)}, bf16[4,1536,384]{2,1,0:T(8,128)(2,1)}) custom-call(bf16[384,256]{1,0:T(8,128)(2,1)} %get-tuple-element.195.qkv_ref, bf16[192,384]{1,0:T(8,128)(2,1)} %get-tuple-element.199.out_ref), custom_call_target="tpu_custom_call" | custom-call | tf_op jit(solution)/shard_map/gather_dense/pallas_call | solution.py:1054
  78.0 4.6 fusion.21
  85.5 4.9 slice_bitcast_fusion.2
  90.4 5.8 all-to-all-start
  96.2 4.9 slice_bitcast_fusion.1
  101.0 51.9 %all-to-all-done = bf16[4,192,1536]{2,1,0:T(8,128)(2,1)} async-done(((bf16[4,192,1536]{2,1,0:T(8,128)(2,1)}), bf16[4,192,1536]{2,1,0:T(8,128)(2,1)}, u32[]{:S(2)}, u32[]{:S(2)}) %all-to-all-start) | async-done | bytes 2359328 | tf_op jit(solution)/shard_map/all_to_all | solution.py:1262
  152.9 6.8 all-to-all-start.1
  160.5 82.4 %all-gather = s32[8,256,4]{1,2,0:T(4,128)S(1)} all-gather(s32[2,256,4]{1,2,0:T(4,128)S(1)} %copy-done.59), channel_id=2, replica_groups=mesh['row'=4,'col'=8] {'row'}, dimensions={0}, use_global_device_ids=true | all-gather | bytes 40960 | tf_op jit(solution)/shard_map/all_gather | solution.py:1278
  243.4 4.9 slice_bitcast_fusion
  248.8 5.9 all-to-all-start.2
  256.0 2.8 eq.117
  258.8 6.0 copy.361
  267.7 6.0 copy.378
  277.0 51.0 %all_gather.24 = bf16[2,32,1536]{2,1,0:T(8,128)(2,1)S(1)} all-gather(bf16[2,32,384]{2,1,0:T(8,128)(2,1)S(1)} %bitcast.342), channel_id=1, replica_groups=mesh['row'=4,'col'=8] {'row'}, dimensions={2}, use_global_device_ids=true | all-gather | bytes 245760 | tf_op jit(solution)/shard_map/all_gather | solution.py:1276
  332.2 6.8 and_convert_fusion
  339.0 6.8 all-to-all-start.3
  349.6 6.6 copy.358
  356.2 4.1 copy.357.kv_ref
  361.7 19.5 %attend_forward.2 = (bf16[256,1536]{1,0:T(8,128)(2,1)}, f32[12,1,256]{2,1,0:T(1,128)}) custom-call(bf16[256,1536]{1,0:T(8,128)(2,1)} %copy.356.q_ref, bf16[2048,512]{1,0:T(8,128)(2,1)} %copy.357.kv_ref, bf16[256,2048]{1,0:T(8,128)(2,1)} %get-tuple-element.171.value_t_ref), custom_call_target="tpu_custom_call" | custom-call | flops 3221225472 | bytes 6291456 | tf_op jit(solution)/shard_map/attend_forward/pallas_call | solution.py:1098
  381.3 4.1 multiply_reduce_fusion.8
  387.0 181.2 %moe_forward.2 = (f32[256,1536]{1,0:T(8,128)}, f32[1024,32]{1,0:T(8,128)}, bf16[1152,1536]{1,0:T(8,128)(2,1)}, bf16[1152,1536]{1,0:T(8,128)(2,1)}) custom-call(bf16[256,1536]{1,0:T(8,128)(2,1)} %multiply_convert_fusion.2.own_ref, bf16[1152,1024]{1,0:T(8,128)(2,1)} %copy.367.place_ref, bf16[1024,1152]{1,0:T(8,128)(2,1)} %bitcast.272, ...), custom_call_target="tpu_custom_call" | custom-call | flops 15401484288 | bytes 41943040 | tf_op jit(solution)/shard_map/moe_forward/pallas_call | solution.py:620
  568.3 5.1 all-to-all-start.4
  576.1 6.4 copy.368
  590.3 35.4 %all-to-all-done.4 = bf16[4,192,1536]{2,1,0:T(8,128)(2,1)} async-done(((bf16[4,192,1536]{2,1,0:T(8,128)(2,1)}), bf16[4,192,1536]{2,1,0:T(8,128)(2,1)}, u32[]{:S(2)}, u32[]{:S(2)}) %all-to-all-start.4) | async-done | bytes 2359328 | tf_op jit(solution)/shard_map/all_to_all | solution.py:1262
  625.7 7.2 all-to-all-start.5
  633.1 4.3 copy.384.place_ref
  640.2 6.0 copy.375
  646.1 3.0 copy.451
  653.8 3.9 copy.374.kv_ref
  657.7 3.1 fusion.50
  660.8 19.6 %attend_forward.3 = (bf16[256,1536]{1,0:T(8,128)(2,1)}, f32[12,1,256]{2,1,0:T(1,128)}) custom-call(bf16[256,1536]{1,0:T(8,128)(2,1)} %copy.373.q_ref, bf16[2048,512]{1,0:T(8,128)(2,1)} %copy.374.kv_ref, bf16[256,2048]{1,0:T(8,128)(2,1)} %get-tuple-element.173.value_t_ref), custom_call_target="tpu_custom_call" | custom-call | flops 3221225472 | bytes 6291456 | tf_op jit(solution)/shard_map/attend_forward/pallas_call | solution.py:1098
  680.4 4.6 multiply_reduce_fusion.6
  686.7 181.1 %moe_forward.3 = (f32[256,1536]{1,0:T(8,128)}, f32[1024,32]{1,0:T(8,128)}, bf16[1152,1536]{1,0:T(8,128)(2,1)}, bf16[1152,1536]{1,0:T(8,128)(2,1)}) custom-call(bf16[256,1536]{1,0:T(8,128)(2,1)} %multiply_convert_fusion.own_ref, bf16[1152,1024]{1,0:T(8,128)(2,1)} %copy.384.place_ref, bf16[1024,1152]{1,0:T(8,128)(2,1)} %bitcast.274, ...), custom_call_target="tpu_custom_call" | custom-call | flops 15401484288 | bytes 41943040 | tf_op jit(solution)/shard_map/moe_forward/pallas_call | solution.py:620
  871.2 181.3 %moe_backward.2 = (f32[256,1536]{1,0:T(8,128)}, f32[4,256,128]{2,1,0:T(8,128)}, bf16[1152,768]{1,0:T(8,128)(2,1)}, bf16[1152,768]{1,0:T(8,128)(2,1)}, bf16[1152,...) custom-call(bf16[256,1536]{1,0:T(8,128)(2,1)} %own_ref, bf16[1152,1024]{1,0:T(8,128)(2,1)} %copy.384.place_ref, ...), custom_call_target="tpu_custom_call" | custom-call | flops 23555211264 | bytes 52428800 | tf_op jit(solution)/shard_map/moe_backward/pallas_call | solution.py:666
  1052.4 7.2 convolution_convert_fusion
  1059.6 5.2 all-to-all-start.11
  1071.7 2.8 multiply_reduce_fusion
  1074.6 3.7 convert_bitcast_fusion.1
  1084.3 24.7 %attend_backward.2 = (bf16[256,1536]{1,0:T(8,128)(2,1)}, bf16[2048,512]{1,0:T(8,128)(2,1)}) custom-call(bf16[256,1536]{1,0:T(8,128)(2,1)} %copy.373.q_ref, bf16[2048,512]{1,0:T(8,128)(2,1)} %copy.374.kv_ref, bf16[256,2048]{1,0:T(8,128)(2,1)} %get-tuple-element.172.key_t_ref, f32[12,1,256]{2,1,0:T(1,128)} %get-tuple-element.61.lse_ref, ...), custom_call_target="tpu_custom_call" | custom-call | flops 8053063680 | bytes 10485760 | tf_op jit(solution)/shard_map/attend_backward/pallas_call | solution.py:1168
  1109.0 7.2 convolution_convert_fusion.2
  1117.2 6.9 all-to-all-start.9
  1136.3 6.0 convolution_convert_fusion.4
  1142.3 8.1 reduce-scatter.3.cloned.1.call-done
  1158.1 6.9 multiply_reduce_fusion.1
  1165.6 10.0 all-to-all-done.9
  1175.6 7.2 all-to-all-start.7
  1182.8 4.3 fusion.47
  1187.0 219.2 %moe_backward.3 = (f32[256,1536]{1,0:T(8,128)}, f32[4,256,128]{2,1,0:T(8,128)}, bf16[1152,768]{1,0:T(8,128)(2,1)}, bf16[1152,768]{1,0:T(8,128)(2,1)}, bf16[1152,...) custom-call(bf16[256,1536]{1,0:T(8,128)(2,1)} %get-tuple-element.157.own_ref, bf16[1152,1024]{1,0:T(8,128)(2,1)} %copy.367.place_ref, ...), custom_call_target="tpu_custom_call" | custom-call | flops 23555211264 | bytes 52428800 | tf_op jit(solution)/shard_map/moe_backward/pallas_call | solution.py:666
  1408.8 7.2 convolution_convert_fusion.1
  1416.0 5.2 all-to-all-start.10
  1427.2 4.6 convert_multiply_fusion.5
  1435.6 24.2 %attend_backward.3 = (bf16[256,1536]{1,0:T(8,128)(2,1)}, bf16[2048,512]{1,0:T(8,128)(2,1)}) custom-call(bf16[256,1536]{1,0:T(8,128)(2,1)} %copy.356.q_ref, bf16[2048,512]{1,0:T(8,128)(2,1)} %copy.357.kv_ref, bf16[256,2048]{1,0:T(8,128)(2,1)} %get-tuple-element.170.key_t_ref, f32[12,1,256]{2,1,0:T(1,128)} %get-tuple-element.69.lse_ref, ...), custom_call_target="tpu_custom_call" | custom-call | flops 8053063680 | bytes 10485760 | tf_op jit(solution)/shard_map/attend_backward/pallas_call | solution.py:1168
  1459.9 7.2 convolution_convert_fusion.3
  1467.1 6.5 all-to-all-done.10
  1473.6 7.2 all-to-all-start.8
  1499.6 95.6 %reduce_dense.3 = (f32[384,256]{1,0:T(8,128)}, f32[192,384]{1,0:T(8,128)}, f32[16,128]{1,0:T(8,128)}) custom-call(bf16[4,384,256]{2,1,0:T(8,128)(2,1)} %bitcast.318, bf16[8,256,256]{2,1,0:T(8,128)(2,1)} %bitcast.308, bf16[8,192,256]{2,1,0:T(8,128)(2,1)} %bitcast.316, bf16[4,256,384]{2,1,0:T(8,128)(2,1)} %bitcast.317, ...), custom_call_target="tpu_custom_call" | custom-call | flops 2818572288 | bytes 8388608 | tf_op jit(solution)/shard_map/reduce_dense/pallas_call | solution.py:899
  1598.7 6.0 convolution_convert_fusion.5
  1611.8 5.9 fusion.8
  1617.8 5.5 all-to-all-start.6
  1626.5 3.4 fusion.20
  1631.8 97.2 %reduce_dense.2 = (f32[384,256]{1,0:T(8,128)}, f32[192,384]{1,0:T(8,128)}, f32[16,128]{1,0:T(8,128)}) custom-call(bf16[4,384,256]{2,1,0:T(8,128)(2,1)} %bitcast.319, bf16[8,256,256]{2,1,0:T(8,128)(2,1)} %bitcast.309, bf16[8,192,256]{2,1,0:T(8,128)(2,1)} %bitcast.315, bf16[4,256,384]{2,1,0:T(8,128)(2,1)} %bitcast.314, ...), custom_call_target="tpu_custom_call" | custom-call | flops 2818572288 | bytes 8388608 | tf_op jit(solution)/shard_map/reduce_dense/pallas_call | solution.py:899
  1734.1 6.7 maximum_convert_fusion.2
  1740.8 6.7 maximum_convert_fusion.1
  1747.6 6.7 maximum_convert_fusion
  (347 shorter events, 136.8 us)
Async XLA Ops:
  7.2 4.5 copy-start.18
  7.2 349.0 %all-gather.6.cloned.1.call-start = ((), (), s32[]{:S(2)}) async-start(), calls=%async_computation.14 | async-start | bytes 2359296 | tf_op jit(solution)/shard_map/all_gather | solution.py:73
  11.6 71.0 %copy-start.47 = (f32[1536]{0:T(1024)}, f32[1536]{0:T(1024)S(1)}, u32[]{:S(2)}) copy-start(f32[1536]{0:T(1024)S(1)} %get-tuple-element.149) | copy-start | bytes 18436
  12.5 70.2 %copy-start.61 = (f32[256]{0:T(256)}, f32[256]{0:T(256)S(1)}, u32[]{:S(2)}) copy-start(f32[256]{0:T(256)S(1)} %get-tuple-element.208) | copy-start | bytes 3076
  82.6 77.8 %copy-start.5 = (f32[256,2048]{1,0:T(8,128)}, f32[256,2048]{1,0:T(8,128)S(1)}, u32[]{:S(2)}) copy-start(f32[256,2048]{1,0:T(8,128)S(1)} %fusion.21) | copy-start | bytes 6291460
  84.8 491.3 %all-gather.8.cloned.1.call-start = ((), (), s32[]{:S(2)}) async-start(), calls=%async_computation.15 | async-start | bytes 6488064 | tf_op jit(solution)/shard_map/all_gather | solution.py:1292
  90.4 62.5 %all-to-all-start = ((bf16[4,192,1536]{2,1,0:T(8,128)(2,1)}), bf16[4,192,1536]{2,1,0:T(8,128)(2,1)}, u32[]{:S(2)}, u32[]{:S(2)}) async-start(bf16[4,192,1536]{2,1,0:T(8,128)(2,1)} %get-tuple-element.169), calls=%async_computation | async-start | bytes 4718592 | tf_op jit(solution)/shard_map/all_to_all | solution.py:1262
  152.9 95.9 %all-to-all-start.1 = ((bf16[4,192,1536]{2,1,0:T(8,128)(2,1)}), bf16[4,192,1536]{2,1,0:T(8,128)(2,1)}, u32[]{:S(2)}, u32[]{:S(2)}) async-start(bf16[4,192,1536]{2,1,0:T(8,128)(2,1)} %get-tuple-element.167), calls=%async_computation.1 | async-start | bytes 4718592 | tf_op jit(solution)/shard_map/all_to_all | solution.py:1262
  159.7 480.5 %all-gather.12.cloned.1.call-start = ((), (), s32[]{:S(2)}) async-start(), calls=%async_computation.17 | async-start | bytes 4866048 | tf_op jit(solution)/shard_map/all_gather | solution.py:1297
  248.8 90.2 %all-to-all-start.2 = ((bf16[4,192,1536]{2,1,0:T(8,128)(2,1)}), bf16[4,192,1536]{2,1,0:T(8,128)(2,1)}, u32[]{:S(2)}, u32[]{:S(2)}) async-start(bf16[4,192,1536]{2,1,0:T(8,128)(2,1)} %get-tuple-element.165), calls=%async_computation.2 | async-start | bytes 4718592 | tf_op jit(solution)/shard_map/all_to_all | solution.py:1262
  274.4 55.0 %slice-start.2 = ((f32[256,2048]{1,0:T(8,128)}), f32[256,1536]{1,0:T(8,128)S(1)}, s32[]{:S(2)}) async-start(f32[256,2048]{1,0:T(8,128)} %copy-done.5), calls=%async_computation.22 | async-start | bytes 3145728 | tf_op jit(solution)/shard_map/slice | solution.py:1309
  339.0 6.9 copy-start.2
  339.0 6.9 copy-start.49
  339.0 229.3 %all-to-all-start.3 = ((bf16[4,192,1536]{2,1,0:T(8,128)(2,1)}), bf16[4,192,1536]{2,1,0:T(8,128)(2,1)}, u32[]{:S(2)}, u32[]{:S(2)}) async-start(bf16[4,192,1536]{2,1,0:T(8,128)(2,1)} %get-tuple-element.168), calls=%async_computation.3 | async-start | bytes 4718592 | tf_op jit(solution)/shard_map/all_to_all | solution.py:1262
  345.9 40.0 %copy-start.44 = (f32[1536]{0:T(1024)}, f32[1536]{0:T(1024)S(1)}, u32[]{:S(2)}) copy-start(f32[1536]{0:T(1024)S(1)} %get-tuple-element.147) | copy-start | bytes 18436
  356.2 4.1 copy-start.3
  361.7 19.5 %copy-start.19 = (bf16[256,1536]{1,0:T(8,128)(2,1)S(1)}, bf16[256,1536]{1,0:T(8,128)(2,1)}, u32[]{:S(2)}) copy-start(bf16[256,1536]{1,0:T(8,128)(2,1)} %param.19) | copy-start | bytes 2359300
  385.9 182.3 %copy-start.50 = (f32[256]{0:T(256)}, f32[256]{0:T(256)S(1)}, u32[]{:S(2)}) copy-start(f32[256]{0:T(256)S(1)} %get-tuple-element.210) | copy-start | bytes 3076
  568.3 57.4 %all-to-all-start.4 = ((bf16[4,192,1536]{2,1,0:T(8,128)(2,1)}), bf16[4,192,1536]{2,1,0:T(8,128)(2,1)}, u32[]{:S(2)}, u32[]{:S(2)}) async-start(bf16[4,192,1536]{2,1,0:T(8,128)(2,1)} %get-tuple-element.166), calls=%async_computation.4 | async-start | bytes 4718592 | tf_op jit(solution)/shard_map/all_to_all | solution.py:1262
  573.4 80.4 %all-gather.10.cloned.1.call-start = ((), (), s32[]{:S(2)}) async-start(), calls=%async_computation.16 | async-start | bytes 2359296 | tf_op jit(solution)/shard_map/all_gather | solution.py:73
  575.4 9.8 copy-start.6
  576.1 9.2 copy-start.67
  625.7 7.2 copy-start.33
  625.7 60.9 %all-to-all-start.5 = ((bf16[4,192,1536]{2,1,0:T(8,128)(2,1)}), bf16[4,192,1536]{2,1,0:T(8,128)(2,1)}, u32[]{:S(2)}, u32[]{:S(2)}) async-start(bf16[4,192,1536]{2,1,0:T(8,128)(2,1)} %get-tuple-element.164), calls=%async_computation.5 | async-start | bytes 4718592 | tf_op jit(solution)/shard_map/all_to_all | solution.py:1262
  633.1 4.3 copy-start.40
  685.6 182.2 %copy-start.52 = (f32[256]{0:T(256)}, f32[256]{0:T(256)S(1)}, u32[]{:S(2)}) copy-start(f32[256]{0:T(256)S(1)} %get-tuple-element.214) | copy-start | bytes 3076
  1059.6 7.8 copy-start.69
  1059.6 57.6 %all-to-all-start.11 = ((bf16[4,192,1536]{2,1,0:T(8,128)(2,1)}), bf16[4,192,1536]{2,1,0:T(8,128)(2,1)}, u32[]{:S(2)}, u32[]{:S(2)}) async-start(bf16[4,192,1536]{2,1,0:T(8,128)(2,1)} %bitcast.303), calls=%async_computation.13 | async-start | bytes 4718592 | tf_op jit(solution)/shard_map/all_to_all | solution.py:1268
  1064.9 85.6 %reduce-scatter.3.cloned.1.call-start = ((), (), s32[]{:S(2)}) async-start(), calls=%async_computation.18 | async-start | bytes 2359296 | tf_op jit(solution)/shard_map/reduce_scatter | solution.py:1459
  1067.4 4.3 copy-start.53
  1071.7 6.6 slice-start
  1074.6 3.7 copy-start.22
  1117.2 58.4 %all-to-all-start.9 = ((bf16[4,192,1536]{2,1,0:T(8,128)(2,1)}), bf16[4,192,1536]{2,1,0:T(8,128)(2,1)}, u32[]{:S(2)}, u32[]{:S(2)}) async-start(bf16[4,192,1536]{2,1,0:T(8,128)(2,1)} %bitcast.305), calls=%async_computation.11 | async-start | bytes 4718592 | tf_op jit(solution)/shard_map/all_to_all | solution.py:1268
  1124.1 6.7 copy-start.17
  1126.4 4.6 copy-start.15
  1142.3 15.8 copy-start.7
  1142.3 15.8 copy-start.68
  1158.1 6.9 copy-start.35
  1175.6 7.2 copy-start.1
  1175.6 7.2 copy-start.66
  1175.6 240.3 %all-to-all-start.7 = ((bf16[4,192,1536]{2,1,0:T(8,128)(2,1)}), bf16[4,192,1536]{2,1,0:T(8,128)(2,1)}, u32[]{:S(2)}, u32[]{:S(2)}) async-start(bf16[4,192,1536]{2,1,0:T(8,128)(2,1)} %bitcast.304), calls=%async_computation.9 | async-start | bytes 4718592 | tf_op jit(solution)/shard_map/all_to_all | solution.py:1268
  1416.0 5.5 copy-start.27
  1416.0 5.5 copy-start.70
  1416.0 57.6 %all-to-all-start.10 = ((bf16[4,192,1536]{2,1,0:T(8,128)(2,1)}), bf16[4,192,1536]{2,1,0:T(8,128)(2,1)}, u32[]{:S(2)}, u32[]{:S(2)}) async-start(bf16[4,192,1536]{2,1,0:T(8,128)(2,1)} %bitcast.302), calls=%async_computation.12 | async-start | bytes 4718592 | tf_op jit(solution)/shard_map/all_to_all | solution.py:1268
  1421.2 183.5 %reduce-scatter.5.cloned.1.call-start = ((), (), s32[]{:S(2)}) async-start(), calls=%async_computation.19 | async-start | bytes 2359296 | tf_op jit(solution)/shard_map/reduce_scatter | solution.py:1459
  1473.6 7.2 copy-start.26
  1473.6 7.2 copy-start.56
  1473.6 8.1 copy-start.23
  1473.6 144.2 %all-to-all-start.8 = ((bf16[4,192,1536]{2,1,0:T(8,128)(2,1)}), bf16[4,192,1536]{2,1,0:T(8,128)(2,1)}, u32[]{:S(2)}, u32[]{:S(2)}) async-start(bf16[4,192,1536]{2,1,0:T(8,128)(2,1)} %bitcast.300), calls=%async_computation.10 | async-start | bytes 4718592 | tf_op jit(solution)/shard_map/all_to_all | solution.py:1268
  1482.9 4.8 copy-start.13
  1482.9 5.0 copy-start.11
  1482.9 5.1 copy-start.65
  1482.9 5.2 copy-start.38
  1485.3 4.1 copy-start.34
  1485.3 4.1 copy-start.36
  1597.2 14.6 copy-start.24
  1604.7 7.1 copy-start.20
  1604.7 7.1 copy-start.48
  1604.7 7.1 copy-start.62
  1617.8 5.6 copy-start.37
  1617.8 129.8 %all-to-all-start.6 = ((bf16[4,192,1536]{2,1,0:T(8,128)(2,1)}), bf16[4,192,1536]{2,1,0:T(8,128)(2,1)}, u32[]{:S(2)}, u32[]{:S(2)}) async-start(bf16[4,192,1536]{2,1,0:T(8,128)(2,1)} %bitcast.301), calls=%async_computation.8 | async-start | bytes 4718592 | tf_op jit(solution)/shard_map/all_to_all | solution.py:1268
  1631.8 99.5 %copy-start.43 = (f32[192,384]{1,0:T(8,128)S(1)}, f32[192,384]{1,0:T(8,128)}, u32[]{:S(2)}) copy-start(f32[192,384]{1,0:T(8,128)} %get-tuple-element.77) | copy-start | bytes 884740
  1729.0 4.2 copy-start.41
  1729.0 4.2 copy-start.42
  (30 other events, 62.3 us)
Sparse Core Ops, SparseCore 0:
  84.9 28.2 all-gather.5
  116.1 118.0 all-gather.7
  237.1 91.9 all-gather.11
  590.4 28.1 all-gather.9
  1109.2 41.2 reduce-scatter.2
  1460.0 41.2 reduce-scatter.4

commit v2 on v1

v2 whole, which is shorter than its diff:
```python
import functools

import jax
import jax.numpy as jnp
from jax import lax
from jax.experimental import pallas as pl
from jax.experimental.pallas import tpu as pltpu
from jax.sharding import PartitionSpec as P

QUERY_HEADS = 12
KEY_VALUE_HEADS = 2
HEAD_SIZE = 128
E = 32
TOPK = 4
BLOCK = 256
QUERY_FEATURES = 1536
CAP = 36


eps_norm = 1e-06
rope_base = 1000000.0
masked_score = -1e30
wide_type = jnp.float32
narrow_type = jnp.bfloat16


def rope_angles(positions, half_dim):
    frequency = rope_base ** (-jnp.arange(half_dim, dtype=jnp.float32) / half_dim)
    angles = positions.astype(jnp.float32)[:, None] * frequency[None, :]
    return (jnp.cos(angles), jnp.sin(angles))


def split_rows(total, most):
    best = 16
    for step in range(16, most + 1, 16):
        if total % step == 0:
            best = step
    return best


def over_blocks(total, block, step):
    def run(index, carry):
        step(pl.ds(pl.multiple_of(index * block, block), block))
        return carry

    lax.fori_loop(0, total // block, run, 0)


def over_chunks(chunks, width, step):
    def run(index, carry):
        step(index, pl.ds(pl.multiple_of(index * width, width), width))
        return carry

    lax.fori_loop(0, chunks, run, 0)


def dot_nt(left, right):
    return lax.dot_general(
        left, right, (((1,), (1,)), ((), ())), preferred_element_type=jnp.float32
    )


def dot_nn(left, right):
    return jnp.dot(left, right, preferred_element_type=jnp.float32)


class Peers:
    def __init__(self, count, place, device_of):
        self.count = count
        self.place = place
        self.device_of = device_of

    def ahead(self, step):
        return lax.rem(self.place + step, self.count)

    def behind(self, step):
        return lax.rem(self.place + self.count - step, self.count)


def expert_peers(col_count, copies, group_rows):
    row_index = lax.axis_index("row")
    share = lax.rem(row_index, copies)
    rows = Peers(group_rows, row_index // copies, lambda place: {"row": share + copies * place})
    return rows, col_peers(col_count)


def col_peers(col_count):
    return Peers(col_count, lax.axis_index("col"), lambda place: {"col": place})


def greet(groups):
    barrier = pltpu.get_barrier_semaphore()
    total = 0
    for peers in groups:
        for step in range(1, peers.count):
            pl.semaphore_signal(
                barrier,
                inc=1,
                device_id=peers.device_of(peers.ahead(step)),
                device_id_type=pl.DeviceIdType.MESH,
            )
            total += 1
    pl.semaphore_wait(barrier, total)


def send_to(source, target, sems, number, device):
    send_sems, recv_sems = sems
    return pltpu.make_async_remote_copy(
        src_ref=source,
        dst_ref=target,
        send_sem=send_sems.at[number],
        recv_sem=recv_sems.at[number],
        device_id=device,
        device_id_type=pl.DeviceIdType.MESH,
    )


class Exchange:
    def __init__(self, peers, send_sems, recv_sems, source, target):
        self.peers = peers
        self.sems = (send_sems, recv_sems)
        self.source = source
        self.target = target

    def out(self, step, index, chunk):
        place = self.peers.ahead(step)
        return send_to(
            self.source(place, chunk),
            self.target(self.peers.place, step, chunk),
            self.sems,
            (index, step - 1),
            self.peers.device_of(place),
        )

    def start(self, index, chunk):
        for step in range(1, self.peers.count):
            self.out(step, index, chunk).start()

    def wait_send(self, index, chunk):
        for step in range(1, self.peers.count):
            self.out(step, index, chunk).wait_send()

    def wait_recv(self, index, chunk):
        for step in range(1, self.peers.count):
            place = self.peers.behind(step)
            landed = self.target(place, step, chunk)
            send_to(
                landed, landed, self.sems, (index, step - 1), self.peers.device_of(place)
            ).wait_recv()


def exchange_sems(chunks, count):
    return [pltpu.SemaphoreType.DMA((chunks, max(count - 1, 1))) for _ in range(2)]


def iota(shape, axis):
    return lax.broadcasted_iota(jnp.int32, shape, axis)


def within(numbers, size, count):
    block = jnp.zeros_like(numbers)
    for index in range(1, count):
        block = block + (numbers >= index * size).astype(jnp.int32)
    return block, numbers - block * size


def slot_block(shape, slot_axis, slot_rows):
    slots = iota(shape, slot_axis)
    block = iota(shape, 1 - slot_axis)
    return (slots >= block * slot_rows) & (slots < (block + 1) * slot_rows)


def build_places(dims, rows, routes_ref, place, place_t, member):
    group_rows, col_count, copies, token_rows, slot_rows, chunks, width = dims
    all_slots = col_count * slot_rows
    number = iota((E, 1), 0)
    ahead, col = within(number, col_count, group_rows)
    owner = ahead + rows.place
    owner = jnp.where(owner >= group_rows, owner - group_rows, owner)
    expert = col * group_rows + owner
    earlier = (iota((token_rows, token_rows), 0) < iota((token_rows, token_rows), 1)).astype(
        jnp.bfloat16
    )
    pick = slot_block((E, all_slots), 1, slot_rows).astype(jnp.bfloat16)
    column = iota((slot_rows, 1), 0)
    lane = within(iota((1, all_slots), 1), slot_rows, col_count)[1]
    for group in range(group_rows):
        tokens = slice(group * token_rows, (group + 1) * token_rows)
        picked = routes_ref[group]
        has = picked[0:1, :] == expert
        for choice in range(1, TOPK):
            has = has | (picked[choice : choice + 1, :] == expert)
        before = dot_nn(has.astype(jnp.float32).astype(jnp.bfloat16), earlier)
        slot_number = jnp.where(has, before, -1.0)
        in_group = (column >= group * CAP) & (column < (group + 1) * CAP)
        wanted = jnp.where(in_group, column - group * CAP, -2).astype(jnp.float32)
        for index in range(col_count):
            slots = slice(index * slot_rows, (index + 1) * slot_rows)
            hit = slot_number[index : index + 1, :] == wanted
            place[slots, tokens] = jnp.where(hit, 1.0, 0.0).astype(jnp.bfloat16)
        turned = slot_number.T
        in_group = (lane >= group * CAP) & (lane < (group + 1) * CAP)
        wanted = jnp.where(in_group, lane - group * CAP, -2).astype(jnp.float32)
        hit = dot_nn(turned.astype(jnp.bfloat16), pick) == wanted
        place_t[tokens, :] = jnp.where(hit, 1.0, 0.0).astype(jnp.bfloat16)
        if member is not None:
            member[tokens, :] = turned


class WeightMove:
    def __init__(self, rows, copies, layer, shards, target, sems):
        self.rows = rows
        self.copies = copies
        self.layer = layer
        self.shards = shards
        self.target = target
        self.remote_sems = sems[:2]
        self.local_sem = sems[2]

    @staticmethod
    def sems(row_count):
        return [pltpu.SemaphoreType.DMA((max(row_count - 1, 1),))] * 2 + [pltpu.SemaphoreType.DMA]

    def shard(self, place):
        return self.shards.at[self.layer, place // self.copies]

    def own(self):
        return pltpu.make_async_copy(
            self.shard(self.rows.place), self.target.at[0], self.local_sem
        )

    def out(self, step):
        place = self.rows.ahead(step)
        return send_to(
            self.shard(place),
            self.target.at[step],
            self.remote_sems,
            step - 1,
            self.rows.device_of(place),
        )

    def start(self):
        for step in range(1, self.rows.count):
            self.out(step).start()
        self.own().start()

    def wait_recv(self):
        self.own().wait()
        for step in range(1, self.rows.count):
            landed = self.target.at[step]
            place = self.rows.behind(step)
            send_to(
                landed, landed, self.remote_sems, step - 1, self.rows.device_of(place)
            ).wait_recv()

    def wait_send(self):
        for step in range(1, self.rows.count):
            self.out(step).wait_send()


def all_rows(row_count):
    return Peers(row_count, lax.axis_index("row"), lambda place: {"row": place})


def moved_shape(row_count, shards):
    return jax.ShapeDtypeStruct((row_count, *shards.shape[2:]), shards.dtype)


vmem_most = 62 * 1024 * 1024
long_cost = pl.CostEstimate(flops=0, bytes_accessed=600 * 1024 * 1024, transcendentals=0)
no_cost = pl.CostEstimate(flops=0, bytes_accessed=0, transcendentals=0)


def moe_forward_kernel(dims, row_count, layer, moving, gather_dims, *refs):
    group_rows, col_count, copies, token_rows, slot_rows, chunks, width = dims
    own_ref, routes_ref, router_ref = refs[:3]
    weight_in = refs[3:6]
    refs = refs[6:]
    next_blocks = refs[: 2 if gather_dims else 0]
    refs = refs[len(next_blocks) :]
    sum_ref, gates_ref, slots_out, returned_out = refs[:4]
    refs = refs[4:]
    moved_out = refs[: len(moving)]
    refs = refs[len(moving) :]
    next_full = refs[: len(next_blocks)]
    refs = refs[len(next_blocks) :]
    dense = None
    if gather_dims:
        count = len(DenseGather.sems(gather_dims, 2))
        dense = DenseGather(gather_dims, next_blocks, next_full, refs[-count:])
        refs = refs[:-count]
    move_sems = refs[len(refs) - 3 * len(moving) :]
    refs = refs[: len(refs) - 3 * len(moving)]
    (
        place,
        place_t,
        member,
        gate,
        up,
        down,
        tokens,
        send,
        slots,
        gate_val,
        up_val,
        act,
        returned,
        landed,
        row_send,
        row_recv,
        there_send,
        there_recv,
        back_send,
        back_recv,
        home_send,
        home_recv,
        local_sem,
    ) = refs
    all_tokens = group_rows * token_rows
    all_slots = col_count * slot_rows
    slot_step = split_rows(all_slots, 320)
    rows, cols = expert_peers(col_count, copies, group_rows)

    def token_part(place):
        return pl.ds(pl.multiple_of(place * token_rows, token_rows), token_rows)

    def slot_part(place):
        return pl.ds(pl.multiple_of(place * slot_rows, slot_rows), slot_rows)

    gather = Exchange(
        rows,
        row_send,
        row_recv,
        lambda place, chunk: own_ref.at[:, chunk],
        lambda place, step, chunk: tokens.at[token_part(place), chunk],
    )
    there = Exchange(
        cols,
        there_send,
        there_recv,
        lambda place, chunk: send.at[slot_part(place), chunk],
        lambda place, step, chunk: slots.at[slot_part(place), chunk],
    )
    back = Exchange(
        cols,
        back_send,
        back_recv,
        lambda place, chunk: send.at[slot_part(place), chunk],
        lambda place, step, chunk: returned.at[slot_part(place), chunk],
    )
    home = Exchange(
        rows,
        home_send,
        home_recv,
        lambda place, chunk: tokens.at[token_part(place), chunk],
        lambda place, step, chunk: landed.at[step - 1, :, chunk],
    )
    weights = (gate, up, down)
    moves = {
        kind: WeightMove(
            all_rows(row_count),
            copies,
            layer,
            weight_in[kind],
            weights[kind],
            move_sems[3 * number : 3 * number + 3],
        )
        for number, kind in enumerate(moving)
    }
    loads = {
        kind: pltpu.make_async_copy(weight_in[kind], weights[kind], local_sem.at[2 + kind])
        for kind in range(3)
        if kind not in moving
    }
    keeps = []

    def weight_ready(kind):
        if kind in loads:
            loads[kind].wait()
        else:
            moves[kind].wait_recv()
            keep = pltpu.make_async_copy(
                weights[kind], moved_out[moving.index(kind)], local_sem.at[2 + kind]
            )
            keep.start()
            keeps.append(keep)

    def weight(kind, chunk):
        return weights[kind][:, :, chunk].reshape(-1, width)

    greet((all_rows(row_count), cols))
    over_chunks(chunks, width, gather.start)
    for kind in moving:
        moves[kind].start()
    if dense:
        for kind in dense.kinds:
            dense.start(kind)
    for copy in loads.values():
        copy.start()
    tokens[token_part(rows.place), :] = own_ref[...]
    build_places(dims, rows, routes_ref, place, place_t, member)

    def dispatch(index, chunk):
        gather.wait_recv(index, chunk)

        def rows_of(part):
            send[part, chunk] = dot_nn(place[part, :], tokens[:, chunk]).astype(jnp.bfloat16)

        over_blocks(all_slots, slot_step, rows_of)
        there.start(index, chunk)
        slots[slot_part(cols.place), chunk] = send[slot_part(cols.place), chunk]

    over_chunks(chunks, width, dispatch)

    def gating(part):
        chosen = member[part, :] >= 0
        logits = jnp.where(chosen, dot_nt(tokens[part, :], router_ref[...]), masked_score)
        peak = jnp.max(logits, axis=-1, keepdims=True)
        exponent = jnp.where(chosen, jnp.exp(logits - peak), 0.0)
        gates = exponent / jnp.sum(exponent, axis=-1, keepdims=True)
        gates_ref[part, :] = gates
        pick = slot_block((E, all_slots), 1, slot_rows).astype(jnp.bfloat16)
        spread = dot_nn(gates.astype(jnp.bfloat16), pick)
        place_t[part, :] = (place_t[part, :].astype(jnp.float32) * spread).astype(jnp.bfloat16)

    over_blocks(all_tokens, token_rows, gating)

    def project(kind, target, wait, index, chunk):
        if wait:
            there.wait_recv(index, chunk)

        def rows_of(part):
            value = dot_nt(slots[part, chunk], weight(kind, chunk))

            @pl.when(index == 0)
            def _():
                target[part, :] = value

            @pl.when(index > 0)
            def _():
                target[part, :] += value

        over_blocks(all_slots, slot_step, rows_of)

    weight_ready(0)
    over_chunks(chunks, width, functools.partial(project, 0, gate_val, True))
    weight_ready(1)
    over_chunks(chunks, width, functools.partial(project, 1, up_val, False))
    keep_slots = pltpu.make_async_copy(slots, slots_out, local_sem.at[0])
    keep_slots.start()

    def activate(part):
        value = gate_val[part, :]
        act[part, :] = (value * jax.nn.sigmoid(value) * up_val[part, :]).astype(jnp.bfloat16)

    over_blocks(all_slots, slot_step, activate)
    weight_ready(2)

    def give_back(index, chunk):
        there.wait_send(index, chunk)

        def rows_of(part):
            send[part, chunk] = dot_nn(act[part, :], weight(2, chunk)).astype(jnp.bfloat16)

        over_blocks(all_slots, slot_step, rows_of)
        back.start(index, chunk)
        returned[slot_part(cols.place), chunk] = send[slot_part(cols.place), chunk]

    over_chunks(chunks, width, give_back)

    def combine(index, chunk):
        back.wait_recv(index, chunk)

        def rows_of(part):
            tokens[part, chunk] = dot_nn(place_t[part, :], returned[:, chunk]).astype(jnp.bfloat16)

        over_blocks(all_tokens, token_rows, rows_of)
        home.start(index, chunk)

    over_chunks(chunks, width, combine)
    keep_returned = pltpu.make_async_copy(returned, returned_out, local_sem.at[1])
    keep_returned.start()
    if dense:
        for kind in dense.kinds:
            dense.pass_rows(kind)

    def finish(index, chunk):
        home.wait_recv(index, chunk)
        total = tokens[token_part(rows.place), chunk].astype(jnp.float32)
        for step in range(1, group_rows):
            total = total + landed[step - 1, :, chunk].astype(jnp.float32)
        sum_ref[:, chunk] = total

    over_chunks(chunks, width, finish)

    def drain(index, chunk):
        gather.wait_send(index, chunk)
        back.wait_send(index, chunk)
        home.wait_send(index, chunk)

    over_chunks(chunks, width, drain)
    if dense:
        for kind in dense.kinds:
            dense.pass_pairs(kind)
        for kind in dense.kinds:
            dense.finish(kind)
    for kind in moving:
        moves[kind].wait_send()
    keep_slots.wait()
    keep_returned.wait()
    for keep in keeps:
        keep.wait()


def moe_backward_kernel(dims, *refs):
    group_rows, col_count, copies, token_rows, slot_rows, chunks, width = dims
    own_ref, routes_ref, router_ref, gates_ref, normed_ref, slots_in, returned_in = refs[:7]
    weight_in = refs[7:10]
    sum_ref, router_grad_ref, grads_out = refs[10:13]
    (
        place,
        place_t,
        gate,
        up,
        down,
        tokens,
        send,
        slots,
        slope,
        silu,
        act,
        weight,
        inner,
        received,
        grad_act,
        grad_gate,
        grad_up,
        returned,
        turned,
        staged,
        landed,
        pair_send,
        pair_landed,
        row_send,
        row_recv,
        there_send,
        there_recv,
        back_send,
        back_recv,
        home_send,
        home_recv,
        pair_send_sem,
        pair_recv_sem,
        local_sem,
    ) = refs[13:]
    all_tokens = group_rows * token_rows
    all_slots = col_count * slot_rows
    slot_step = split_rows(all_slots, 320)
    block_count, slice_width = weight_in[0].shape[:2]
    rows, cols = expert_peers(col_count, copies, group_rows)

    def token_part(place):
        return pl.ds(pl.multiple_of(place * token_rows, token_rows), token_rows)

    def slot_part(place):
        return pl.ds(pl.multiple_of(place * slot_rows, slot_rows), slot_rows)

    gather = Exchange(
        rows,
        row_send,
        row_recv,
        lambda place, chunk: own_ref.at[:, chunk],
        lambda place, step, chunk: tokens.at[token_part(place), chunk],
    )
    there = Exchange(
        cols,
        there_send,
        there_recv,
        lambda place, chunk: send.at[slot_part(place), chunk],
        lambda place, step, chunk: received.at[slot_part(place), chunk],
    )
    back = Exchange(
        cols,
        back_send,
        back_recv,
        lambda place, chunk: send.at[slot_part(place), chunk],
        lambda place, step, chunk: returned.at[slot_part(place), chunk],
    )
    home = Exchange(
        rows,
        home_send,
        home_recv,
        lambda place, chunk: tokens.at[token_part(place), chunk],
        lambda place, step, chunk: landed.at[step - 1, :, chunk],
    )
    pair = Exchange(
        rows,
        pair_send_sem,
        pair_recv_sem,
        lambda place, chunk: pair_send.at[token_part(place), :],
        lambda place, step, chunk: pair_landed.at[step - 1],
    )
    greet((rows, cols))
    over_chunks(chunks, width, gather.start)
    load_slots = pltpu.make_async_copy(slots_in, slots, local_sem.at[0])
    load_slots.start()
    weights = (gate, up, down)
    loads = [
        pltpu.make_async_copy(weight_in[kind], weights[kind], local_sem.at[4 + kind])
        for kind in range(3)
    ]
    for copy in loads:
        copy.start()

    def weight_part(kind, chunk):
        return weights[kind][:, :, chunk].reshape(block_count * slice_width, width)

    load_returned = pltpu.make_async_copy(returned_in, returned, local_sem.at[1])
    load_returned.start()
    tokens[token_part(rows.place), :] = own_ref[...]
    build_places(dims, rows, routes_ref, place, place_t, None)
    load_slots.wait()
    for copy in loads:
        copy.wait()

    def recompute(part):
        gate_val = dot_nt(slots[part, :], gate[...].reshape(-1, gate.shape[2]))
        up_val = dot_nt(slots[part, :], up[...].reshape(-1, up.shape[2]))
        sigmoid = jax.nn.sigmoid(gate_val)
        value = gate_val * sigmoid
        act[part, :] = (value * up_val).astype(jnp.bfloat16)
        silu[part, :] = value.astype(jnp.bfloat16)
        slope[part, :] = (up_val * sigmoid * (1.0 + gate_val * (1.0 - sigmoid))).astype(
            jnp.bfloat16
        )
        picked = dot_nn(place[part, :], gates_ref[...].astype(jnp.bfloat16))
        block = iota(picked.shape, 1)
        slot = iota(picked.shape, 0) + part.start
        in_block = (slot >= block * slot_rows) & (slot < (block + 1) * slot_rows)
        weight[part, :] = jnp.sum(jnp.where(in_block, picked, 0.0), axis=1, keepdims=True)

    over_blocks(all_slots, slot_step, recompute)
    load_returned.wait()

    def dispatch(index, chunk):
        gather.wait_recv(index, chunk)

        def rows_of(part):
            grad = dot_nn(place[part, :], tokens[:, chunk])
            share = jnp.sum(
                grad * returned[part, chunk].astype(jnp.float32), axis=1, keepdims=True
            )
            send[part, chunk] = (weight[part, :] * grad).astype(jnp.bfloat16)

            @pl.when(index == 0)
            def _():
                inner[part, :] = share

            @pl.when(index > 0)
            def _():
                inner[part, :] += share

        over_blocks(all_slots, slot_step, rows_of)
        there.start(index, chunk)
        received[slot_part(cols.place), chunk] = send[slot_part(cols.place), chunk]

    over_chunks(chunks, width, dispatch)

    def pairs(part):
        picked = slot_block((all_slots, pair_send.shape[1]), 0, slot_rows)
        spread = jnp.where(picked, inner[...], 0.0)
        high = spread.astype(jnp.bfloat16)
        low = (spread - high.astype(jnp.float32)).astype(jnp.bfloat16)
        pair_send[part, :] = dot_nn(place_t[part, :], high) + dot_nn(place_t[part, :], low)

    over_blocks(all_tokens, token_rows, pairs)
    pair.start(0, None)

    def project(index, chunk):
        there.wait_recv(index, chunk)

        def rows_of(part):
            grad = dot_nt(received[part, chunk], weight_part(2, chunk))

            @pl.when(index == 0)
            def _():
                grad_act[part, :] = grad

            @pl.when(index > 0)
            def _():
                grad_act[part, :] += grad

        over_blocks(all_slots, slot_step, rows_of)

    over_chunks(chunks, width, project)

    def slopes(part):
        grad = grad_act[part, :]
        grad_gate[part, :] = (grad * slope[part, :].astype(jnp.float32)).astype(jnp.bfloat16)
        grad_up[part, :] = (grad * silu[part, :].astype(jnp.float32)).astype(jnp.bfloat16)

    over_blocks(all_slots, slot_step, slopes)

    def give_back(index, chunk):
        there.wait_send(index, chunk)

        def rows_of(part):
            send[part, chunk] = (
                dot_nn(grad_gate[part, :], weight_part(0, chunk))
                + dot_nn(grad_up[part, :], weight_part(1, chunk))
            ).astype(jnp.bfloat16)

        over_blocks(all_slots, slot_step, rows_of)
        back.start(index, chunk)

    over_chunks(chunks, width, give_back)

    def keep(kind, index):
        return pltpu.make_async_copy(
            staged.at[lax.rem(index, 2)],
            grads_out.at[index, kind],
            local_sem.at[2 + lax.rem(index, 2)],
        )

    for kind, (left, right) in enumerate(
        ((grad_gate, slots), (grad_up, slots), (act, received))
    ):
        turned[...] = left[...].T

        def one_slice(index, carry, kind=kind, right=right):
            @pl.when(index >= 2)
            def _():
                keep(kind, index - 2).wait()

            part = pl.ds(pl.multiple_of(index * slice_width, slice_width), slice_width)
            staged[lax.rem(index, 2)] = dot_nn(turned[part, :], right[...]).astype(jnp.bfloat16)
            keep(kind, index).start()
            return carry

        lax.fori_loop(0, block_count, one_slice, 0)
        for index in range(max(block_count - 2, 0), block_count):
            keep(kind, index).wait()

    returned[slot_part(cols.place), :] = send[slot_part(cols.place), :]

    def combine(index, chunk):
        back.wait_recv(index, chunk)

        def rows_of(part):
            tokens[part, chunk] = dot_nn(place_t[part, :], returned[:, chunk]).astype(jnp.bfloat16)

        over_blocks(all_tokens, token_rows, rows_of)
        home.start(index, chunk)

    over_chunks(chunks, width, combine)
    pair.wait_recv(0, None)
    grad_pair = pair_send[token_part(rows.place), :]
    for ahead in range(1, group_rows):
        shifted = pltpu.roll(pair_landed[group_rows - ahead - 1], ahead * col_count, 1)
        grad_pair = grad_pair + shifted
    grad_pair = grad_pair[:, :E]
    gates = gates_ref[token_part(rows.place), :]
    grad_logits = gates * (grad_pair - jnp.sum(gates * grad_pair, axis=-1, keepdims=True))
    grad_logits = grad_logits.astype(jnp.bfloat16)
    router_grad_ref[...] = dot_nn(grad_logits.astype(jnp.float32).T.astype(jnp.bfloat16), normed_ref[...])

    def finish(index, chunk):
        home.wait_recv(index, chunk)
        total = tokens[token_part(rows.place), chunk].astype(jnp.float32)
        for step in range(1, group_rows):
            total = total + landed[step - 1, :, chunk].astype(jnp.float32)
        sum_ref[:, chunk] = total + dot_nn(grad_logits, router_ref[:, chunk])

    over_chunks(chunks, width, finish)

    def drain(index, chunk):
        gather.wait_send(index, chunk)
        back.wait_send(index, chunk)
        home.wait_send(index, chunk)

    over_chunks(chunks, width, drain)
    pair.wait_send(0, None)


def moe_forward(dims, row_count, layer, own, routes, router, weights, moving, next_blocks):
    group_rows, col_count, copies, token_rows, slot_rows, chunks, width = dims
    all_tokens, all_slots = group_rows * token_rows, col_count * slot_rows
    model_width = own.shape[1]
    slice_width = weights[0].shape[-2]
    hidden = row_count * slice_width
    gather_dims = (row_count, col_count // 2) if next_blocks else None
    dense_sems = DenseGather.sems(gather_dims, 2) if next_blocks else []
    vmem = pl.BlockSpec(memory_space=pltpu.VMEM)
    outside = pl.BlockSpec(memory_space=pl.ANY)
    slot_array = pltpu.VMEM((all_slots, model_width), jnp.bfloat16)
    hidden_wide = pltpu.VMEM((all_slots, hidden), jnp.float32)
    weight_array = pltpu.VMEM((row_count, slice_width, model_width), jnp.bfloat16)
    return pl.pallas_call(
        functools.partial(
            moe_forward_kernel, dims, row_count, layer, moving, gather_dims
        ),
        out_shape=(
            jax.ShapeDtypeStruct((token_rows, model_width), jnp.float32),
            jax.ShapeDtypeStruct((all_tokens, E), jnp.float32),
            jax.ShapeDtypeStruct((all_slots, model_width), jnp.bfloat16),
            jax.ShapeDtypeStruct((all_slots, model_width), jnp.bfloat16),
            *(moved_shape(row_count, weights[kind]) for kind in moving),
            *(gathered_shapes(gather_dims, next_blocks) if next_blocks else ()),
        ),
        in_specs=[vmem] * 3 + [outside] * (3 + len(next_blocks)),
        out_specs=(vmem, vmem) + (outside,) * (2 + len(moving) + len(next_blocks)),
        scratch_shapes=[
            pltpu.VMEM((all_slots, all_tokens), jnp.bfloat16),
            pltpu.VMEM((all_tokens, all_slots), jnp.bfloat16),
            pltpu.VMEM((all_tokens, E), jnp.float32),
            weight_array,
            weight_array,
            weight_array,
            pltpu.VMEM((all_tokens, model_width), jnp.bfloat16),
            slot_array,
            slot_array,
            hidden_wide,
            hidden_wide,
            pltpu.VMEM((all_slots, hidden), jnp.bfloat16),
            slot_array,
            pltpu.VMEM((max(group_rows - 1, 1), token_rows, model_width), jnp.bfloat16),
            *exchange_sems(chunks, group_rows),
            *exchange_sems(chunks, col_count),
            *exchange_sems(chunks, col_count),
            *exchange_sems(chunks, group_rows),
            pltpu.SemaphoreType.DMA((5,)),
            *(WeightMove.sems(row_count) * len(moving)),
            *dense_sems,
        ],
        compiler_params=pltpu.CompilerParams(
            collective_id=1 + 7 * layer, has_side_effects=True, vmem_limit_bytes=vmem_most
        ),
        cost_estimate=long_cost,
        name="moe_forward",
    )(own, routes, router, *weights, *next_blocks)


def moe_backward(dims, own, routes, router, gates, normed, slots, returned, weights):
    group_rows, col_count, copies, token_rows, slot_rows, chunks, width = dims
    all_tokens, all_slots = group_rows * token_rows, col_count * slot_rows
    model_width = own.shape[1]
    block_count, slice_width = weights[0].shape[:2]
    hidden = block_count * slice_width
    vmem = pl.BlockSpec(memory_space=pltpu.VMEM)
    outside = pl.BlockSpec(memory_space=pl.ANY)
    slot_array = pltpu.VMEM((all_slots, model_width), jnp.bfloat16)
    hidden_narrow = pltpu.VMEM((all_slots, hidden), jnp.bfloat16)
    weight_array = pltpu.VMEM((block_count, slice_width, model_width), jnp.bfloat16)
    return pl.pallas_call(
        functools.partial(moe_backward_kernel, dims),
        out_shape=(
            jax.ShapeDtypeStruct((token_rows, model_width), jnp.float32),
            jax.ShapeDtypeStruct((E, model_width), jnp.float32),
            jax.ShapeDtypeStruct((block_count, 3, slice_width, model_width), jnp.bfloat16),
        ),
        in_specs=[vmem] * 5 + [outside] * 5,
        out_specs=(vmem, vmem, outside),
        scratch_shapes=[
            pltpu.VMEM((all_slots, all_tokens), jnp.bfloat16),
            pltpu.VMEM((all_tokens, all_slots), jnp.bfloat16),
            weight_array,
            weight_array,
            weight_array,
            pltpu.VMEM((all_tokens, model_width), jnp.bfloat16),
            slot_array,
            slot_array,
            hidden_narrow,
            hidden_narrow,
            hidden_narrow,
            pltpu.VMEM((all_slots, 1), jnp.float32),
            pltpu.VMEM((all_slots, 1), jnp.float32),
            slot_array,
            pltpu.VMEM((all_slots, hidden), jnp.float32),
            hidden_narrow,
            hidden_narrow,
            slot_array,
            pltpu.VMEM((hidden, all_slots), jnp.bfloat16),
            pltpu.VMEM((2, slice_width, model_width), jnp.bfloat16),
            pltpu.VMEM((max(group_rows - 1, 1), token_rows, model_width), jnp.bfloat16),
            pltpu.VMEM((all_tokens, 128), jnp.float32),
            pltpu.VMEM((max(group_rows - 1, 1), token_rows, 128), jnp.float32),
            *exchange_sems(chunks, group_rows),
            *exchange_sems(chunks, col_count),
            *exchange_sems(chunks, col_count),
            *exchange_sems(chunks, group_rows),
            *exchange_sems(1, group_rows),
            pltpu.SemaphoreType.DMA((7,)),
        ],
        compiler_params=pltpu.CompilerParams(
            collective_id=2, has_side_effects=True, vmem_limit_bytes=vmem_most
        ),
        cost_estimate=long_cost,
        name="moe_backward",
    )(own, routes, router, gates, normed, slots, returned, *weights)


def col_pairs():
    col_index = lax.axis_index("col")
    return col_index // 2, lax.rem(col_index, 2)


def dense_peers(row_count, pair_count):
    row_index = lax.axis_index("row")
    pair, side = col_pairs()
    rows = Peers(row_count, row_index, lambda place: {"row": place})
    pairs = Peers(pair_count, pair, lambda place: {"col": place * 2 + side})
    sides = Peers(2, side, lambda place: {"col": pair * 2 + place})
    return rows, pairs, sides


def reduce_dense_kernel(
    dims,
    normed_ref,
    grad_proj_ref,
    grad_mid_ref,
    attended_ref,
    small_ref,
    qkv_ref,
    out_ref,
    small_out_ref,
    *scratch,
):
    row_count, pair_count = dims
    kinds = 3
    buffers = [scratch[6 * kind : 6 * kind + 6] for kind in range(kinds)]
    sems = scratch[6 * kinds : 12 * kinds]
    normed_t, grad_proj, grad_mid_t, attended = scratch[12 * kinds :]
    side_sems = [(sems[6 * kind], sems[6 * kind + 1]) for kind in range(kinds)]
    pair_sems = [(sems[6 * kind + 2], sems[6 * kind + 3]) for kind in range(kinds)]
    row_sems = [(sems[6 * kind + 4], sems[6 * kind + 5]) for kind in range(kinds)]
    rows, pairs, sides = dense_peers(row_count, pair_count)
    other = 1 - sides.place

    def spread(target, source, turn):
        count = target.shape[0]
        size = source.shape[1] // count
        for index in range(count):
            part = source[:, index * size : (index + 1) * size]
            target[index] = part.T if turn else part

    spread(normed_t, normed_ref, True)
    spread(grad_proj, grad_proj_ref, False)
    spread(grad_mid_t, grad_mid_ref, True)
    spread(attended, attended_ref, False)

    def block(kind, row, pair, side):
        col = pair * 2 + side
        if kind == 0:
            return dot_nn(normed_t[row], grad_proj[col])
        if kind == 1:
            return dot_nn(grad_mid_t[col], attended[row])
        return small_ref[col, row].astype(jnp.float32)

    greet((rows, pairs, sides))
    outputs = (qkv_ref, out_ref, small_out_ref)

    def side_copy(kind, pair):
        side_send, side_recv = buffers[kind][0], buffers[kind][1]
        return send_to(
            side_send.at[pair],
            side_recv.at[pair],
            side_sems[kind],
            pair,
            sides.device_of(other),
        )

    def pair_copy(kind, step, row):
        place = pairs.ahead(step)
        half, pair_recv = buffers[kind][2], buffers[kind][3]
        return send_to(
            half.at[place, row],
            pair_recv.at[step - 1, row],
            pair_sems[kind],
            (step - 1) * row_count + row,
            pairs.device_of(place),
        )

    def row_copy(kind, step):
        place = rows.ahead(step)
        whole, row_recv = buffers[kind][4], buffers[kind][5]
        return send_to(
            whole.at[place],
            row_recv.at[step - 1],
            row_sems[kind],
            step - 1,
            rows.device_of(place),
        )

    def first(step, carry):
        pair = lax.rem(pairs.place + step, pair_count)
        for kind in range(kinds):
            for row in range(row_count):
                buffers[kind][0][pair, row] = block(kind, row, pair, other).astype(jnp.bfloat16)
            side_copy(kind, pair).start()
        return carry

    lax.fori_loop(1, pair_count + 1, first, 0)

    def second(step, carry):
        pair = lax.rem(pairs.place + step, pair_count)
        for kind in range(kinds):
            side_copy(kind, pair).wait_recv()
            side_recv, half = buffers[kind][1], buffers[kind][2]
            for row in range(row_count):
                total = block(kind, row, pair, sides.place)
                total = total + side_recv[pair, row].astype(jnp.float32)
                half[pair, row] = total.astype(jnp.bfloat16)

                @pl.when(step < pair_count)
                def _():
                    pair_copy(kind, step, row).start()

        return carry

    lax.fori_loop(1, pair_count + 1, second, 0)

    def third(step, carry):
        row = lax.rem(rows.place + step, row_count)
        for kind in range(kinds):
            half, pair_recv, whole = buffers[kind][2], buffers[kind][3], buffers[kind][4]
            total = half[pairs.place, row].astype(jnp.float32)
            for ahead in range(1, pair_count):
                pair_copy(kind, ahead, row).wait_recv()
                total = total + pair_recv[ahead - 1, row].astype(jnp.float32)

            whole[row] = total.astype(jnp.bfloat16)

            @pl.when(step < row_count)
            def _():
                row_copy(kind, step).start()

        return carry

    lax.fori_loop(1, row_count + 1, third, 0)
    for kind in range(kinds):
        whole, row_recv = buffers[kind][4], buffers[kind][5]
        total = whole[rows.place].astype(jnp.float32)
        for step in range(1, row_count):
            row_copy(kind, step).wait_recv()
            total = total + row_recv[step - 1].astype(jnp.float32)
        outputs[kind][...] = total

    def drain_sides(pair, carry):
        for kind in range(kinds):
            side_copy(kind, pair).wait_send()
        return carry

    lax.fori_loop(0, pair_count, drain_sides, 0)

    def drain_pairs(step, carry):
        for kind in range(kinds):
            for row in range(row_count):
                pair_copy(kind, step, row).wait_send()
        return carry

    lax.fori_loop(1, pair_count, drain_pairs, 0)
    for kind in range(kinds):
        for step in range(1, row_count):
            row_copy(kind, step).wait_send()


def reduce_dense(row_count, col_count, normed, grad_projected, grad_mid_b, attended, small):
    token_rows, model_width = normed.shape
    qkv_width, out_rows = grad_projected.shape[1], attended.shape[1]
    pair_count = col_count // 2
    shapes = (
        (model_width // row_count, qkv_width // col_count),
        (model_width // col_count, out_rows // row_count),
        small.shape[2:],
    )
    vmem = pl.BlockSpec(memory_space=pltpu.VMEM)
    scratch = []
    sems = []
    for height, breadth in shapes:
        for lead in (
            (pair_count, row_count),
            (pair_count, row_count),
            (pair_count, row_count),
            (max(pair_count - 1, 1), row_count),
            (row_count,),
            (max(row_count - 1, 1),),
        ):
            scratch.append(pltpu.VMEM((*lead, height, breadth), jnp.bfloat16))
        for count in (pair_count, max(pair_count - 1, 1) * row_count, max(row_count - 1, 1)):
            sems.extend([pltpu.SemaphoreType.DMA((count,))] * 2)
    operands = [
        pltpu.VMEM((row_count, shapes[0][0], token_rows), jnp.bfloat16),
        pltpu.VMEM((col_count, token_rows, shapes[0][1]), jnp.bfloat16),
        pltpu.VMEM((col_count, shapes[1][0], token_rows), jnp.bfloat16),
        pltpu.VMEM((row_count, token_rows, shapes[1][1]), jnp.bfloat16),
    ]
    return pl.pallas_call(
        functools.partial(reduce_dense_kernel, (row_count, pair_count)),
        out_shape=tuple(jax.ShapeDtypeStruct(shape, jnp.float32) for shape in shapes),
        in_specs=[vmem] * 5,
        out_specs=(vmem,) * 3,
        scratch_shapes=scratch + sems + operands,
        compiler_params=pltpu.CompilerParams(
            collective_id=3, has_side_effects=True, vmem_limit_bytes=vmem_most
        ),
        cost_estimate=no_cost,
        name="reduce_dense",
    )(normed, grad_projected, grad_mid_b, attended, small)


class DenseGather:
    def __init__(self, dims, own_blocks, fulls, sems):
        self.row_count, self.pair_count = dims
        self.rows, self.pairs, self.sides = dense_peers(*dims)
        self.own_blocks = own_blocks
        self.fulls = fulls
        self.kinds = range(len(own_blocks))
        self.row_sems = [sems[6 * kind : 6 * kind + 2] for kind in self.kinds]
        self.pair_sems = [sems[6 * kind + 2 : 6 * kind + 4] for kind in self.kinds]
        self.side_sems = [sems[6 * kind + 4 : 6 * kind + 6] for kind in self.kinds]
        self.local_sems = sems[6 * len(own_blocks)]

    @staticmethod
    def sems(dims, kinds):
        row_count, pair_count = dims
        sems = []
        for _ in range(kinds):
            for count in (
                max(row_count - 1, 1),
                max(pair_count - 1, 1) * row_count,
                pair_count * row_count,
            ):
                sems.extend([pltpu.SemaphoreType.DMA((count,))] * 2)
        return sems + [pltpu.SemaphoreType.DMA((kinds,))]

    def groups(self):
        return (self.rows, self.pairs, self.sides)

    def spot(self, kind, row, pair, side):
        col = pair * 2 + side
        height = self.own_blocks[kind].shape[0]
        return self.fulls[kind].at[row, pl.ds(pl.multiple_of(col * height, height), height), :]

    def own_spot(self, kind):
        return self.spot(kind, self.rows.place, self.pairs.place, self.sides.place)

    def own_copy(self, kind):
        return pltpu.make_async_copy(
            self.own_blocks[kind], self.own_spot(kind), self.local_sems.at[kind]
        )

    def row_copy(self, kind, step):
        return send_to(
            self.own_blocks[kind],
            self.own_spot(kind),
            self.row_sems[kind],
            step - 1,
            self.rows.device_of(self.rows.ahead(step)),
        )

    def row_landed(self, kind, step):
        place = self.rows.behind(step)
        landed = self.spot(kind, place, self.pairs.place, self.sides.place)
        return send_to(
            landed, landed, self.row_sems[kind], step - 1, self.rows.device_of(place)
        )

    def pair_copy(self, kind, step, number):
        block = self.spot(kind, self.rows.behind(number), self.pairs.place, self.sides.place)
        return send_to(
            block if number else self.own_blocks[kind],
            block,
            self.pair_sems[kind],
            (step - 1) * self.row_count + number,
            self.pairs.device_of(self.pairs.ahead(step)),
        )

    def pair_landed(self, kind, step, number):
        place = self.pairs.behind(step)
        landed = self.spot(kind, self.rows.behind(number), place, self.sides.place)
        return send_to(
            landed,
            landed,
            self.pair_sems[kind],
            (step - 1) * self.row_count + number,
            self.pairs.device_of(place),
        )

    def side_copy(self, kind, step, number):
        place = self.pairs.behind(step)
        block = self.spot(kind, self.rows.behind(number), place, self.sides.place)
        return send_to(
            block if step or number else self.own_blocks[kind],
            block,
            self.side_sems[kind],
            step * self.row_count + number,
            self.sides.device_of(1 - self.sides.place),
        )

    def side_landed(self, kind, step, number):
        place = self.pairs.behind(step)
        landed = self.spot(kind, self.rows.behind(number), place, 1 - self.sides.place)
        return send_to(
            landed,
            landed,
            self.side_sems[kind],
            step * self.row_count + number,
            self.sides.device_of(1 - self.sides.place),
        )

    def start(self, kind):
        self.own_copy(kind).start()
        for step in range(1, self.row_count):
            self.row_copy(kind, step).start()
        for step in range(1, self.pair_count):
            self.pair_copy(kind, step, 0).start()
        self.side_copy(kind, 0, 0).start()

    def pass_rows(self, kind):
        for number in range(1, self.row_count):
            self.row_landed(kind, number).wait_recv()
            for step in range(1, self.pair_count):
                self.pair_copy(kind, step, number).start()
            self.side_copy(kind, 0, number).start()

    def pass_pairs(self, kind):
        for number in range(self.row_count):
            for step in range(1, self.pair_count):
                self.pair_landed(kind, step, number).wait_recv()
                self.side_copy(kind, step, number).start()

    def finish(self, kind):
        self.own_copy(kind).wait()
        for step in range(self.pair_count):
            for number in range(self.row_count):
                self.side_landed(kind, step, number).wait_recv()
        for step in range(1, self.row_count):
            self.row_copy(kind, step).wait_send()
        for number in range(self.row_count):
            for step in range(1, self.pair_count):
                self.pair_copy(kind, step, number).wait_send()
            for step in range(self.pair_count):
                self.side_copy(kind, step, number).wait_send()


def gathered_shapes(dims, blocks):
    row_count, pair_count = dims
    return tuple(
        jax.ShapeDtypeStruct(
            (row_count, 2 * pair_count * block.shape[0], block.shape[1]), block.dtype
        )
        for block in blocks
    )


def gather_dense_kernel(
    dims,
    copies,
    qkv_ref,
    out_ref,
    routes_ref,
    router_ref,
    shards_ref,
    qkv_full,
    out_full,
    routes_all,
    router_all,
    moved,
    *sems,
):
    gather = DenseGather(dims, (qkv_ref, out_ref), (qkv_full, out_full), sems[:13])
    small_send, small_recv, local_sems = sems[13:16]
    rows = gather.rows
    move = WeightMove(rows, copies, 0, shards_ref, moved, sems[16:])
    small = [
        Exchange(
            rows,
            small_send,
            small_recv,
            lambda place, chunk, ref=ref: ref,
            lambda place, step, chunk, full=full: full.at[place],
        )
        for ref, full in ((routes_ref, routes_all), (router_ref, router_all))
    ]
    greet(gather.groups())
    own_copies = [
        pltpu.make_async_copy(ref, full.at[rows.place], local_sems.at[number])
        for number, (ref, full) in enumerate(((routes_ref, routes_all), (router_ref, router_all)))
    ]
    for kind in range(2):
        gather.start(kind)
        own_copies[kind].start()
        small[kind].start(kind, None)
    move.start()
    for kind in range(2):
        gather.pass_rows(kind)
    for kind in range(2):
        gather.pass_pairs(kind)
    for kind in range(2):
        small[kind].wait_recv(kind, None)
        gather.finish(kind)
        own_copies[kind].wait()
        small[kind].wait_send(kind, None)
    move.wait_recv()
    move.wait_send()


def gather_dense(row_count, col_count, copies, qkv_block, out_block, routes, router, shards):
    dims = (row_count, col_count // 2)
    outside = pl.BlockSpec(memory_space=pl.ANY)
    return pl.pallas_call(
        functools.partial(gather_dense_kernel, dims, copies),
        out_shape=gathered_shapes(dims, (qkv_block, out_block))
        + tuple(jax.ShapeDtypeStruct((row_count, *x.shape), x.dtype) for x in (routes, router))
        + (moved_shape(row_count, shards),),
        in_specs=[outside] * 5,
        out_specs=(outside,) * 5,
        scratch_shapes=DenseGather.sems(dims, 2)
        + [
            *exchange_sems(2, row_count),
            pltpu.SemaphoreType.DMA((2,)),
            *WeightMove.sems(row_count),
        ],
        compiler_params=pltpu.CompilerParams(collective_id=4, has_side_effects=True),
        cost_estimate=no_cost,
        name="gather_dense",
    )(qkv_block, out_block, routes, router, shards)


def order_grads_kernel(layer_count, block_count, *refs):
    blocks = refs[: layer_count * block_count]
    outputs = refs[layer_count * block_count : layer_count * block_count + 3]
    came, wide, in_sems, out_sems = refs[layer_count * block_count + 3 :]
    row_index = lax.axis_index("row")
    items = [
        (layer, step, kind)
        for layer in range(layer_count)
        for step in range(block_count)
        for kind in range(3)
    ]

    def load(number):
        layer, step, kind = items[number]
        return pltpu.make_async_copy(
            blocks[layer * block_count + step].at[kind],
            came.at[number % 4],
            in_sems.at[number % 4],
        )

    def store(number):
        layer, step, kind = items[number]
        expert = lax.rem(row_index + step, block_count)
        return pltpu.make_async_copy(
            wide.at[number % 4], outputs[kind].at[layer, expert], out_sems.at[number % 4]
        )

    count = len(items)
    for number in range(min(3, count)):
        load(number).start()
    for number in range(count):
        if number + 3 < count:
            load(number + 3).start()
        load(number).wait()
        if number >= 4:
            store(number - 4).wait()
        wide[number % 4] = came[number % 4].astype(jnp.float32)
        store(number).start()
    for number in range(max(count - 4, 0), count):
        store(number).wait()


def order_grads(layers):
    layer_count, block_count = len(layers), len(layers[0])
    _, slice_width, model_width = layers[0][0].shape
    outside = pl.BlockSpec(memory_space=pl.ANY)
    shape = jax.ShapeDtypeStruct((layer_count, block_count, slice_width, model_width), jnp.float32)
    return pl.pallas_call(
        functools.partial(order_grads_kernel, layer_count, block_count),
        out_shape=(shape,) * 3,
        in_specs=[outside] * (layer_count * block_count),
        out_specs=(outside,) * 3,
        scratch_shapes=[
            pltpu.VMEM((4, slice_width, model_width), jnp.bfloat16),
            pltpu.VMEM((4, slice_width, model_width), jnp.float32),
            pltpu.SemaphoreType.DMA((4,)),
            pltpu.SemaphoreType.DMA((4,)),
        ],
        compiler_params=pltpu.CompilerParams(vmem_limit_bytes=vmem_most),
        cost_estimate=no_cost,
        name="order_grads",
    )(*[block for blocks in layers for block in blocks])


def pieces_nt(left, weights_ref):
    pieces, _, size = weights_ref.shape
    total = None
    for index in range(pieces):
        part = dot_nt(left[:, index * size : (index + 1) * size], weights_ref[index])
        total = part if total is None else total + part
    return total


def rotate(values, cosine, sine):
    return values * cosine + pltpu.roll(values, HEAD_SIZE // 2, 1) * sine


def seen_keys(token_rows):
    position = lax.axis_index("col") * token_rows + iota((1, token_rows), 1)
    return (position // BLOCK + 1) * BLOCK


def attend_forward_kernel(
    dims,
    x_ref,
    gain_attn_ref,
    gain_moe_ref,
    cosine_ref,
    sine_ref,
    qkv_ref,
    out_w_ref,
    shards_ref,
    mid_ref,
    normed_ref,
    q_ref,
    kv_out,
    attended_ref,
    lse_ref,
    normed_moe_ref,
    moved,
    kv_all,
    value_t,
    proj,
    send_sem,
    recv_sem,
    local_sem,
    *move_sems,
):
    col_count, row_count, copies, layer, score_scale = dims
    token_rows = x_ref.shape[0]
    group = QUERY_HEADS // KEY_VALUE_HEADS
    kv_width = KEY_VALUE_HEADS * HEAD_SIZE
    cols = col_peers(col_count)

    def part(place):
        return pl.ds(pl.multiple_of(place * token_rows, token_rows), token_rows)

    share = Exchange(
        cols,
        send_sem,
        recv_sem,
        lambda place, chunk: kv_all.at[part(cols.place), :],
        lambda place, step, chunk: kv_all.at[part(place), :],
    )
    move = WeightMove(all_rows(row_count), copies, layer, shards_ref, moved, move_sems)
    greet((cols, move.rows))
    move.start()
    x = x_ref[...]
    inverse = lax.rsqrt(jnp.mean(x * x, axis=-1, keepdims=True) + eps_norm)
    normed_ref[...] = (x * inverse * gain_attn_ref[...]).astype(jnp.bfloat16)
    proj[...] = pieces_nt(normed_ref[...], qkv_ref)
    for head in range(KEY_VALUE_HEADS):
        lanes = slice(head * HEAD_SIZE, (head + 1) * HEAD_SIZE)
        start = QUERY_FEATURES + head * HEAD_SIZE
        turned = rotate(proj[:, start : start + HEAD_SIZE], cosine_ref[...], sine_ref[...])
        kv_all[part(cols.place), lanes] = turned.astype(jnp.bfloat16)
    kv_all[part(cols.place), kv_width:] = proj[:, QUERY_FEATURES + kv_width :].astype(jnp.bfloat16)
    share.start(0, None)
    for head in range(QUERY_HEADS):
        lanes = slice(head * HEAD_SIZE, (head + 1) * HEAD_SIZE)
        q_ref[:, lanes] = rotate(proj[:, lanes], cosine_ref[...], sine_ref[...]).astype(
            jnp.bfloat16
        )
    share.wait_recv(0, None)
    keep = pltpu.make_async_copy(kv_all, kv_out, local_sem)
    keep.start()
    value_t[...] = kv_all[:, kv_width:].T
    seen = seen_keys(token_rows)

    def head_step(index, carry):
        kv_head = index // group
        lanes = pl.ds(pl.multiple_of(index * HEAD_SIZE, HEAD_SIZE), HEAD_SIZE)
        kv_lanes = pl.ds(pl.multiple_of(kv_head * HEAD_SIZE, HEAD_SIZE), HEAD_SIZE)
        scores = dot_nt(kv_all[:, kv_lanes], q_ref[:, lanes]) * score_scale
        scores = jnp.where(iota(scores.shape, 0) < seen, scores, masked_score)
        peak = jnp.max(scores, axis=0, keepdims=True)
        exponent = jnp.exp(scores - peak)
        total = jnp.sum(exponent, axis=0, keepdims=True)
        attended = dot_nn(value_t[kv_lanes, :], exponent.astype(jnp.bfloat16)) / total
        attended_ref[:, lanes] = attended.T.astype(jnp.bfloat16)
        lse_ref[index] = peak + jnp.log(total)
        return carry

    lax.fori_loop(0, QUERY_HEADS, head_step, 0)
    mid = x_ref[...] + pieces_nt(attended_ref[...], out_w_ref)
    mid_ref[...] = mid
    inverse = lax.rsqrt(jnp.mean(mid * mid, axis=-1, keepdims=True) + eps_norm)
    normed_moe_ref[...] = (mid * inverse * gain_moe_ref[...]).astype(jnp.bfloat16)
    share.wait_send(0, None)
    keep.wait()
    move.wait_recv()
    move.wait_send()


def attend_forward(
    col_count,
    row_count,
    copies,
    layer,
    x,
    gain_attn,
    gain_moe,
    cosine,
    sine,
    qkv_full,
    out_full,
    shards,
):
    token_rows, model_width = x.shape
    seq_rows = col_count * token_rows
    kv_width = KEY_VALUE_HEADS * HEAD_SIZE
    vmem = pl.BlockSpec(memory_space=pltpu.VMEM)
    outside = pl.BlockSpec(memory_space=pl.ANY)
    rows_b = jax.ShapeDtypeStruct((token_rows, model_width), jnp.bfloat16)
    heads_b = jax.ShapeDtypeStruct((token_rows, QUERY_FEATURES), jnp.bfloat16)
    return pl.pallas_call(
        functools.partial(
            attend_forward_kernel, (col_count, row_count, copies, layer, HEAD_SIZE ** (-0.5))
        ),
        out_shape=(
            jax.ShapeDtypeStruct((token_rows, model_width), jnp.float32),
            rows_b,
            heads_b,
            jax.ShapeDtypeStruct((seq_rows, 2 * kv_width), jnp.bfloat16),
            heads_b,
            jax.ShapeDtypeStruct((QUERY_HEADS, 1, token_rows), jnp.float32),
            rows_b,
            moved_shape(row_count, shards),
        ),
        in_specs=[vmem] * 7 + [outside],
        out_specs=(vmem, vmem, vmem, outside, vmem, vmem, vmem, outside),
        scratch_shapes=[
            pltpu.VMEM((seq_rows, 2 * kv_width), jnp.bfloat16),
            pltpu.VMEM((kv_width, seq_rows), jnp.bfloat16),
            pltpu.VMEM((token_rows, QUERY_FEATURES + 2 * kv_width), jnp.float32),
            *exchange_sems(1, col_count),
            pltpu.SemaphoreType.DMA,
            *WeightMove.sems(row_count),
        ],
        compiler_params=pltpu.CompilerParams(
            collective_id=5 + 5 * layer, has_side_effects=True, vmem_limit_bytes=vmem_most
        ),
        cost_estimate=no_cost,
        name="attend_forward",
    )(x, gain_attn, gain_moe, cosine, sine, qkv_full, out_full, shards)


def norm_backward(values, gain, incoming):
    inverse = lax.rsqrt(jnp.mean(values * values, axis=-1, keepdims=True) + eps_norm)
    scaled = incoming * gain
    inner_mean = jnp.mean(scaled * values, axis=-1, keepdims=True)
    grad = inverse * scaled - values * (inverse * inverse * inverse) * inner_mean
    return grad, jnp.sum(incoming * values * inverse, axis=0, keepdims=True)


def attend_backward_kernel(
    dims,
    incoming_ref,
    grad_moe_ref,
    mid_ref,
    x_ref,
    gain_attn_ref,
    gain_moe_ref,
    cosine_ref,
    sine_ref,
    qkv_ref,
    out_w_ref,
    q_ref,
    kv_ref,
    attended_ref,
    lse_ref,
    grad_x_ref,
    grad_mid_ref,
    grad_proj_ref,
    grad_gain_attn_ref,
    grad_gain_moe_ref,
    grad_attended,
    key_t,
    key_sum,
    value_sum,
    grad_kv,
    landed,
    send_sem,
    recv_sem,
):
    col_count, score_scale = dims
    token_rows = x_ref.shape[0]
    group = QUERY_HEADS // KEY_VALUE_HEADS
    kv_width = KEY_VALUE_HEADS * HEAD_SIZE
    cols = col_peers(col_count)

    def part(place):
        return pl.ds(pl.multiple_of(place * token_rows, token_rows), token_rows)

    share = Exchange(
        cols,
        send_sem,
        recv_sem,
        lambda place, chunk: grad_kv.at[part(place), :],
        lambda place, step, chunk: landed.at[step - 1],
    )
    grad, gain_sum = norm_backward(mid_ref[...], gain_moe_ref[...], grad_moe_ref[...])
    grad_gain_moe_ref[...] = gain_sum
    grad_x_ref[...] = incoming_ref[...] + grad
    grad_mid_ref[...] = grad_x_ref[...].astype(jnp.bfloat16)
    pieces, _, size = out_w_ref.shape
    for index in range(pieces):
        lanes = slice(index * size, (index + 1) * size)
        grad_attended[:, lanes] = dot_nn(grad_mid_ref[...], out_w_ref[index]).astype(jnp.bfloat16)
    key_t[...] = kv_ref[:, :kv_width].T
    seen = seen_keys(token_rows)
    for kv_head in range(KEY_VALUE_HEADS):
        kv_lanes = slice(kv_head * HEAD_SIZE, (kv_head + 1) * HEAD_SIZE)
        value_lanes = slice(kv_width + kv_head * HEAD_SIZE, kv_width + (kv_head + 1) * HEAD_SIZE)
        key_sum[...] = jnp.zeros_like(key_sum)
        value_sum[...] = jnp.zeros_like(value_sum)

        def head_step(step, carry, kv_lanes=kv_lanes, value_lanes=value_lanes, kv_head=kv_head):
            index = kv_head * group + step
            lanes = pl.ds(pl.multiple_of(index * HEAD_SIZE, HEAD_SIZE), HEAD_SIZE)
            query = q_ref[:, lanes]
            grad_out = grad_attended[:, lanes]
            product = grad_out.astype(jnp.float32) * attended_ref[:, lanes].astype(jnp.float32)
            inner = jnp.sum(product.T, axis=0, keepdims=True)
            scores = dot_nt(kv_ref[:, kv_lanes], query) * score_scale
            soft = jnp.where(
                iota(scores.shape, 0) < seen, jnp.exp(scores - lse_ref[index]), 0.0
            )
            grad_soft = dot_nt(kv_ref[:, value_lanes], grad_out)
            grad_scores = (soft * (grad_soft - inner)).astype(jnp.bfloat16)
            value_sum[...] += dot_nn(soft.astype(jnp.bfloat16), grad_out)
            key_sum[...] += dot_nn(grad_scores, query)
            grad_q = (dot_nn(key_t[kv_lanes, :], grad_scores) * score_scale).T
            grad_q = rotate(grad_q, cosine_ref[...], -sine_ref[...])
            grad_proj_ref[:, lanes] = grad_q.astype(jnp.bfloat16)
            return carry

        lax.fori_loop(0, group, head_step, 0)
        grad_kv[:, kv_lanes] = (key_sum[...] * score_scale).astype(jnp.bfloat16)
        grad_kv[:, value_lanes] = value_sum[...].astype(jnp.bfloat16)
    greet((cols,))
    share.start(0, None)
    share.wait_recv(0, None)
    total = grad_kv[part(cols.place), :].astype(jnp.float32)
    for step in range(1, col_count):
        total = total + landed[step - 1].astype(jnp.float32)
    for head in range(KEY_VALUE_HEADS):
        start = QUERY_FEATURES + head * HEAD_SIZE
        grad_key = total[:, head * HEAD_SIZE : (head + 1) * HEAD_SIZE]
        grad_key = rotate(grad_key, cosine_ref[...], -sine_ref[...])
        grad_proj_ref[:, start : start + HEAD_SIZE] = grad_key.astype(jnp.bfloat16)
    grad_proj_ref[:, QUERY_FEATURES + kv_width :] = total[:, kv_width:].astype(jnp.bfloat16)
    pieces = qkv_ref.shape[0]
    grad_normed = [dot_nn(grad_proj_ref[...], qkv_ref[index]) for index in range(pieces)]
    grad_normed = jnp.concatenate(grad_normed, axis=1) if pieces > 1 else grad_normed[0]
    grad, gain_sum = norm_backward(x_ref[...], gain_attn_ref[...], grad_normed)
    grad_gain_attn_ref[...] = gain_sum
    grad_x_ref[...] += grad
    share.wait_send(0, None)


def attend_backward(
    col_count,
    incoming,
    grad_moe,
    mid,
    x,
    gain_attn,
    gain_moe,
    cosine,
    sine,
    qkv_full,
    out_full,
    queries,
    key_value,
    attended,
    log_sums,
):
    token_rows, model_width = x.shape
    seq_rows = col_count * token_rows
    kv_width = KEY_VALUE_HEADS * HEAD_SIZE
    vmem = pl.BlockSpec(memory_space=pltpu.VMEM)
    gain = jax.ShapeDtypeStruct((1, model_width), jnp.float32)
    return pl.pallas_call(
        functools.partial(attend_backward_kernel, (col_count, HEAD_SIZE ** (-0.5))),
        out_shape=(
            jax.ShapeDtypeStruct((token_rows, model_width), jnp.float32),
            jax.ShapeDtypeStruct((token_rows, model_width), jnp.bfloat16),
            jax.ShapeDtypeStruct((token_rows, QUERY_FEATURES + 2 * kv_width), jnp.bfloat16),
            gain,
            gain,
        ),
        in_specs=[vmem] * 14,
        out_specs=(vmem,) * 5,
        scratch_shapes=[
            pltpu.VMEM((token_rows, QUERY_FEATURES), jnp.bfloat16),
            pltpu.VMEM((kv_width, seq_rows), jnp.bfloat16),
            pltpu.VMEM((seq_rows, HEAD_SIZE), jnp.float32),
            pltpu.VMEM((seq_rows, HEAD_SIZE), jnp.float32),
            pltpu.VMEM((seq_rows, 2 * kv_width), jnp.bfloat16),
            pltpu.VMEM((max(col_count - 1, 1), token_rows, 2 * kv_width), jnp.bfloat16),
            *exchange_sems(1, col_count),
        ],
        compiler_params=pltpu.CompilerParams(
            collective_id=6, has_side_effects=True, vmem_limit_bytes=vmem_most
        ),
        cost_estimate=no_cost,
        name="attend_backward",
    )(
        incoming,
        grad_moe,
        mid,
        x,
        gain_attn,
        gain_moe,
        cosine,
        sine,
        qkv_full,
        out_full,
        queries,
        key_value,
        attended,
        log_sums,
    )


def place_first(values, group_rows, expert_pick):
    rolled = jnp.roll(values.reshape(-1, group_rows, values.shape[1]), -expert_pick, axis=1)
    return rolled.transpose(1, 0, 2).reshape(values.shape)


def place_back(values, group_rows, expert_pick):
    rolled = values.reshape(group_rows, -1, values.shape[1]).transpose(1, 0, 2)
    return jnp.roll(rolled, expert_pick, axis=1).reshape(values.shape)


def body(
    hidden_in, routes, norm_attn, w_qkv, w_out, norm_moe, w_router, w_gate, w_up, w_down, cotangent
):
    row_count = lax.axis_size("row")
    col_count = lax.axis_size("col")
    device_count = row_count * col_count
    row_index = lax.axis_index("row")
    col_index = lax.axis_index("col")
    layer_count = w_qkv.shape[0]
    token_rows = hidden_in.shape[0]
    model_width = hidden_in.shape[1]
    local_experts = w_gate.shape[1]
    slice_width = w_gate.shape[3]
    copies = row_count // local_experts
    expert_pick = row_index // copies
    slot_rows = -(-local_experts * CAP // 16) * 16
    chunks = model_width // 384
    dims = (
        local_experts,
        col_count,
        copies,
        token_rows,
        slot_rows,
        chunks,
        model_width // chunks,
    )
    positions = col_index * token_rows + jnp.arange(token_rows, dtype=jnp.int32)
    cosine, sine = rope_angles(positions, HEAD_SIZE // 2)
    cosine = jnp.concatenate([cosine, cosine], axis=1)
    sine = jnp.concatenate([-sine, sine], axis=1)

    def behind(step):
        return [(index, (index + step) % row_count) for index in range(row_count)]

    def move_grads(grads):
        blocks = [grads[0]]
        for step in range(1, row_count):
            blocks.append(lax.ppermute(grads[step], "row", behind(row_count - step)))
        return tuple(blocks)

    def own_grads(blocks):
        stacked = jnp.stack(blocks)
        ordered = [
            lax.dynamic_index_in_dim(
                stacked, (index - row_index) % row_count, axis=0, keepdims=False
            ).astype(wide_type)
            for index in range(row_count)
        ]
        return [
            functools.reduce(jnp.add, ordered[index * copies : (index + 1) * copies])
            for index in range(local_experts)
        ]

    def pieced(full):
        if full.shape[2] % 128 == 0:
            return full
        return full.transpose(1, 0, 2).reshape(1, full.shape[1], -1)

    def packed(values):
        return jnp.pad(values.reshape(-1), (0, -values.size % 2048)).reshape(-1, 128)

    shards = (w_gate.transpose(0, 1, 3, 2), w_up.transpose(0, 1, 3, 2), w_down)
    experts = []
    route_lines = routes.transpose(0, 2, 1)
    router_lines = w_router.transpose(0, 2, 1)
    qkv_full, out_full, routes_all, router_all, moved_gate = gather_dense(
        row_count,
        col_count,
        copies,
        w_qkv[0].T,
        w_out[0].T,
        packed(route_lines),
        packed(router_lines),
        shards[0],
    )
    dense = [(pieced(qkv_full), pieced(out_full))]
    routes_all = routes_all.reshape(row_count, -1)[:, : route_lines.size]
    routes_all = routes_all.reshape(row_count, *route_lines.shape)
    if copies > 1:
        routes_all = jnp.take(
            routes_all, row_index % copies + copies * jnp.arange(local_experts), axis=0
        )
    router_all = router_all.reshape(row_count, -1)[:, : router_lines.size]
    router_all = router_all.reshape(row_count, *router_lines.shape)
    router_all = router_all.transpose(1, 2, 0, 3).reshape(layer_count, E, model_width)
    routers = [
        place_first(router_all[index], local_experts, expert_pick) for index in range(layer_count)
    ]
    gains_attn = norm_attn.astype(wide_type)[:, None, :]
    gains_moe = norm_moe.astype(wide_type)[:, None, :]
    hidden = hidden_in.astype(wide_type)
    saved = []
    for layer_index in range(layer_count):
        early = 0 if layer_index else 1
        mid, normed, queries, key_value, attended, log_sums, normed_moe, moved = attend_forward(
            col_count,
            row_count,
            copies,
            layer_index,
            hidden,
            gains_attn[layer_index],
            gains_moe[layer_index],
            cosine,
            sine,
            *dense[layer_index],
            shards[early],
        )
        if layer_index == 0:
            weights, moving = [moved_gate, moved, shards[2]], (2,)
        else:
            weights, moving = [moved, shards[1], shards[2]], (1, 2)
        next_blocks = ()
        if layer_index + 1 < layer_count:
            next_blocks = (w_qkv[layer_index + 1].T, w_out[layer_index + 1].T)
        mixed, gates, slots, returned, *rest = moe_forward(
            dims,
            row_count,
            layer_index,
            normed_moe,
            routes_all[:, layer_index],
            routers[layer_index],
            weights,
            moving,
            next_blocks,
        )
        for kind, moved in zip(moving, rest):
            weights[kind] = moved
        experts.append(weights)
        if next_blocks:
            dense.append(tuple(pieced(full) for full in rest[len(moving) :]))
        saved.append(
            (hidden, mid, normed, queries, key_value, attended, log_sums, normed_moe)
            + (gates, slots, returned)
        )
        hidden = mid + mixed
    incoming = cotangent.astype(wide_type)
    dense_results = [None] * layer_count
    small_results = [None] * layer_count
    expert_results = [None] * layer_count
    for layer_index in reversed(range(layer_count)):
        x, mid, normed, queries, key_value, attended, log_sums, normed_moe = saved[layer_index][:8]
        gates, slots, returned = saved[layer_index][8:]
        grad_moe, grad_router, expert_grads = moe_backward(
            dims,
            incoming.astype(narrow_type),
            routes_all[:, layer_index],
            routers[layer_index],
            gates,
            normed_moe,
            slots,
            returned,
            experts[layer_index],
        )
        expert_results[layer_index] = move_grads(expert_grads)
        incoming, grad_mid, grad_projected, grad_gain_attn, grad_gain_moe = attend_backward(
            col_count,
            incoming,
            grad_moe,
            mid,
            x,
            gains_attn[layer_index],
            gains_moe[layer_index],
            cosine,
            sine,
            *dense[layer_index],
            queries,
            key_value,
            attended,
            log_sums,
        )
        small = jnp.concatenate(
            [
                place_back(grad_router, local_experts, expert_pick),
                grad_gain_attn,
                grad_gain_moe,
            ],
            axis=0,
        ).astype(narrow_type)
        small = small.reshape(E + 2, device_count, -1).transpose(1, 0, 2).reshape(device_count, -1)
        small_size = small.shape[1]
        small_rows = -(-small_size // 2048) * 16
        small = jnp.pad(small, ((0, 0), (0, small_rows * 128 - small_size)))
        small = small.reshape(row_count, col_count, small_rows, 128).transpose(1, 0, 2, 3)
        grad_qkv_block, grad_out_block, small = reduce_dense(
            row_count, col_count, normed, grad_projected, grad_mid, attended, small
        )
        dense_results[layer_index] = (grad_qkv_block, grad_out_block.T)
        small_results[layer_index] = small.reshape(-1)[:small_size].reshape(E + 2, -1).T
        if layer_index > 0:
            incoming, dense_results[layer_index], expert_results[layer_index] = (
                lax.optimization_barrier(
                    (incoming, dense_results[layer_index], expert_results[layer_index])
                )
            )
    small = jnp.stack(small_results)
    if copies == 1:
        grad_gate, grad_up, grad_down = order_grads(expert_results)
    else:
        expert_results = [own_grads(blocks) for blocks in expert_results]
        grad_gate, grad_up, grad_down = (
            jnp.stack([jnp.stack([got[kind] for got in layer]) for layer in expert_results])
            for kind in range(3)
        )
    grad_gate, grad_up = grad_gate.swapaxes(2, 3), grad_up.swapaxes(2, 3)
    return (
        hidden,
        incoming,
        small[:, :, E],
        jnp.stack([dense_results[index][0] for index in range(layer_count)]),
        jnp.stack([dense_results[index][1] for index in range(layer_count)]),
        small[:, :, E + 1],
        small[:, :, :E],
        grad_gate,
        grad_up,
        grad_down,
    )


def solution(mesh):
    in_specs = (
        P(("row", "col"), None),
        P(None, ("row", "col"), None),
        P(),
        P(None, "row", "col"),
        P(None, "row", "col"),
        P(),
        P(None, "row", None),
        P(None, "col", None, "row"),
        P(None, "col", None, "row"),
        P(None, "col", "row", None),
        P(("row", "col"), None),
    )
    out_specs = (
        P(("row", "col"), None),
        P(("row", "col"), None),
        P(None, ("row", "col")),
        P(None, "row", "col"),
        P(None, "row", "col"),
        P(None, ("row", "col")),
        P(None, ("row", "col"), None),
        P(None, "col", None, "row"),
        P(None, "col", None, "row"),
        P(None, "col", "row", None),
    )
    return jax.shard_map(body, mesh=mesh, in_specs=in_specs, out_specs=out_specs, check_vma=False)
```

time: 1770 us -> 1510 us (0.85)
  Pallas kernels: 1110 us -> 1440 us
  blocking collectives: 133 us -> 0 us
  local copies, waits for them, and re-layouts: 160 us -> 30.6 us
  waiting for transfers between devices: 114 us -> 0.02 us
  matrix products: 82.9 us -> 0 us
  starting transfers between devices: 75.5 us -> 7.65 us
  other arithmetic: 70.7 us -> 19.4 us
    pallas_call x7 -> x8, Pallas kernels: 516 us -> 827 us  [the longest x2 483 us: moe_forward(): pl.pallas_call(functools.partial(moe_forward_kernel, dims, row_count, lay...]
    all_gather x2 -> x0, blocking collectives: 133 us -> none  [the longest x1 82.4 us: body(): lax.all_gather(routes, 'row', axis=0, axis_index_groups=token_rows_of)]
    all_to_all x12 -> x0, waiting for transfers between devices: 105 us -> none  [the longest x6 87.3 us: move_weights(): lax.all_to_all(spread, 'row', split_axis=0, concat_axis=0, tiled=True)]
    dot_general x20 -> x0, matrix products: 82.9 us -> none  [the longest x2 14.4 us: body(): jnp.einsum('cf,cd->fd', grad_up_b, slot_inputs, preferred_element_type=wi...]
    all_to_all x12 -> x0, starting transfers between devices: 74.8 us -> none  [the longest x6 37.6 us: move_weights(): lax.all_to_all(spread, 'row', split_axis=0, concat_axis=0, tiled=True)]
    pallas_call x2, Pallas kernels: 193 us -> 240 us  [reduce_dense(): pl.pallas_call(functools.partial(reduce_dense_kernel, (row_count, pair_co...]
    pallas_call x2, Pallas kernels: 400 us -> 377 us  [moe_backward(): pl.pallas_call(functools.partial(moe_backward_kernel, dims), out_shape=(j...]
    transpose x14 -> x5, local copies, waits for them, and re-layouts: 26.4 us -> 3.27 us  [the longest x1 1.72 us: body(): next_blocks = (w_qkv[layer_index + 1].T, w_out[layer_index + 1].T)]
  transfers between devices with their start and end apart: 18 -> 6, of which waited for: 6 -> 0; matrix products, arithmetic and copies ran while one was open for 16% -> 1% of each run, Pallas kernels for 39% -> 24%
where the time goes in v2:
time: 1510 us; the launch traced here: 1500 us
  Pallas kernels  1440 us (95%)
  local copies, waits for them, and re-layouts  30.6 us (2%)
  other arithmetic  19.4 us (1%)
    pallas_call x2, Pallas kernels, moe_forward(): pl.pallas_call(functools.partial(moe_forward_kernel, dims, row_count, lay...  483 us
    pallas_call x2, Pallas kernels, moe_backward(): pl.pallas_call(functools.partial(moe_backward_kernel, dims), out_shape=(j...  377 us
    pallas_call x2, Pallas kernels, reduce_dense(): pl.pallas_call(functools.partial(reduce_dense_kernel, (row_count, pair_co...  240 us
    pallas_call x2, Pallas kernels, attend_forward(): pl.pallas_call(functools.partial(attend_forward_kernel, (col_count, row_c...  123 us
    pallas_call x2, Pallas kernels, attend_backward(): pl.pallas_call(functools.partial(attend_backward_kernel, (col_count, HEAD...  116 us
    pallas_call x1, Pallas kernels, gather_dense(): pl.pallas_call(functools.partial(gather_dense_kernel, dims, copies), out_...  90 us
  transfers between devices with their start and end apart: 6, of which 0 were waited for; matrix products, arithmetic and copies ran while one was open for 1% of the time, Pallas kernels for 24%

profile of v2, /device:TPU:30, one launch (start us, length us, event | category | flops | bytes accessed | tf_op | source)
XLA Modules:
  0.0 1503.4 jit_solution(11381967086011486698)
XLA Ops:
  0.7 1.1 fusion.9
  1.8 0.8 copy.36
  2.6 1.7 slice_bitcast_fusion.8
  4.3 0.7 reshape.109.router_ref
  5.0 0.6 reshape.108.routes_ref
  5.6 90.0 %gather_dense.1 = (bf16[4,2048,384]{2,1,0:T(8,128)(2,1)}, bf16[4,1536,384]{2,1,0:T(8,128)(2,1)}, s32[4,16,128]{2,1,0:T(8,128)}, bf16[4,192,128]{2,1,0:T(8,128)(2,1)}, bf16[4,192,1536]{2,1,0:T(8,128)(2,1)}) custom-call(bf16[256,384]{1,0:T(8,128)(2,1)} %bitcast.112, bf16[192,384]{1,0:T(8,128)(2,1)} %get-tuple-element.155.out_ref, ...), custom_call_target="tpu_custom_call" | custom-call | tf_op jit(solution)/shard_map/gather_dense/pallas_call | solution.py:1311
  95.6 1.1 reshape_reshape.7
  96.7 0.2 copy.55
  97.0 0.4 fusion.5
  97.4 0.7 copy.57
  98.1 1.3 convert_element_type.30.x_ref
  99.4 0.6 slice_bitcast_fusion.10
  100.1 0.8 copy.38
  100.9 0.7 copy.56
  101.5 0.5 fusion.8
  102.1 0.6 fusion.11
  102.7 0.8 pad_maximum_fusion.2
  103.6 60.9 %attend_forward.2 = (f32[256,1536]{1,0:T(8,128)}, bf16[256,1536]{1,0:T(8,128)(2,1)}, bf16[256,1536]{1,0:T(8,128)(2,1)}, bf16[2048,512]{1,0:T(8,128)(2,1)}, bf16[...) custom-call(f32[256,1536]{1,0:T(8,128)} %convert_element_type.30.x_ref,, ...), custom_call_target="tpu_custom_call" | custom-call | tf_op jit(solution)/shard_map/attend_forward/pallas_call | solution.py:1525
  164.5 229.5 %moe_forward.2 = (f32[256,1536]{1,0:T(8,128)}, f32[1024,32]{1,0:T(8,128)}, bf16[1152,1536]{1,0:T(8,128)(2,1)}, bf16[1152,1536]{1,0:T(8,128)(2,1)}, bf16[4,192,15...) custom-call(bf16[256,1536]{1,0:T(8,128)(2,1)} %get-tuple-element.81.refs_0_.refs_4_, ...), custom_call_target="tpu_custom_call" | custom-call | bytes 629145600 | tf_op jit(solution)/shard_map/moe_forward/pallas_call | solution.py:798
  394.0 2.7 add.38.x_ref
  396.8 62.2 %attend_forward.3 = (f32[256,1536]{1,0:T(8,128)}, bf16[256,1536]{1,0:T(8,128)(2,1)}, bf16[256,1536]{1,0:T(8,128)(2,1)}, bf16[2048,512]{1,0:T(8,128)(2,1)}, bf16[...) custom-call(f32[256,1536]{1,0:T(8,128)} %add.38.x_ref, ...), custom_call_target="tpu_custom_call" | custom-call | tf_op jit(solution)/shard_map/attend_forward/pallas_call | solution.py:1525
  459.0 253.4 %moe_forward.3 = (f32[256,1536]{1,0:T(8,128)}, f32[1024,32]{1,0:T(8,128)}, bf16[1152,1536]{1,0:T(8,128)(2,1)}, bf16[1152,1536]{1,0:T(8,128)(2,1)}, bf16[4,192,15...) custom-call(bf16[256,1536]{1,0:T(8,128)(2,1)} %get-tuple-element.90.refs_0_.refs_4_, ...), custom_call_target="tpu_custom_call" | custom-call | bytes 629145600 | tf_op jit(solution)/shard_map/moe_forward/pallas_call | solution.py:798
  712.4 189.2 %moe_backward.2 = (f32[256,1536]{1,0:T(8,128)}, f32[32,1536]{1,0:T(8,128)}, bf16[4,3,192,1536]{3,2,1,0:T(8,128)(2,1)}) custom-call(bf16[256,1536]{1,0:T(8,128)(2,1)} %refs_0_, s32[4,4,256]{2,1,0:T(4,128)} %get-tuple-element.160.refs_1_, bf16[32,1536]{1,0:T(8,128)(2,1)} %bitcast.109, f32[1024,32]{1,0:T(8,128)} %get-tuple-element.93.refs_3_, ...), custom_call_target="tpu_custom_call" | custom-call | bytes 629145600 | tf_op jit(solution)/shard_map/moe_backward/pallas_call | solution.py:854
  901.6 6.2 slice_bitcast_fusion.4
  907.9 3.8 collective-permute-start.2
  911.7 1.3 convert_element_type.34.incoming_ref
  913.0 58.4 %attend_backward.2 = (f32[256,1536]{1,0:T(8,128)}, bf16[256,1536]{1,0:T(8,128)(2,1)}, bf16[256,2048]{1,0:T(8,128)(2,1)}, f32[1,1536]{1,0:T(1,128)}, f32[1,1536]{1,0:T(1,128)}) custom-call(f32[256,1536]{1,0:T(8,128)} %convert_element_type.34.incoming_ref, f32[256,1536]{1,0:T(8,128)} %get-tuple-element.98.grad_moe_ref, f32[256,1536]{1,0:T(8,128)} %get-tuple-element.89.mid_ref, ...), custom_call_target="tpu_custom_call" | custom-call | tf_op jit(solution)/shard_map/attend_backward/pallas_call | solution.py:1693
  971.5 0.7 convert_reduce_fusion.3
  972.2 0.1 concatenate.37
  972.3 0.7 convert_reduce_fusion.2
  973.0 0.1 concatenate.38
  973.1 0.1 copy.54
  973.3 0.2 fusion.3
  973.5 0.2 concatenate.36
  973.8 0.1 copy.31
  973.9 0.2 reshape.113
  974.1 0.7 copy_bitcast_fusion.6.small_ref
  974.8 120.6 %reduce_dense.2 = (f32[384,256]{1,0:T(8,128)}, f32[192,384]{1,0:T(8,128)}, f32[16,128]{1,0:T(8,128)}) custom-call(bf16[256,1536]{1,0:T(8,128)(2,1)} %get-tuple-element.104.normed_ref, bf16[256,2048]{1,0:T(8,128)(2,1)} %get-tuple-element.105.grad_proj_ref, bf16[256,1536]{1,0:T(8,128)(2,1)} %get-tuple-element.106.grad_mid_ref, ...), custom_call_target="tpu_custom_call" | custom-call | tf_op jit(solution)/shard_map/reduce_dense/pallas_call | solution.py:1097
  1095.5 1.0 convert_element_type.35.refs_0_
  1096.4 188.1 %moe_backward.3 = (f32[256,1536]{1,0:T(8,128)}, f32[32,1536]{1,0:T(8,128)}, bf16[4,3,192,1536]{3,2,1,0:T(8,128)(2,1)}) custom-call(bf16[256,1536]{1,0:T(8,128)(2,1)} %convert_element_type.35.refs_0_, s32[4,4,256]{2,1,0:T(4,128)} %get-tuple-element.161.refs_1_, bf16[32,1536]{1,0:T(8,128)(2,1)} %bitcast.111, f32[1024,32]{1,0:T(8,128)} %get-tuple-element.114.refs_3_, ...), custom_call_target="tpu_custom_call" | custom-call | bytes 629145600 | tf_op jit(solution)/shard_map/moe_backward/pallas_call | solution.py:854
  1284.6 6.2 slice_bitcast_fusion
  1290.8 3.8 collective-permute-start.5
  1294.6 0.7 reshape.121
  1295.3 2.7 add.39
  1298.1 57.5 %attend_backward.3 = (f32[256,1536]{1,0:T(8,128)}, bf16[256,1536]{1,0:T(8,128)(2,1)}, bf16[256,2048]{1,0:T(8,128)(2,1)}, f32[1,1536]{1,0:T(1,128)}, f32[1,1536]{1,0:T(1,128)}) custom-call(f32[256,1536]{1,0:T(8,128)} %get-tuple-element.113.incoming_ref, f32[256,1536]{1,0:T(8,128)} %get-tuple-element.118.grad_moe_ref, f32[256,1536]{1,0:T(8,128)} %get-tuple-element.80.mid_ref, ...), custom_call_target="tpu_custom_call" | custom-call | tf_op jit(solution)/shard_map/attend_backward/pallas_call | solution.py:1693
  1355.5 0.7 convert_reduce_fusion.1
  1356.3 0.1 concatenate.41
  1356.3 0.7 convert_reduce_fusion
  1357.1 0.1 concatenate.42
  1357.2 0.1 copy.53
  1357.3 0.2 fusion.1
  1357.5 0.2 concatenate.40
  1357.8 0.1 copy.34
  1358.0 0.2 reshape.116
  1358.2 0.7 copy_bitcast_fusion.5.small_ref
  1358.9 119.5 %reduce_dense.3 = (f32[384,256]{1,0:T(8,128)}, f32[192,384]{1,0:T(8,128)}, f32[16,128]{1,0:T(8,128)}) custom-call(bf16[256,1536]{1,0:T(8,128)(2,1)} %get-tuple-element.124.normed_ref, bf16[256,2048]{1,0:T(8,128)(2,1)} %get-tuple-element.125.grad_proj_ref, bf16[256,1536]{1,0:T(8,128)(2,1)} %get-tuple-element.126.grad_mid_ref, ...), custom_call_target="tpu_custom_call" | custom-call | tf_op jit(solution)/shard_map/reduce_dense/pallas_call | solution.py:1097
  1478.4 0.8 reshape.119
  1479.2 0.6 pad_maximum_fusion.5
  1479.7 0.6 pad_maximum_fusion.4
  1480.3 1.9 pad_maximum_fusion.1
  1482.2 2.0 pad_maximum_fusion
  1484.3 1.2 copy-done.4
  1485.5 15.0 %order_grads.1 = (f32[2,4,192,1536]{3,2,1,0:T(8,128)}, f32[2,4,192,1536]{3,2,1,0:T(8,128)}, f32[2,4,192,1536]{3,2,1,0:T(8,128)}) custom-call(bf16[3,192,1536]{2,1,0:T(8,128)(2,1)} %get-tuple-element.147.refs_0_, bf16[3,192,1536]{2,1,0:T(8,128)(2,1)} %copy-done.4, bf16[3,192,1536]{2,1,0:T(8,128)(2,1)} %collective-permute-done.4.refs_2_, ...), custom_call_target="tpu_custom_call" | custom-call | tf_op jit(solution)/shard_map/order_grads/pallas_call | solution.py:1377
  1500.6 2.7 copy.59
  (49 shorter events, 0.4 us)
Async XLA Ops:
  0.6 3.7 copy-start.9
  0.7 4.3 copy-start.14
  95.6 2.5 copy-start.5
  96.9 2.5 copy-start.10
  98.1 4.0 copy-start.11
  98.1 4.0 copy-start.12
  164.5 229.6 %copy-start = (f32[256,1536]{1,0:T(8,128)S(1)}, f32[256,1536]{1,0:T(8,128)}, u32[]{:S(2)}) copy-start(f32[256,1536]{1,0:T(8,128)} %get-tuple-element.80.mid_ref) | copy-start | bytes 4718596
  901.6 10.1 copy-start.3
  907.9 187.5 %collective-permute-start = (bf16[3,192,1536]{2,1,0:T(8,128)(2,1)}, bf16[3,192,1536]{2,1,0:T(8,128)(2,1)}, u32[]{:S(2)}, u32[]{:S(2)}) collective-permute-start(bf16[3,192,1536]{2,1,0:T(8,128)(2,1)} %get-tuple-element.150), channel_id=1, source_target_pairs={{0,24},{8,0},{16,8},{24,16},{1,25},{9,1},{17,9},{25,17},{2,26},{10... | collective-permute-start | bytes 5308424 | tf_op jit(solution)/shard_map/ppermute | solution.py:1783
  907.9 187.5 %collective-permute-start.1 = (bf16[3,192,1536]{2,1,0:T(8,128)(2,1)}, bf16[3,192,1536]{2,1,0:T(8,128)(2,1)}, u32[]{:S(2)}, u32[]{:S(2)}) collective-permute-start(bf16[3,192,1536]{2,1,0:T(8,128)(2,1)} %get-tuple-element.149), channel_id=1, source_target_pairs={{0,16},{8,24},{16,0},{24,8},{1,17},{9,25},{17,1},{25,9},{2,18},{10... | collective-permute-start | bytes 5308424 | tf_op jit(solution)/shard_map/ppermute | solution.py:1783
  907.9 187.6 %collective-permute-start.2 = (bf16[3,192,1536]{2,1,0:T(8,128)(2,1)}, bf16[3,192,1536]{2,1,0:T(8,128)(2,1)}, u32[]{:S(2)}, u32[]{:S(2)}) collective-permute-start(bf16[3,192,1536]{2,1,0:T(8,128)(2,1)} %get-tuple-element.148), channel_id=1, source_target_pairs={{0,8},{8,16},{16,24},{24,0},{1,9},{9,17},{17,25},{25,1},{2,10},{10... | collective-permute-start | bytes 5308424 | tf_op jit(solution)/shard_map/ppermute | solution.py:1783
  913.0 60.1 %copy-start.6 = (f32[32,1536]{1,0:T(8,128)S(1)}, f32[32,1536]{1,0:T(8,128)}, u32[]{:S(2)}) copy-start(f32[32,1536]{1,0:T(8,128)} %get-tuple-element.107) | copy-start | bytes 589828
  974.8 120.7 %copy-start.2 = (f32[256,1536]{1,0:T(8,128)S(1)}, f32[256,1536]{1,0:T(8,128)}, u32[]{:S(2)}) copy-start(f32[256,1536]{1,0:T(8,128)} %get-tuple-element.113.incoming_ref) | copy-start | bytes 4718596
  1284.5 10.1 copy-start.13
  1284.6 10.8 copy-start.1
  1290.8 193.5 %collective-permute-start.3 = (bf16[3,192,1536]{2,1,0:T(8,128)(2,1)}, bf16[3,192,1536]{2,1,0:T(8,128)(2,1)S(1)}, u32[]{:S(2)}, u32[]{:S(2)}) collective-permute-start(bf16[3,192,1536]{2,1,0:T(8,128)(2,1)} %get-tuple-element.146), channel_id=1, source_target_pairs={{0,24},{8,0},{16,8},{24,16},{1,25},{9,1},{17,9},{25,17},{2,26},{10... | collective-permute-start | bytes 5308424 | tf_op jit(solution)/shard_map/ppermute | solution.py:1783
  1290.8 193.5 %collective-permute-start.4 = (bf16[3,192,1536]{2,1,0:T(8,128)(2,1)}, bf16[3,192,1536]{2,1,0:T(8,128)(2,1)}, u32[]{:S(2)}, u32[]{:S(2)}) collective-permute-start(bf16[3,192,1536]{2,1,0:T(8,128)(2,1)} %get-tuple-element.145), channel_id=1, source_target_pairs={{0,16},{8,24},{16,0},{24,8},{1,17},{9,25},{17,1},{25,9},{2,18},{10... | collective-permute-start | bytes 5308424 | tf_op jit(solution)/shard_map/ppermute | solution.py:1783
  1290.8 193.5 %collective-permute-start.5 = (bf16[3,192,1536]{2,1,0:T(8,128)(2,1)}, bf16[3,192,1536]{2,1,0:T(8,128)(2,1)}, u32[]{:S(2)}, u32[]{:S(2)}) collective-permute-start(bf16[3,192,1536]{2,1,0:T(8,128)(2,1)} %get-tuple-element.144), channel_id=1, source_target_pairs={{0,8},{8,16},{16,24},{24,0},{1,9},{9,17},{17,25},{25,1},{2,10},{10... | collective-permute-start | bytes 5308424 | tf_op jit(solution)/shard_map/ppermute | solution.py:1783
  1298.1 59.1 %copy-start.7 = (f32[32,1536]{1,0:T(8,128)S(1)}, f32[32,1536]{1,0:T(8,128)}, u32[]{:S(2)}) copy-start(f32[32,1536]{1,0:T(8,128)} %get-tuple-element.127) | copy-start | bytes 589828
  1358.9 120.3 %copy-start.8 = (f32[34,48]{1,0:T(8,128)S(1)}, f32[34,48]{1,0:T(8,128)}, u32[]{:S(2)}) copy-start(f32[34,48]{1,0:T(8,128)} %reshape.121) | copy-start | bytes 19588
  1484.3 1.2 copy-start.4

commit v3 on v2

--- a/solution.py
+++ b/solution.py
@@ -151,6 +151,140 @@
 
 def exchange_sems(chunks, count):
     return [pltpu.SemaphoreType.DMA((chunks, max(count - 1, 1))) for _ in range(2)]
+
+
+class LineGather:
+    def __init__(self, rows, own, tokens, part, sems):
+        self.rows = rows
+        self.own = own
+        self.tokens = tokens
+        self.part = part
+        self.own_send, self.pass_send, self.recv = sems
+
+    @staticmethod
+    def sems(chunks, count):
+        return [
+            pltpu.SemaphoreType.DMA((chunks, 2)),
+            pltpu.SemaphoreType.DMA((chunks, count)),
+            pltpu.SemaphoreType.DMA((chunks, count)),
+        ]
+
+    def copy(self, source, origin, index, chunk, sem, place):
+        return pltpu.make_async_remote_copy(
+            src_ref=source,
+            dst_ref=self.tokens.at[self.part(origin), chunk],
+            send_sem=sem,
+            recv_sem=self.recv.at[index, origin],
+            device_id=self.rows.device_of(place),
+            device_id_type=pl.DeviceIdType.MESH,
+        )
+
+    def own_copies(self, index, chunk):
+        me, last = self.rows.place, self.rows.count - 1
+        for way, (there, place) in enumerate(((me < last, me + 1), (me > 0, me - 1))):
+            yield there, self.copy(
+                self.own.at[:, chunk], me, index, chunk, self.own_send.at[index, way], place
+            )
+
+    def passed(self, index, chunk):
+        me, last = self.rows.place, self.rows.count - 1
+        for distance in range(1, self.rows.count):
+            for arrives, origin, goes_on, place in (
+                (me >= distance, me - distance, me < last, me + 1),
+                (me + distance <= last, me + distance, me > 0, me - 1),
+            ):
+                yield arrives, goes_on, self.copy(
+                    self.tokens.at[self.part(origin), chunk],
+                    origin,
+                    index,
+                    chunk,
+                    self.pass_send.at[index, origin],
+                    place,
+                )
+
+    def start_own(self, index, chunk):
+        for there, copy in self.own_copies(index, chunk):
+            pl.when(there)(copy.start)
+
+    def arrive(self, index, chunk):
+        for arrives, goes_on, copy in self.passed(index, chunk):
+
+            @pl.when(arrives)
+            def _():
+                copy.wait_recv()
+                pl.when(goes_on)(copy.start)
+
+    def wait_send(self, index, chunk):
+        for there, copy in self.own_copies(index, chunk):
+            pl.when(there)(copy.wait_send)
+        for arrives, goes_on, copy in self.passed(index, chunk):
+            pl.when(arrives & goes_on)(copy.wait_send)
+
+
+class LineSum:
+    def __init__(self, rows, tokens, part, landed, sems):
+        self.rows = rows
+        self.tokens = tokens
+        self.part = part
+        self.landed = landed
+        self.send, self.recv = sems
+
+    @staticmethod
+    def sems(chunks, count):
+        return [
+            pltpu.SemaphoreType.DMA((chunks, count)),
+            pltpu.SemaphoreType.DMA((chunks, count + 1)),
+        ]
+
+    def copy(self, target, slot, index, chunk, place):
+        return pltpu.make_async_remote_copy(
+            src_ref=self.tokens.at[self.part(target), chunk],
+            dst_ref=self.landed.at[slot, :, chunk],
+            send_sem=self.send.at[index, target],
+            recv_sem=self.recv.at[index, slot],
+            device_id=self.rows.device_of(place),
+            device_id_type=pl.DeviceIdType.MESH,
+        )
+
+    def passed(self, index, chunk):
+        me, last = self.rows.place, self.rows.count - 1
+        for number in range(self.rows.count):
+            for goes, arrives, slot, target, place in (
+                (me > number, me < last, number, number, me - 1),
+                (me < last - number, me > 0, last - number + 1, last - number, me + 1),
+            ):
+                yield goes, arrives, slot, target, self.copy(target, slot, index, chunk, place)
+
+    def pass_on(self, index, chunk):
+        for goes, arrives, slot, target, copy in self.passed(index, chunk):
+
+            @pl.when(goes)
+            def _():
+                @pl.when(arrives)
+                def _():
+                    copy.wait_recv()
+                    total = self.tokens[self.part(target), chunk].astype(jnp.float32)
+                    total = total + self.landed[slot, :, chunk].astype(jnp.float32)
+                    self.tokens[self.part(target), chunk] = total.astype(jnp.bfloat16)
+
+                copy.start()
+
+    def is_middle(self):
+        return (self.rows.place > 0) & (self.rows.place < self.rows.count - 1)
+
+    def total(self, index, chunk, out):
+        me, last = self.rows.place, self.rows.count - 1
+        out[:, chunk] = self.tokens[self.part(me), chunk].astype(jnp.float32)
+        for arrives, slot in ((me < last, me), (me > 0, me + 1)):
+
+            @pl.when(arrives)
+            def _():
+                self.copy(me, slot, index, chunk, me).wait_recv()
+                out[:, chunk] += self.landed[slot, :, chunk].astype(jnp.float32)
+
+    def wait_send(self, index, chunk):
+        for goes, _, _, _, copy in self.passed(index, chunk):
+            pl.when(goes)(copy.wait_send)
 
 
 def iota(shape, axis):
@@ -207,6 +341,15 @@
             member[tokens, :] = turned
 
 
+def far_first(rows):
+    for distance in range(rows.count - 1, 0, -1):
+        for there, place in (
+            (rows.place + distance < rows.count, rows.place + distance),
+            (rows.place >= distance, rows.place - distance),
+        ):
+            yield there, place
+
+
 class WeightMove:
     def __init__(self, rows, copies, layer, shards, target, sems):
         self.rows = rows
@@ -240,8 +383,13 @@
         )
 
     def start(self):
-        for step in range(1, self.rows.count):
-            self.out(step).start()
+        for there, place in far_first(self.rows):
+            step = lax.rem(place - self.rows.place + self.rows.count, self.rows.count)
+
+            @pl.when(there)
+            def _():
+                self.out(step).start()
+
         self.own().start()
 
     def wait_recv(self):
@@ -271,15 +419,19 @@
 no_cost = pl.CostEstimate(flops=0, bytes_accessed=0, transcendentals=0)
 
 
-def moe_forward_kernel(dims, row_count, layer, moving, gather_dims, *refs):
+def moe_forward_kernel(dims, row_count, layer, moving, gather_dims, closing, *refs):
     group_rows, col_count, copies, token_rows, slot_rows, chunks, width = dims
     own_ref, routes_ref, router_ref = refs[:3]
     weight_in = refs[3:6]
     refs = refs[6:]
     next_blocks = refs[: 2 if gather_dims else 0]
     refs = refs[len(next_blocks) :]
+    closing_in = refs[: 1 if closing else 0]
+    refs = refs[len(closing_in) :]
     sum_ref, gates_ref, slots_out, returned_out = refs[:4]
     refs = refs[4:]
+    closing_out = refs[: len(closing_in)]
+    refs = refs[len(closing_in) :]
     moved_out = refs[: len(moving)]
     refs = refs[len(moving) :]
     next_full = refs[: len(next_blocks)]
@@ -289,6 +441,10 @@
         count = len(DenseGather.sems(gather_dims, 2))
         dense = DenseGather(gather_dims, next_blocks, next_full, refs[-count:])
         refs = refs[:-count]
+    closing_sems = ()
+    if closing:
+        closing_sems = refs[-4:]
+        refs = refs[:-4]
     move_sems = refs[len(refs) - 3 * len(moving) :]
     refs = refs[: len(refs) - 3 * len(moving)]
     (
@@ -306,7 +462,8 @@
         act,
         returned,
         landed,
-        row_send,
+        own_send,
+        pass_send,
         row_recv,
         there_send,
         there_recv,
@@ -327,13 +484,7 @@
     def slot_part(place):
         return pl.ds(pl.multiple_of(place * slot_rows, slot_rows), slot_rows)
 
-    gather = Exchange(
-        rows,
-        row_send,
-        row_recv,
-        lambda place, chunk: own_ref.at[:, chunk],
-        lambda place, step, chunk: tokens.at[token_part(place), chunk],
-    )
+    gather = LineGather(rows, own_ref, tokens, token_part, (own_send, pass_send, row_recv))
     there = Exchange(
         cols,
         there_send,
@@ -348,13 +499,13 @@
         lambda place, chunk: send.at[slot_part(place), chunk],
         lambda place, step, chunk: returned.at[slot_part(place), chunk],
     )
-    home = Exchange(
-        rows,
-        home_send,
-        home_recv,
-        lambda place, chunk: tokens.at[token_part(place), chunk],
-        lambda place, step, chunk: landed.at[step - 1, :, chunk],
-    )
+    home = LineSum(rows, tokens, token_part, landed, (home_send, home_recv))
+    ahead = None
+    if closing:
+        ahead = LineGather(rows, *closing_in, *closing_out, token_part, closing_sems[:3])
+        ahead_own = pltpu.make_async_copy(
+            closing_in[0], closing_out[0].at[token_part(rows.place), :], closing_sems[3]
+        )
     weights = (gate, up, down)
     moves = {
         kind: WeightMove(
@@ -389,28 +540,35 @@
         return weights[kind][:, :, chunk].reshape(-1, width)
 
     greet((all_rows(row_count), cols))
-    over_chunks(chunks, width, gather.start)
-    for kind in moving:
-        moves[kind].start()
-    if dense:
-        for kind in dense.kinds:
-            dense.start(kind)
+    for index in range(min(2, chunks)):
+        gather.start_own(index, pl.ds(index * width, width))
     for copy in loads.values():
         copy.start()
     tokens[token_part(rows.place), :] = own_ref[...]
     build_places(dims, rows, routes_ref, place, place_t, member)
 
     def dispatch(index, chunk):
-        gather.wait_recv(index, chunk)
+        gather.arrive(index, chunk)
+
+        @pl.when(index + 2 < chunks)
+        def _():
+            later = pl.ds(pl.multiple_of((index + 2) * width, width), width)
+            gather.start_own(index + 2, later)
+
 
         def rows_of(part):
             send[part, chunk] = dot_nn(place[part, :], tokens[:, chunk]).astype(jnp.bfloat16)
 
-        over_blocks(all_slots, slot_step, rows_of)
+        over_blocks(all_slots, all_slots, rows_of)
         there.start(index, chunk)
         slots[slot_part(cols.place), chunk] = send[slot_part(cols.place), chunk]
 
     over_chunks(chunks, width, dispatch)
+    if dense:
+        for kind in dense.kinds:
+            dense.start(kind)
+    for kind in moving:
+        moves[kind].start()
 
     def gating(part):
         chosen = member[part, :] >= 0
@@ -440,7 +598,7 @@
             def _():
                 target[part, :] += value
 
-        over_blocks(all_slots, slot_step, rows_of)
+        over_blocks(all_slots, all_slots, rows_of)
 
     weight_ready(0)
     over_chunks(chunks, width, functools.partial(project, 0, gate_val, True))
@@ -454,7 +612,13 @@
         act[part, :] = (value * jax.nn.sigmoid(value) * up_val[part, :]).astype(jnp.bfloat16)
 
     over_blocks(all_slots, slot_step, activate)
+    if dense:
+        for kind in dense.kinds:
+            dense.pass_rows(kind)
     weight_ready(2)
+    if ahead:
+        ahead_own.start()
+        over_chunks(chunks, width, ahead.start_own)
 
     def give_back(index, chunk):
         there.wait_send(index, chunk)
@@ -462,12 +626,14 @@
         def rows_of(part):
             send[part, chunk] = dot_nn(act[part, :], weight(2, chunk)).astype(jnp.bfloat16)
 
-        over_blocks(all_slots, slot_step, rows_of)
+        over_blocks(all_slots, all_slots, rows_of)
         back.start(index, chunk)
         returned[slot_part(cols.place), chunk] = send[slot_part(cols.place), chunk]
 
     over_chunks(chunks, width, give_back)
 
+    over_chunks(chunks, width, gather.wait_send)
+
     def combine(index, chunk):
         back.wait_recv(index, chunk)
 
@@ -475,48 +641,70 @@
             tokens[part, chunk] = dot_nn(place_t[part, :], returned[:, chunk]).astype(jnp.bfloat16)
 
         over_blocks(all_tokens, token_rows, rows_of)
-        home.start(index, chunk)
+        if ahead:
+            ahead.arrive(index, chunk)
+            return
+        pl.when(~home.is_middle())(functools.partial(home.pass_on, index, chunk))
+
+        @pl.when(home.is_middle() & (index > 0))
+        def _():
+            before = pl.ds(pl.multiple_of((index - 1) * width, width), width)
+            home.pass_on(index - 1, before)
 
     over_chunks(chunks, width, combine)
+    if ahead:
+        keep_mixed = pltpu.make_async_copy(tokens, sum_ref, local_sem.at[5])
+        keep_mixed.start()
+    else:
+        last_chunk = pl.ds((chunks - 1) * width, width)
+        pl.when(home.is_middle())(functools.partial(home.pass_on, chunks - 1, last_chunk))
     keep_returned = pltpu.make_async_copy(returned, returned_out, local_sem.at[1])
     keep_returned.start()
     if dense:
         for kind in dense.kinds:
-            dense.pass_rows(kind)
+            dense.pass_pairs(kind)
 
     def finish(index, chunk):
-        home.wait_recv(index, chunk)
-        total = tokens[token_part(rows.place), chunk].astype(jnp.float32)
-        for step in range(1, group_rows):
-            total = total + landed[step - 1, :, chunk].astype(jnp.float32)
-        sum_ref[:, chunk] = total
-
-    over_chunks(chunks, width, finish)
+        home.total(index, chunk, sum_ref)
+
+    if not ahead:
+        over_chunks(chunks, width, finish)
 
     def drain(index, chunk):
-        gather.wait_send(index, chunk)
         back.wait_send(index, chunk)
-        home.wait_send(index, chunk)
+        (ahead or home).wait_send(index, chunk)
 
     over_chunks(chunks, width, drain)
     if dense:
-        for kind in dense.kinds:
-            dense.pass_pairs(kind)
         for kind in dense.kinds:
             dense.finish(kind)
     for kind in moving:
         moves[kind].wait_send()
+    if ahead:
+        ahead_own.wait()
+        keep_mixed.wait()
     keep_slots.wait()
     keep_returned.wait()
     for keep in keeps:
         keep.wait()
 
 
-def moe_backward_kernel(dims, *refs):
+def moe_backward_kernel(dims, opening, *refs):
     group_rows, col_count, copies, token_rows, slot_rows, chunks, width = dims
     own_ref, routes_ref, router_ref, gates_ref, normed_ref, slots_in, returned_in = refs[:7]
     weight_in = refs[7:10]
-    sum_ref, router_grad_ref, grads_out = refs[10:13]
+    refs = refs[10:]
+    opening_in = refs[: 1 if opening else 0]
+    refs = refs[len(opening_in) :]
+    block_count, slice_width = weight_in[0].shape[:2]
+    sum_ref, router_grad_ref, *grads_out = refs[: 2 + block_count]
+    refs = refs[2 + block_count :]
+    opening_out = refs[: len(opening_in)]
+    refs = refs[len(opening_in) :]
+    opening_scratch = ()
+    if opening:
+        opening_scratch = refs[-3:]
+        refs = refs[:-3]
     (
         place,
         place_t,
@@ -541,7 +729,8 @@
         landed,
         pair_send,
         pair_landed,
-        row_send,
+        own_send,
+        pass_send,
         row_recv,
         there_send,
         there_recv,
@@ -552,11 +741,10 @@
         pair_send_sem,
         pair_recv_sem,
         local_sem,
-    ) = refs[13:]
+    ) = refs
     all_tokens = group_rows * token_rows
     all_slots = col_count * slot_rows
     slot_step = split_rows(all_slots, 320)
-    block_count, slice_width = weight_in[0].shape[:2]
     rows, cols = expert_peers(col_count, copies, group_rows)
 
     def token_part(place):
@@ -565,13 +753,7 @@
     def slot_part(place):
         return pl.ds(pl.multiple_of(place * slot_rows, slot_rows), slot_rows)
 
-    gather = Exchange(
-        rows,
-        row_send,
-        row_recv,
-        lambda place, chunk: own_ref.at[:, chunk],
-        lambda place, step, chunk: tokens.at[token_part(place), chunk],
-    )
+    gather = LineGather(rows, own_ref, tokens, token_part, (own_send, pass_send, row_recv))
     there = Exchange(
         cols,
         there_send,
@@ -586,13 +768,10 @@
         lambda place, chunk: send.at[slot_part(place), chunk],
         lambda place, step, chunk: returned.at[slot_part(place), chunk],
     )
-    home = Exchange(
-        rows,
-        home_send,
-        home_recv,
-        lambda place, chunk: tokens.at[token_part(place), chunk],
-        lambda place, step, chunk: landed.at[step - 1, :, chunk],
-    )
+    home = LineSum(rows, tokens, token_part, landed, (home_send, home_recv))
+    before = None
+    if opening:
+        before = LineSum(rows, tokens, token_part, opening_scratch[0], opening_scratch[1:])
     pair = Exchange(
         rows,
         pair_send_sem,
@@ -600,8 +779,15 @@
         lambda place, chunk: pair_send.at[token_part(place), :],
         lambda place, step, chunk: pair_landed.at[step - 1],
     )
-    greet((rows, cols))
-    over_chunks(chunks, width, gather.start)
+    greet((all_rows(block_count), cols))
+    if before:
+        load_tokens = pltpu.make_async_copy(own_ref, tokens, local_sem.at[7])
+        load_tokens.start()
+    else:
+        for index in range(min(2, chunks)):
+            gather.start_own(index, pl.ds(index * width, width))
+    load_returned = pltpu.make_async_copy(returned_in, returned, local_sem.at[1])
+    load_returned.start()
     load_slots = pltpu.make_async_copy(slots_in, slots, local_sem.at[0])
     load_slots.start()
     weights = (gate, up, down)
@@ -615,13 +801,9 @@
     def weight_part(kind, chunk):
         return weights[kind][:, :, chunk].reshape(block_count * slice_width, width)
 
-    load_returned = pltpu.make_async_copy(returned_in, returned, local_sem.at[1])
-    load_returned.start()
-    tokens[token_part(rows.place), :] = own_ref[...]
+    if not before:
+        tokens[token_part(rows.place), :] = own_ref[...]
     build_places(dims, rows, routes_ref, place, place_t, None)
-    load_slots.wait()
-    for copy in loads:
-        copy.wait()
 
     def recompute(part):
         gate_val = dot_nt(slots[part, :], gate[...].reshape(-1, gate.shape[2]))
@@ -633,17 +815,36 @@
         slope[part, :] = (up_val * sigmoid * (1.0 + gate_val * (1.0 - sigmoid))).astype(
             jnp.bfloat16
         )
+
+    def slot_gates(part):
         picked = dot_nn(place[part, :], gates_ref[...].astype(jnp.bfloat16))
         block = iota(picked.shape, 1)
         slot = iota(picked.shape, 0) + part.start
         in_block = (slot >= block * slot_rows) & (slot < (block + 1) * slot_rows)
         weight[part, :] = jnp.sum(jnp.where(in_block, picked, 0.0), axis=1, keepdims=True)
 
-    over_blocks(all_slots, slot_step, recompute)
+    def recompute_all():
+        load_slots.wait()
+        for copy in loads:
+            copy.wait()
+        over_blocks(all_slots, slot_step, recompute)
+
+    over_blocks(all_slots, slot_step, slot_gates)
+    if before:
+        load_tokens.wait()
+    else:
+        recompute_all()
     load_returned.wait()
 
     def dispatch(index, chunk):
-        gather.wait_recv(index, chunk)
+        if not before:
+            gather.arrive(index, chunk)
+
+            @pl.when(index + 2 < chunks)
+            def _():
+                later = pl.ds(pl.multiple_of((index + 2) * width, width), width)
+                gather.start_own(index + 2, later)
+
 
         def rows_of(part):
             grad = dot_nn(place[part, :], tokens[:, chunk])
@@ -660,7 +861,7 @@
             def _():
                 inner[part, :] += share
 
-        over_blocks(all_slots, slot_step, rows_of)
+        over_blocks(all_slots, all_slots, rows_of)
         there.start(index, chunk)
         received[slot_part(cols.place), chunk] = send[slot_part(cols.place), chunk]
 
@@ -673,10 +874,23 @@
         low = (spread - high.astype(jnp.float32)).astype(jnp.bfloat16)
         pair_send[part, :] = dot_nn(place_t[part, :], high) + dot_nn(place_t[part, :], low)
 
+    if before:
+        load_mixed = pltpu.make_async_copy(opening_in[0], tokens, local_sem.at[7])
+        load_mixed.start()
     over_blocks(all_tokens, token_rows, pairs)
     pair.start(0, None)
+    if before:
+        load_mixed.wait()
+
+        @pl.when(~before.is_middle())
+        def _():
+            over_chunks(chunks, width, before.pass_on)
+
+        recompute_all()
 
     def project(index, chunk):
+        if before:
+            pl.when(before.is_middle())(functools.partial(before.pass_on, index, chunk))
         there.wait_recv(index, chunk)
 
         def rows_of(part):
@@ -690,7 +904,7 @@
             def _():
                 grad_act[part, :] += grad
 
-        over_blocks(all_slots, slot_step, rows_of)
+        over_blocks(all_slots, all_slots, rows_of)
 
     over_chunks(chunks, width, project)
 
@@ -710,49 +924,54 @@
                 + dot_nn(grad_up[part, :], weight_part(1, chunk))
             ).astype(jnp.bfloat16)
 
-        over_blocks(all_slots, slot_step, rows_of)
+        over_blocks(all_slots, all_slots, rows_of)
         back.start(index, chunk)
 
     over_chunks(chunks, width, give_back)
 
+    returned[slot_part(cols.place), :] = send[slot_part(cols.place), :]
+    if before:
+        over_chunks(
+            chunks, width, lambda index, chunk: before.total(index, chunk, opening_out[0])
+        )
+        over_chunks(chunks, width, before.wait_send)
+
+    if not before:
+        over_chunks(chunks, width, gather.wait_send)
+
+    def combine(index, chunk):
+        back.wait_recv(index, chunk)
+
+        def rows_of(part):
+            tokens[part, chunk] = dot_nn(place_t[part, :], returned[:, chunk]).astype(jnp.bfloat16)
+
+        over_blocks(all_tokens, token_rows, rows_of)
+        pl.when(~home.is_middle())(functools.partial(home.pass_on, index, chunk))
+
+        @pl.when(home.is_middle() & (index > 0))
+        def _():
+            before = pl.ds(pl.multiple_of((index - 1) * width, width), width)
+            home.pass_on(index - 1, before)
+
+    over_chunks(chunks, width, combine)
+    last_chunk = pl.ds((chunks - 1) * width, width)
+    pl.when(home.is_middle())(functools.partial(home.pass_on, chunks - 1, last_chunk))
     def keep(kind, index):
         return pltpu.make_async_copy(
-            staged.at[lax.rem(index, 2)],
-            grads_out.at[index, kind],
-            local_sem.at[2 + lax.rem(index, 2)],
-        )
-
-    for kind, (left, right) in enumerate(
-        ((grad_gate, slots), (grad_up, slots), (act, received))
-    ):
+            staged.at[index % 2], grads_out[index].at[kind], local_sem.at[2 + index % 2]
+        )
+
+    for kind, (left, right) in enumerate(((grad_gate, slots), (grad_up, slots), (act, received))):
         turned[...] = left[...].T
-
-        def one_slice(index, carry, kind=kind, right=right):
-            @pl.when(index >= 2)
-            def _():
+        for index in range(block_count):
+            if index >= 2:
                 keep(kind, index - 2).wait()
-
-            part = pl.ds(pl.multiple_of(index * slice_width, slice_width), slice_width)
-            staged[lax.rem(index, 2)] = dot_nn(turned[part, :], right[...]).astype(jnp.bfloat16)
+            part = slice(index * slice_width, (index + 1) * slice_width)
+            staged[index % 2] = dot_nn(turned[part, :], right[...]).astype(jnp.bfloat16)
             keep(kind, index).start()
-            return carry
-
-        lax.fori_loop(0, block_count, one_slice, 0)
         for index in range(max(block_count - 2, 0), block_count):
             keep(kind, index).wait()
 
-    returned[slot_part(cols.place), :] = send[slot_part(cols.place), :]
-
-    def combine(index, chunk):
-        back.wait_recv(index, chunk)
-
-        def rows_of(part):
-            tokens[part, chunk] = dot_nn(place_t[part, :], returned[:, chunk]).astype(jnp.bfloat16)
-
-        over_blocks(all_tokens, token_rows, rows_of)
-        home.start(index, chunk)
-
-    over_chunks(chunks, width, combine)
     pair.wait_recv(0, None)
     grad_pair = pair_send[token_part(rows.place), :]
     for ahead in range(1, group_rows):
@@ -765,16 +984,12 @@
     router_grad_ref[...] = dot_nn(grad_logits.astype(jnp.float32).T.astype(jnp.bfloat16), normed_ref[...])
 
     def finish(index, chunk):
-        home.wait_recv(index, chunk)
-        total = tokens[token_part(rows.place), chunk].astype(jnp.float32)
-        for step in range(1, group_rows):
-            total = total + landed[step - 1, :, chunk].astype(jnp.float32)
-        sum_ref[:, chunk] = total + dot_nn(grad_logits, router_ref[:, chunk])
+        home.total(index, chunk, sum_ref)
+        sum_ref[:, chunk] += dot_nn(grad_logits, router_ref[:, chunk])
 
     over_chunks(chunks, width, finish)
 
     def drain(index, chunk):
-        gather.wait_send(index, chunk)
         back.wait_send(index, chunk)
         home.wait_send(index, chunk)
 
@@ -782,7 +997,9 @@
     pair.wait_send(0, None)
 
 
-def moe_forward(dims, row_count, layer, own, routes, router, weights, moving, next_blocks):
+def moe_forward(
+    dims, row_count, layer, own, routes, router, weights, moving, next_blocks, closing
+):
     group_rows, col_count, copies, token_rows, slot_rows, chunks, width = dims
     all_tokens, all_slots = group_rows * token_rows, col_count * slot_rows
     model_width = own.shape[1]
@@ -792,23 +1009,26 @@
     dense_sems = DenseGather.sems(gather_dims, 2) if next_blocks else []
     vmem = pl.BlockSpec(memory_space=pltpu.VMEM)
     outside = pl.BlockSpec(memory_space=pl.ANY)
+    every_row = jax.ShapeDtypeStruct((all_tokens, model_width), jnp.bfloat16)
     slot_array = pltpu.VMEM((all_slots, model_width), jnp.bfloat16)
     hidden_wide = pltpu.VMEM((all_slots, hidden), jnp.float32)
     weight_array = pltpu.VMEM((row_count, slice_width, model_width), jnp.bfloat16)
     return pl.pallas_call(
         functools.partial(
-            moe_forward_kernel, dims, row_count, layer, moving, gather_dims
+            moe_forward_kernel, dims, row_count, layer, moving, gather_dims, bool(closing)
         ),
         out_shape=(
-            jax.ShapeDtypeStruct((token_rows, model_width), jnp.float32),
+            every_row if closing else jax.ShapeDtypeStruct((token_rows, model_width), jnp.float32),
             jax.ShapeDtypeStruct((all_tokens, E), jnp.float32),
             jax.ShapeDtypeStruct((all_slots, model_width), jnp.bfloat16),
             jax.ShapeDtypeStruct((all_slots, model_width), jnp.bfloat16),
+            *([every_row] * len(closing)),
             *(moved_shape(row_count, weights[kind]) for kind in moving),
             *(gathered_shapes(gather_dims, next_blocks) if next_blocks else ()),
         ),
-        in_specs=[vmem] * 3 + [outside] * (3 + len(next_blocks)),
-        out_specs=(vmem, vmem) + (outside,) * (2 + len(moving) + len(next_blocks)),
+        in_specs=[vmem] * 3 + [outside] * (3 + len(next_blocks) + len(closing)),
+        out_specs=(outside if closing else vmem, vmem)
+        + (outside,) * (2 + len(closing) + len(moving) + len(next_blocks)),
         scratch_shapes=[
             pltpu.VMEM((all_slots, all_tokens), jnp.bfloat16),
             pltpu.VMEM((all_tokens, all_slots), jnp.bfloat16),
@@ -823,13 +1043,14 @@
             hidden_wide,
             pltpu.VMEM((all_slots, hidden), jnp.bfloat16),
             slot_array,
-            pltpu.VMEM((max(group_rows - 1, 1), token_rows, model_width), jnp.bfloat16),
-            *exchange_sems(chunks, group_rows),
+            pltpu.VMEM((group_rows + 1, token_rows, model_width), jnp.bfloat16),
+            *LineGather.sems(chunks, group_rows),
             *exchange_sems(chunks, col_count),
             *exchange_sems(chunks, col_count),
-            *exchange_sems(chunks, group_rows),
-            pltpu.SemaphoreType.DMA((5,)),
+            *LineSum.sems(chunks, group_rows),
+            pltpu.SemaphoreType.DMA((6,)),
             *(WeightMove.sems(row_count) * len(moving)),
+            *((*LineGather.sems(chunks, group_rows), pltpu.SemaphoreType.DMA) if closing else ()),
             *dense_sems,
         ],
         compiler_params=pltpu.CompilerParams(
@@ -837,14 +1058,16 @@
         ),
         cost_estimate=long_cost,
         name="moe_forward",
-    )(own, routes, router, *weights, *next_blocks)
-
-
-def moe_backward(dims, own, routes, router, gates, normed, slots, returned, weights):
+    )(own, routes, router, *weights, *next_blocks, *closing)
+
+
+def moe_backward(dims, own, routes, router, gates, normed, slots, returned, weights, opening):
     group_rows, col_count, copies, token_rows, slot_rows, chunks, width = dims
     all_tokens, all_slots = group_rows * token_rows, col_count * slot_rows
     model_width = own.shape[1]
+    opened = len(opening)
     block_count, slice_width = weights[0].shape[:2]
+    grads = jax.ShapeDtypeStruct((3, slice_width, model_width), jnp.bfloat16)
     hidden = block_count * slice_width
     vmem = pl.BlockSpec(memory_space=pltpu.VMEM)
     outside = pl.BlockSpec(memory_space=pl.ANY)
@@ -852,14 +1075,17 @@
     hidden_narrow = pltpu.VMEM((all_slots, hidden), jnp.bfloat16)
     weight_array = pltpu.VMEM((block_count, slice_width, model_width), jnp.bfloat16)
     return pl.pallas_call(
-        functools.partial(moe_backward_kernel, dims),
+        functools.partial(moe_backward_kernel, dims, bool(opening)),
         out_shape=(
             jax.ShapeDtypeStruct((token_rows, model_width), jnp.float32),
             jax.ShapeDtypeStruct((E, model_width), jnp.float32),
-            jax.ShapeDtypeStruct((block_count, 3, slice_width, model_width), jnp.bfloat16),
+            *([grads] * block_count),
+            *([jax.ShapeDtypeStruct((token_rows, model_width), jnp.float32)] * opened),
         ),
-        in_specs=[vmem] * 5 + [outside] * 5,
-        out_specs=(vmem, vmem, outside),
+        in_specs=[outside if opening else vmem]
+        + [vmem] * 4
+        + [outside] * (5 + opened),
+        out_specs=(vmem, vmem) + (outside,) * block_count + (vmem,) * opened,
         scratch_shapes=[
             pltpu.VMEM((all_slots, all_tokens), jnp.bfloat16),
             pltpu.VMEM((all_tokens, all_slots), jnp.bfloat16),
@@ -881,22 +1107,30 @@
             slot_array,
             pltpu.VMEM((hidden, all_slots), jnp.bfloat16),
             pltpu.VMEM((2, slice_width, model_width), jnp.bfloat16),
-            pltpu.VMEM((max(group_rows - 1, 1), token_rows, model_width), jnp.bfloat16),
+            pltpu.VMEM((group_rows + 1, token_rows, model_width), jnp.bfloat16),
             pltpu.VMEM((all_tokens, 128), jnp.float32),
             pltpu.VMEM((max(group_rows - 1, 1), token_rows, 128), jnp.float32),
-            *exchange_sems(chunks, group_rows),
+            *LineGather.sems(chunks, group_rows),
             *exchange_sems(chunks, col_count),
             *exchange_sems(chunks, col_count),
-            *exchange_sems(chunks, group_rows),
+            *LineSum.sems(chunks, group_rows),
             *exchange_sems(1, group_rows),
-            pltpu.SemaphoreType.DMA((7,)),
+            pltpu.SemaphoreType.DMA((8,)),
+            *(
+                (
+                    pltpu.VMEM((group_rows + 1, token_rows, model_width), jnp.bfloat16),
+                    *LineSum.sems(chunks, group_rows),
+                )
+                if opening
+                else ()
+            ),
         ],
         compiler_params=pltpu.CompilerParams(
-            collective_id=2, has_side_effects=True, vmem_limit_bytes=vmem_most
+            collective_id=9 if opening else 2, has_side_effects=True, vmem_limit_bytes=vmem_most
         ),
         cost_estimate=long_cost,
         name="moe_backward",
-    )(own, routes, router, gates, normed, slots, returned, *weights)
+    )(own, routes, router, gates, normed, slots, returned, *weights, *opening)
 
 
 def col_pairs():
@@ -1404,6 +1638,18 @@
     return values * cosine + pltpu.roll(values, HEAD_SIZE // 2, 1) * sine
 
 
+def head_lanes(head):
+    return slice(2 * head * HEAD_SIZE, 2 * (head + 1) * HEAD_SIZE)
+
+
+def key_lanes(head):
+    return slice(2 * head * HEAD_SIZE, (2 * head + 1) * HEAD_SIZE)
+
+
+def value_lanes(head):
+    return slice((2 * head + 1) * HEAD_SIZE, 2 * (head + 1) * HEAD_SIZE)
+
+
 def seen_keys(token_rows):
     position = lax.axis_index("col") * token_rows + iota((1, token_rows), 1)
     return (position // BLOCK + 1) * BLOCK
@@ -1448,8 +1694,8 @@
         cols,
         send_sem,
         recv_sem,
-        lambda place, chunk: kv_all.at[part(cols.place), :],
-        lambda place, step, chunk: kv_all.at[part(place), :],
+        lambda place, chunk: kv_all.at[part(cols.place), chunk],
+        lambda place, step, chunk: kv_all.at[part(place), chunk],
     )
     move = WeightMove(all_rows(row_count), copies, layer, shards_ref, moved, move_sems)
     greet((cols, move.rows))
@@ -1458,44 +1704,46 @@
     inverse = lax.rsqrt(jnp.mean(x * x, axis=-1, keepdims=True) + eps_norm)
     normed_ref[...] = (x * inverse * gain_attn_ref[...]).astype(jnp.bfloat16)
     proj[...] = pieces_nt(normed_ref[...], qkv_ref)
+    own = part(cols.place)
     for head in range(KEY_VALUE_HEADS):
-        lanes = slice(head * HEAD_SIZE, (head + 1) * HEAD_SIZE)
         start = QUERY_FEATURES + head * HEAD_SIZE
         turned = rotate(proj[:, start : start + HEAD_SIZE], cosine_ref[...], sine_ref[...])
-        kv_all[part(cols.place), lanes] = turned.astype(jnp.bfloat16)
-    kv_all[part(cols.place), kv_width:] = proj[:, QUERY_FEATURES + kv_width :].astype(jnp.bfloat16)
-    share.start(0, None)
+        kv_all[own, key_lanes(head)] = turned.astype(jnp.bfloat16)
+        start = start + kv_width
+        kv_all[own, value_lanes(head)] = proj[:, start : start + HEAD_SIZE].astype(jnp.bfloat16)
+        share.start(head, head_lanes(head))
     for head in range(QUERY_HEADS):
         lanes = slice(head * HEAD_SIZE, (head + 1) * HEAD_SIZE)
         q_ref[:, lanes] = rotate(proj[:, lanes], cosine_ref[...], sine_ref[...]).astype(
             jnp.bfloat16
         )
-    share.wait_recv(0, None)
+    seen = seen_keys(token_rows)
+    for kv_head in range(KEY_VALUE_HEADS):
+        share.wait_recv(kv_head, head_lanes(kv_head))
+        value_t[...] = kv_all[:, value_lanes(kv_head)].T
+
+        def head_step(step, carry, kv_head=kv_head):
+            index = kv_head * group + step
+            lanes = pl.ds(pl.multiple_of(index * HEAD_SIZE, HEAD_SIZE), HEAD_SIZE)
+            scores = dot_nt(kv_all[:, key_lanes(kv_head)], q_ref[:, lanes]) * score_scale
+            scores = jnp.where(iota(scores.shape, 0) < seen, scores, masked_score)
+            peak = jnp.max(scores, axis=0, keepdims=True)
+            exponent = jnp.exp(scores - peak)
+            total = jnp.sum(exponent, axis=0, keepdims=True)
+            attended = dot_nn(value_t[...], exponent.astype(jnp.bfloat16)) / total
+            attended_ref[:, lanes] = attended.T.astype(jnp.bfloat16)
+            lse_ref[index] = peak + jnp.log(total)
+            return carry
+
+        lax.fori_loop(0, group, head_step, 0)
     keep = pltpu.make_async_copy(kv_all, kv_out, local_sem)
     keep.start()
-    value_t[...] = kv_all[:, kv_width:].T
-    seen = seen_keys(token_rows)
-
-    def head_step(index, carry):
-        kv_head = index // group
-        lanes = pl.ds(pl.multiple_of(index * HEAD_SIZE, HEAD_SIZE), HEAD_SIZE)
-        kv_lanes = pl.ds(pl.multiple_of(kv_head * HEAD_SIZE, HEAD_SIZE), HEAD_SIZE)
-        scores = dot_nt(kv_all[:, kv_lanes], q_ref[:, lanes]) * score_scale
-        scores = jnp.where(iota(scores.shape, 0) < seen, scores, masked_score)
-        peak = jnp.max(scores, axis=0, keepdims=True)
-        exponent = jnp.exp(scores - peak)
-        total = jnp.sum(exponent, axis=0, keepdims=True)
-        attended = dot_nn(value_t[kv_lanes, :], exponent.astype(jnp.bfloat16)) / total
-        attended_ref[:, lanes] = attended.T.astype(jnp.bfloat16)
-        lse_ref[index] = peak + jnp.log(total)
-        return carry
-
-    lax.fori_loop(0, QUERY_HEADS, head_step, 0)
     mid = x_ref[...] + pieces_nt(attended_ref[...], out_w_ref)
     mid_ref[...] = mid
     inverse = lax.rsqrt(jnp.mean(mid * mid, axis=-1, keepdims=True) + eps_norm)
     normed_moe_ref[...] = (mid * inverse * gain_moe_ref[...]).astype(jnp.bfloat16)
-    share.wait_send(0, None)
+    for head in range(KEY_VALUE_HEADS):
+        share.wait_send(head, head_lanes(head))
     keep.wait()
     move.wait_recv()
     move.wait_send()
@@ -1540,9 +1788,9 @@
         out_specs=(vmem, vmem, vmem, outside, vmem, vmem, vmem, outside),
         scratch_shapes=[
             pltpu.VMEM((seq_rows, 2 * kv_width), jnp.bfloat16),
-            pltpu.VMEM((kv_width, seq_rows), jnp.bfloat16),
+            pltpu.VMEM((HEAD_SIZE, seq_rows), jnp.bfloat16),
             pltpu.VMEM((token_rows, QUERY_FEATURES + 2 * kv_width), jnp.float32),
-            *exchange_sems(1, col_count),
+            *exchange_sems(KEY_VALUE_HEADS, col_count),
             pltpu.SemaphoreType.DMA,
             *WeightMove.sems(row_count),
         ],
@@ -1605,9 +1853,10 @@
         cols,
         send_sem,
         recv_sem,
-        lambda place, chunk: grad_kv.at[part(place), :],
-        lambda place, step, chunk: landed.at[step - 1],
+        lambda place, chunk: grad_kv.at[part(place), chunk],
+        lambda place, step, chunk: landed.at[step - 1, :, chunk],
     )
+    greet((cols,))
     grad, gain_sum = norm_backward(mid_ref[...], gain_moe_ref[...], grad_moe_ref[...])
     grad_gain_moe_ref[...] = gain_sum
     grad_x_ref[...] = incoming_ref[...] + grad
@@ -1616,56 +1865,54 @@
     for index in range(pieces):
         lanes = slice(index * size, (index + 1) * size)
         grad_attended[:, lanes] = dot_nn(grad_mid_ref[...], out_w_ref[index]).astype(jnp.bfloat16)
-    key_t[...] = kv_ref[:, :kv_width].T
     seen = seen_keys(token_rows)
     for kv_head in range(KEY_VALUE_HEADS):
-        kv_lanes = slice(kv_head * HEAD_SIZE, (kv_head + 1) * HEAD_SIZE)
-        value_lanes = slice(kv_width + kv_head * HEAD_SIZE, kv_width + (kv_head + 1) * HEAD_SIZE)
+        key_t[...] = kv_ref[:, key_lanes(kv_head)].T
         key_sum[...] = jnp.zeros_like(key_sum)
         value_sum[...] = jnp.zeros_like(value_sum)
 
-        def head_step(step, carry, kv_lanes=kv_lanes, value_lanes=value_lanes, kv_head=kv_head):
+        def head_step(step, carry, kv_head=kv_head):
             index = kv_head * group + step
             lanes = pl.ds(pl.multiple_of(index * HEAD_SIZE, HEAD_SIZE), HEAD_SIZE)
             query = q_ref[:, lanes]
             grad_out = grad_attended[:, lanes]
             product = grad_out.astype(jnp.float32) * attended_ref[:, lanes].astype(jnp.float32)
             inner = jnp.sum(product.T, axis=0, keepdims=True)
-            scores = dot_nt(kv_ref[:, kv_lanes], query) * score_scale
+            scores = dot_nt(kv_ref[:, key_lanes(kv_head)], query) * score_scale
             soft = jnp.where(
                 iota(scores.shape, 0) < seen, jnp.exp(scores - lse_ref[index]), 0.0
             )
-            grad_soft = dot_nt(kv_ref[:, value_lanes], grad_out)
+            grad_soft = dot_nt(kv_ref[:, value_lanes(kv_head)], grad_out)
             grad_scores = (soft * (grad_soft - inner)).astype(jnp.bfloat16)
             value_sum[...] += dot_nn(soft.astype(jnp.bfloat16), grad_out)
             key_sum[...] += dot_nn(grad_scores, query)
-            grad_q = (dot_nn(key_t[kv_lanes, :], grad_scores) * score_scale).T
+            grad_q = (dot_nn(key_t[...], grad_scores) * score_scale).T
             grad_q = rotate(grad_q, cosine_ref[...], -sine_ref[...])
             grad_proj_ref[:, lanes] = grad_q.astype(jnp.bfloat16)
             return carry
 
         lax.fori_loop(0, group, head_step, 0)
-        grad_kv[:, kv_lanes] = (key_sum[...] * score_scale).astype(jnp.bfloat16)
-        grad_kv[:, value_lanes] = value_sum[...].astype(jnp.bfloat16)
-    greet((cols,))
-    share.start(0, None)
-    share.wait_recv(0, None)
-    total = grad_kv[part(cols.place), :].astype(jnp.float32)
-    for step in range(1, col_count):
-        total = total + landed[step - 1].astype(jnp.float32)
+        grad_kv[:, key_lanes(kv_head)] = (key_sum[...] * score_scale).astype(jnp.bfloat16)
+        grad_kv[:, value_lanes(kv_head)] = value_sum[...].astype(jnp.bfloat16)
+        share.start(kv_head, head_lanes(kv_head))
     for head in range(KEY_VALUE_HEADS):
+        share.wait_recv(head, head_lanes(head))
+        total = grad_kv[part(cols.place), head_lanes(head)].astype(jnp.float32)
+        for step in range(1, col_count):
+            total = total + landed[step - 1, :, head_lanes(head)].astype(jnp.float32)
         start = QUERY_FEATURES + head * HEAD_SIZE
-        grad_key = total[:, head * HEAD_SIZE : (head + 1) * HEAD_SIZE]
-        grad_key = rotate(grad_key, cosine_ref[...], -sine_ref[...])
+        grad_key = rotate(total[:, :HEAD_SIZE], cosine_ref[...], -sine_ref[...])
         grad_proj_ref[:, start : start + HEAD_SIZE] = grad_key.astype(jnp.bfloat16)
-    grad_proj_ref[:, QUERY_FEATURES + kv_width :] = total[:, kv_width:].astype(jnp.bfloat16)
+        start = start + kv_width
+        grad_proj_ref[:, start : start + HEAD_SIZE] = total[:, HEAD_SIZE:].astype(jnp.bfloat16)
     pieces = qkv_ref.shape[0]
     grad_normed = [dot_nn(grad_proj_ref[...], qkv_ref[index]) for index in range(pieces)]
     grad_normed = jnp.concatenate(grad_normed, axis=1) if pieces > 1 else grad_normed[0]
     grad, gain_sum = norm_backward(x_ref[...], gain_attn_ref[...], grad_normed)
     grad_gain_attn_ref[...] = gain_sum
     grad_x_ref[...] += grad
-    share.wait_send(0, None)
+    for head in range(KEY_VALUE_HEADS):
+        share.wait_send(head, head_lanes(head))
 
 
 def attend_backward(
@@ -1703,12 +1950,12 @@
         out_specs=(vmem,) * 5,
         scratch_shapes=[
             pltpu.VMEM((token_rows, QUERY_FEATURES), jnp.bfloat16),
-            pltpu.VMEM((kv_width, seq_rows), jnp.bfloat16),
+            pltpu.VMEM((HEAD_SIZE, seq_rows), jnp.bfloat16),
             pltpu.VMEM((seq_rows, HEAD_SIZE), jnp.float32),
             pltpu.VMEM((seq_rows, HEAD_SIZE), jnp.float32),
             pltpu.VMEM((seq_rows, 2 * kv_width), jnp.bfloat16),
             pltpu.VMEM((max(col_count - 1, 1), token_rows, 2 * kv_width), jnp.bfloat16),
-            *exchange_sems(1, col_count),
+            *exchange_sems(KEY_VALUE_HEADS, col_count),
         ],
         compiler_params=pltpu.CompilerParams(
             collective_id=6, has_side_effects=True, vmem_limit_bytes=vmem_most
@@ -1774,27 +2021,16 @@
     cosine = jnp.concatenate([cosine, cosine], axis=1)
     sine = jnp.concatenate([-sine, sine], axis=1)
 
-    def behind(step):
-        return [(index, (index + step) % row_count) for index in range(row_count)]
-
     def move_grads(grads):
         blocks = [grads[0]]
         for step in range(1, row_count):
-            blocks.append(lax.ppermute(grads[step], "row", behind(row_count - step)))
+            pairs = [(index, (index - step) % row_count) for index in range(row_count)]
+            blocks.append(lax.ppermute(grads[step], "row", pairs))
         return tuple(blocks)
 
     def own_grads(blocks):
-        stacked = jnp.stack(blocks)
-        ordered = [
-            lax.dynamic_index_in_dim(
-                stacked, (index - row_index) % row_count, axis=0, keepdims=False
-            ).astype(wide_type)
-            for index in range(row_count)
-        ]
-        return [
-            functools.reduce(jnp.add, ordered[index * copies : (index + 1) * copies])
-            for index in range(local_experts)
-        ]
+        ordered = jnp.roll(jnp.stack(blocks), row_index, axis=0).astype(wide_type)
+        return jnp.sum(ordered.reshape(local_experts, copies, *blocks[0].shape), axis=1)
 
     def pieced(full):
         if full.shape[2] % 128 == 0:
@@ -1857,6 +2093,7 @@
         next_blocks = ()
         if layer_index + 1 < layer_count:
             next_blocks = (w_qkv[layer_index + 1].T, w_out[layer_index + 1].T)
+        closing = (cotangent,) if layer_index + 1 == layer_count else ()
         mixed, gates, slots, returned, *rest = moe_forward(
             dims,
             row_count,
@@ -1867,7 +2104,10 @@
             weights,
             moving,
             next_blocks,
-        )
+            closing,
+        )
+        if closing:
+            closing = (rest.pop(0), mixed)
         for kind, moved in zip(moving, rest):
             weights[kind] = moved
         experts.append(weights)
@@ -1877,7 +2117,8 @@
             (hidden, mid, normed, queries, key_value, attended, log_sums, normed_moe)
             + (gates, slots, returned)
         )
-        hidden = mid + mixed
+        if not closing:
+            hidden = mid + mixed
     incoming = cotangent.astype(wide_type)
     dense_results = [None] * layer_count
     small_results = [None] * layer_count
@@ -1885,9 +2126,9 @@
     for layer_index in reversed(range(layer_count)):
         x, mid, normed, queries, key_value, attended, log_sums, normed_moe = saved[layer_index][:8]
         gates, slots, returned = saved[layer_index][8:]
-        grad_moe, grad_router, expert_grads = moe_backward(
+        grad_moe, grad_router, *rest = moe_backward(
             dims,
-            incoming.astype(narrow_type),
+            closing[0] if closing else incoming.astype(narrow_type),
             routes_all[:, layer_index],
             routers[layer_index],
             gates,
@@ -1895,8 +2136,12 @@
             slots,
             returned,
             experts[layer_index],
-        )
-        expert_results[layer_index] = move_grads(expert_grads)
+            closing[1:],
+        )
+        if closing:
+            hidden = mid + rest.pop()
+            closing = ()
+        expert_results[layer_index] = move_grads(rest)
         incoming, grad_mid, grad_projected, grad_gain_attn, grad_gain_moe = attend_backward(
             col_count,
             incoming,
@@ -1941,11 +2186,8 @@
     if copies == 1:
         grad_gate, grad_up, grad_down = order_grads(expert_results)
     else:
-        expert_results = [own_grads(blocks) for blocks in expert_results]
-        grad_gate, grad_up, grad_down = (
-            jnp.stack([jnp.stack([got[kind] for got in layer]) for layer in expert_results])
-            for kind in range(3)
-        )
+        ordered = jnp.stack([own_grads(blocks) for blocks in expert_results])
+        grad_gate, grad_up, grad_down = (ordered[:, :, kind] for kind in range(3))
     grad_gate, grad_up = grad_gate.swapaxes(2, 3), grad_up.swapaxes(2, 3)
     return (
         hidden,

time: 1510 us -> 1420 us (0.940)
  Pallas kernels: 1440 us -> 1340 us
  starting transfers between devices: 7.65 us -> 28.5 us
  local copies, waits for them, and re-layouts: 30.6 us -> 14.8 us
    pallas_call x2, Pallas kernels: 377 us -> 337 us  [moe_backward(): pl.pallas_call(functools.partial(moe_backward_kernel, dims, bool(opening)...]
    pallas_call x2, Pallas kernels: 483 us -> 457 us  [moe_forward(): pl.pallas_call(functools.partial(moe_forward_kernel, dims, row_count, lay...]
    ppermute x6, starting transfers between devices: 7.65 us -> 28.5 us  [move_grads(): blocks.append(lax.ppermute(grads[step], 'row', pairs))]
where the time goes in v3:
time: 1420 us; the launch traced here: 1400 us
  Pallas kernels  1340 us (94%)
  starting transfers between devices  28.5 us (2%)
  other arithmetic  19.3 us (1%)
  local copies, waits for them, and re-layouts  14.8 us (1%)
    pallas_call x2, Pallas kernels, moe_forward(): pl.pallas_call(functools.partial(moe_forward_kernel, dims, row_count, lay...  457 us
    pallas_call x2, Pallas kernels, moe_backward(): pl.pallas_call(functools.partial(moe_backward_kernel, dims, bool(opening)...  337 us
    pallas_call x2, Pallas kernels, reduce_dense(): pl.pallas_call(functools.partial(reduce_dense_kernel, (row_count, pair_co...  231 us
    pallas_call x2, Pallas kernels, attend_forward(): pl.pallas_call(functools.partial(attend_forward_kernel, (col_count, row_c...  110 us
    pallas_call x2, Pallas kernels, attend_backward(): pl.pallas_call(functools.partial(attend_backward_kernel, (col_count, HEAD...  104 us
    pallas_call x1, Pallas kernels, gather_dense(): pl.pallas_call(functools.partial(gather_dense_kernel, dims, copies), out_...  84 us
    ppermute x6, starting transfers between devices, move_grads(): blocks.append(lax.ppermute(grads[step], 'row', pairs))  28.5 us
  transfers between devices with their start and end apart: 6, of which 0 were waited for; matrix products, arithmetic and copies ran while one was open for 1% of the time, Pallas kernels for 24%

profile of v3, /device:TPU:30, one launch (start us, length us, event | category | flops | bytes accessed | tf_op | source)
XLA Modules:
  0.0 1401.5 jit_solution(11306654908389921884)
XLA Ops:
  0.7 1.1 fusion.9
  1.8 0.8 copy.36
  2.6 1.7 slice_bitcast_fusion
  4.3 0.7 reshape.109.router_ref
  5.0 0.6 reshape.108.routes_ref
  5.6 84.0 %gather_dense.1 = (bf16[4,2048,384]{2,1,0:T(8,128)(2,1)}, bf16[4,1536,384]{2,1,0:T(8,128)(2,1)}, s32[4,16,128]{2,1,0:T(8,128)}, bf16[4,192,128]{2,1,0:T(8,128)(2,1)}, bf16[4,192,1536]{2,1,0:T(8,128)(2,1)}) custom-call(bf16[256,384]{1,0:T(8,128)(2,1)} %bitcast.96, bf16[192,384]{1,0:T(8,128)(2,1)} %get-tuple-element.163.out_ref, ...), custom_call_target="tpu_custom_call" | custom-call | tf_op jit(solution)/shard_map/gather_dense/pallas_call | solution.py:1545
  89.6 1.1 reshape_reshape.7
  90.7 0.2 copy.55
  90.9 0.1 fusion.10
  91.1 0.4 fusion.5
  91.5 0.7 copy.57
  92.1 1.3 convert_element_type.29.x_ref
  93.5 0.6 slice_bitcast_fusion.2
  94.1 0.8 copy.38
  94.9 0.7 copy.56
  95.6 0.5 fusion.8
  96.1 0.6 fusion.11
  96.7 0.8 pad_maximum_fusion.2
  97.6 54.0 %attend_forward.2 = (f32[256,1536]{1,0:T(8,128)}, bf16[256,1536]{1,0:T(8,128)(2,1)}, bf16[256,1536]{1,0:T(8,128)(2,1)}, bf16[2048,512]{1,0:T(8,128)(2,1)}, bf16[...) custom-call(f32[256,1536]{1,0:T(8,128)} %convert_element_type.29.x_ref,, ...), custom_call_target="tpu_custom_call" | custom-call | tf_op jit(solution)/shard_map/attend_forward/pallas_call | solution.py:1773
  151.6 231.1 %moe_forward.2 = (f32[256,1536]{1,0:T(8,128)}, f32[1024,32]{1,0:T(8,128)}, bf16[1152,1536]{1,0:T(8,128)(2,1)}, bf16[1152,1536]{1,0:T(8,128)(2,1)}, bf16[4,192,15...) custom-call(bf16[256,1536]{1,0:T(8,128)(2,1)} %get-tuple-element.89.refs_0_.refs_4_, ...), custom_call_target="tpu_custom_call" | custom-call | bytes 629145600 | tf_op jit(solution)/shard_map/moe_forward/pallas_call | solution.py:1016
  382.7 2.7 add.38.x_ref
  385.4 55.7 %attend_forward.3 = (f32[256,1536]{1,0:T(8,128)}, bf16[256,1536]{1,0:T(8,128)(2,1)}, bf16[256,1536]{1,0:T(8,128)(2,1)}, bf16[2048,512]{1,0:T(8,128)(2,1)}, bf16[...) custom-call(f32[256,1536]{1,0:T(8,128)} %add.38.x_ref, ...), custom_call_target="tpu_custom_call" | custom-call | tf_op jit(solution)/shard_map/attend_forward/pallas_call | solution.py:1773
  441.1 225.8 %moe_forward.3 = (bf16[1024,1536]{1,0:T(8,128)(2,1)}, f32[1024,32]{1,0:T(8,128)}, bf16[1152,1536]{1,0:T(8,128)(2,1)}, bf16[1152,1536]{1,0:T(8,128)(2,1)}, bf16[1...) custom-call(bf16[256,1536]{1,0:T(8,128)(2,1)} %get-tuple-element.98.refs_0_.refs_4_, ...), custom_call_target="tpu_custom_call" | custom-call | bytes 629145600 | tf_op jit(solution)/shard_map/moe_forward/pallas_call | solution.py:1016
  666.9 177.5 %moe_backward.2 = (f32[256,1536]{1,0:T(8,128)}, f32[32,1536]{1,0:T(8,128)}, bf16[3,192,1536]{2,1,0:T(8,128)(2,1)}, bf16[3,192,1536]{2,1,0:T(8,128)(2,1)}, bf16[3...) custom-call(bf16[1024,1536]{1,0:T(8,128)(2,1)} %get-tuple-element.100.refs_0_, ...), custom_call_target="tpu_custom_call" | custom-call | bytes 629145600 | tf_op jit(solution)/shard_map/moe_backward/pallas_call | solution.py:1077
  844.4 11.8 collective-permute-start
  856.2 2.4 collective-permute-start.2
  858.7 1.3 convert_element_type.33.incoming_ref
  860.0 49.8 %attend_backward.2 = (f32[256,1536]{1,0:T(8,128)}, bf16[256,1536]{1,0:T(8,128)(2,1)}, bf16[256,2048]{1,0:T(8,128)(2,1)}, f32[1,1536]{1,0:T(1,128)}, f32[1,1536]{1,0:T(1,128)}) custom-call(f32[256,1536]{1,0:T(8,128)} %convert_element_type.33.incoming_ref, f32[256,1536]{1,0:T(8,128)} %get-tuple-element.108.grad_moe_ref, ...), custom_call_target="tpu_custom_call" | custom-call | tf_op jit(solution)/shard_map/attend_backward/pallas_call | solution.py:1940
  909.8 0.7 convert_reduce_fusion.3
  910.5 0.1 concatenate.37
  910.6 0.7 convert_reduce_fusion.2
  911.3 0.1 concatenate.38
  911.4 0.1 copy.54
  911.6 0.2 fusion.3
  911.8 0.2 concatenate.36
  912.1 0.1 copy.31
  912.2 0.2 reshape.113
  912.5 0.7 copy_bitcast_fusion.6.small_ref
  913.1 116.5 %reduce_dense.2 = (f32[384,256]{1,0:T(8,128)}, f32[192,384]{1,0:T(8,128)}, f32[16,128]{1,0:T(8,128)}) custom-call(bf16[256,1536]{1,0:T(8,128)(2,1)} %get-tuple-element.114.normed_ref, bf16[256,2048]{1,0:T(8,128)(2,1)} %get-tuple-element.115.grad_proj_ref, bf16[256,1536]{1,0:T(8,128)(2,1)} %get-tuple-element.116.grad_mid_ref, ...), custom_call_target="tpu_custom_call" | custom-call | tf_op jit(solution)/shard_map/reduce_dense/pallas_call | solution.py:1331
  1029.7 1.0 convert_element_type.34.refs_0_
  1030.6 159.3 %moe_backward.3 = (f32[256,1536]{1,0:T(8,128)}, f32[32,1536]{1,0:T(8,128)}, bf16[3,192,1536]{2,1,0:T(8,128)(2,1)}, bf16[3,192,1536]{2,1,0:T(8,128)(2,1)}, bf16[3...) custom-call(bf16[256,1536]{1,0:T(8,128)(2,1)} %convert_element_type.34.refs_0_, ...), custom_call_target="tpu_custom_call" | custom-call | bytes 629145600 | tf_op jit(solution)/shard_map/moe_backward/pallas_call | solution.py:1077
  1189.9 11.9 collective-permute-start.3
  1201.8 2.4 collective-permute-start.5
  1204.2 0.1 reshape.121
  1204.3 2.8 add.39
  1207.1 53.8 %attend_backward.3 = (f32[256,1536]{1,0:T(8,128)}, bf16[256,1536]{1,0:T(8,128)(2,1)}, bf16[256,2048]{1,0:T(8,128)(2,1)}, f32[1,1536]{1,0:T(1,128)}, f32[1,1536]{1,0:T(1,128)}) custom-call(f32[256,1536]{1,0:T(8,128)} %get-tuple-element.126.incoming_ref, f32[256,1536]{1,0:T(8,128)} %get-tuple-element.131.grad_moe_ref, f32[256,1536]{1,0:T(8,128)} %get-tuple-element.88.mid_ref, ...), custom_call_target="tpu_custom_call" | custom-call | tf_op jit(solution)/shard_map/attend_backward/pallas_call | solution.py:1940
  1260.9 0.7 convert_reduce_fusion.1
  1261.6 0.1 concatenate.41
  1261.7 0.7 convert_reduce_fusion
  1262.4 0.1 concatenate.42
  1262.5 0.1 copy.53
  1262.7 0.2 fusion.1
  1262.9 0.2 concatenate.40
  1263.2 0.1 copy.34
  1263.3 0.2 reshape.116
  1263.5 0.7 copy_bitcast_fusion.5.small_ref
  1264.2 115.0 %reduce_dense.3 = (f32[384,256]{1,0:T(8,128)}, f32[192,384]{1,0:T(8,128)}, f32[16,128]{1,0:T(8,128)}) custom-call(bf16[256,1536]{1,0:T(8,128)(2,1)} %get-tuple-element.137.normed_ref, bf16[256,2048]{1,0:T(8,128)(2,1)} %get-tuple-element.138.grad_proj_ref, bf16[256,1536]{1,0:T(8,128)(2,1)} %get-tuple-element.139.grad_mid_ref, ...), custom_call_target="tpu_custom_call" | custom-call | tf_op jit(solution)/shard_map/reduce_dense/pallas_call | solution.py:1331
  1379.2 0.8 reshape.119
  1380.0 0.6 pad_maximum_fusion.5
  1380.6 0.6 pad_maximum_fusion.4
  1381.2 1.8 pad_maximum_fusion.1
  1383.0 1.9 pad_maximum_fusion
  1384.9 15.2 %order_grads.1 = (f32[2,4,192,1536]{3,2,1,0:T(8,128)}, f32[2,4,192,1536]{3,2,1,0:T(8,128)}, f32[2,4,192,1536]{3,2,1,0:T(8,128)}) custom-call(bf16[3,192,1536]{2,1,0:T(8,128)(2,1)} %get-tuple-element.149.refs_0_, bf16[3,192,1536]{2,1,0:T(8,128)(2,1)} %collective-permute-done.3.refs_1_, bf16[3,192,1536]{2,1,0:T(8,128)(2,1)} %collective-permute-done.4.refs_2_, ...), custom_call_target="tpu_custom_call" | custom-call | tf_op jit(solution)/shard_map/order_grads/pallas_call | solution.py:1611
  1400.1 1.1 copy.59
  (49 shorter events, 0.4 us)
Async XLA Ops:
  0.6 3.7 copy-start.10
  0.7 4.3 copy-start.15
  89.6 2.5 copy-start.5
  91.0 2.5 copy-start.11
  92.1 4.0 copy-start.12
  92.1 4.0 copy-start.13
  151.6 231.1 %copy-start = (f32[256,1536]{1,0:T(8,128)S(1)}, f32[256,1536]{1,0:T(8,128)}, u32[]{:S(2)}) copy-start(f32[256,1536]{1,0:T(8,128)} %get-tuple-element.88.mid_ref) | copy-start | bytes 4718596
  666.9 191.7 %copy-start.3 = (bf16[256,1536]{1,0:T(8,128)(2,1)S(1)}, bf16[256,1536]{1,0:T(8,128)(2,1)}, u32[]{:S(2)}) copy-start(bf16[256,1536]{1,0:T(8,128)(2,1)} %refs_6_.1) | copy-start | bytes 2359300
  844.4 185.2 %collective-permute-start = (bf16[3,192,1536]{2,1,0:T(8,128)(2,1)}, bf16[3,192,1536]{2,1,0:T(8,128)(2,1)}, u32[]{:S(2)}, u32[]{:S(2)}) collective-permute-start(bf16[3,192,1536]{2,1,0:T(8,128)(2,1)} %get-tuple-element.123), channel_id=1, source_target_pairs={{0,24},{8,0},{16,8},{24,16},{1,25},{9,1},{17,9},{25,17},{2,26},{10... | collective-permute-start | bytes 5308424 | tf_op jit(solution)/shard_map/ppermute | solution.py:2028
  856.2 173.4 %collective-permute-start.1 = (bf16[3,192,1536]{2,1,0:T(8,128)(2,1)}, bf16[3,192,1536]{2,1,0:T(8,128)(2,1)}, u32[]{:S(2)}, u32[]{:S(2)}) collective-permute-start(bf16[3,192,1536]{2,1,0:T(8,128)(2,1)} %get-tuple-element.124), channel_id=1, source_target_pairs={{0,16},{8,24},{16,0},{24,8},{1,17},{9,25},{17,1},{25,9},{2,18},{10... | collective-permute-start | bytes 5308424 | tf_op jit(solution)/shard_map/ppermute | solution.py:2028
  856.2 173.5 %collective-permute-start.2 = (bf16[3,192,1536]{2,1,0:T(8,128)(2,1)}, bf16[3,192,1536]{2,1,0:T(8,128)(2,1)}, u32[]{:S(2)}, u32[]{:S(2)}) collective-permute-start(bf16[3,192,1536]{2,1,0:T(8,128)(2,1)} %get-tuple-element.125), channel_id=1, source_target_pairs={{0,8},{8,16},{16,24},{24,0},{1,9},{9,17},{17,25},{25,1},{2,10},{10... | collective-permute-start | bytes 5308424 | tf_op jit(solution)/shard_map/ppermute | solution.py:2028
  860.0 51.5 %copy-start.8 = (f32[32,1536]{1,0:T(8,128)S(1)}, f32[32,1536]{1,0:T(8,128)}, u32[]{:S(2)}) copy-start(f32[32,1536]{1,0:T(8,128)} %get-tuple-element.117) | copy-start | bytes 589828
  913.1 116.5 %copy-start.2 = (f32[256,1536]{1,0:T(8,128)S(1)}, f32[256,1536]{1,0:T(8,128)}, u32[]{:S(2)}) copy-start(f32[256,1536]{1,0:T(8,128)} %get-tuple-element.126.incoming_ref) | copy-start | bytes 4718596
  1030.6 173.6 %copy-start.14 = (f32[16,128]{1,0:T(8,128)S(1)}, f32[16,128]{1,0:T(8,128)}, u32[]{:S(2)}) copy-start(f32[16,128]{1,0:T(8,128)} %get-tuple-element.144) | copy-start | bytes 24580
  1030.6 173.7 %copy-start.1 = (f32[256,1536]{1,0:T(8,128)S(1)}, f32[256,1536]{1,0:T(8,128)}, u32[]{:S(2)}) copy-start(f32[256,1536]{1,0:T(8,128)} %get-tuple-element.97.mid_ref) | copy-start | bytes 4718596
  1189.9 195.0 %collective-permute-start.3 = (bf16[3,192,1536]{2,1,0:T(8,128)(2,1)}, bf16[3,192,1536]{2,1,0:T(8,128)(2,1)}, u32[]{:S(2)}, u32[]{:S(2)}) collective-permute-start(bf16[3,192,1536]{2,1,0:T(8,128)(2,1)} %get-tuple-element.150), channel_id=1, source_target_pairs={{0,24},{8,0},{16,8},{24,16},{1,25},{9,1},{17,9},{25,17},{2,26},{10... | collective-permute-start | bytes 5308424 | tf_op jit(solution)/shard_map/ppermute | solution.py:2028
  1201.8 183.1 %collective-permute-start.4 = (bf16[3,192,1536]{2,1,0:T(8,128)(2,1)}, bf16[3,192,1536]{2,1,0:T(8,128)(2,1)}, u32[]{:S(2)}, u32[]{:S(2)}) collective-permute-start(bf16[3,192,1536]{2,1,0:T(8,128)(2,1)} %get-tuple-element.151), channel_id=1, source_target_pairs={{0,16},{8,24},{16,0},{24,8},{1,17},{9,25},{17,1},{25,9},{2,18},{10... | collective-permute-start | bytes 5308424 | tf_op jit(solution)/shard_map/ppermute | solution.py:2028
  1201.8 183.1 %collective-permute-start.5 = (bf16[3,192,1536]{2,1,0:T(8,128)(2,1)}, bf16[3,192,1536]{2,1,0:T(8,128)(2,1)}, u32[]{:S(2)}, u32[]{:S(2)}) collective-permute-start(bf16[3,192,1536]{2,1,0:T(8,128)(2,1)} %get-tuple-element.152), channel_id=1, source_target_pairs={{0,8},{8,16},{16,24},{24,0},{1,9},{9,17},{17,25},{25,1},{2,10},{10... | collective-permute-start | bytes 5308424 | tf_op jit(solution)/shard_map/ppermute | solution.py:2028
  1207.1 55.4 %copy-start.9 = (f32[32,1536]{1,0:T(8,128)S(1)}, f32[32,1536]{1,0:T(8,128)}, u32[]{:S(2)}) copy-start(f32[32,1536]{1,0:T(8,128)} %get-tuple-element.140) | copy-start | bytes 589828
  1264.2 117.0 %copy-start.7 = (f32[192,384]{1,0:T(8,128)S(1)}, f32[192,384]{1,0:T(8,128)}, u32[]{:S(2)}) copy-start(f32[192,384]{1,0:T(8,128)} %get-tuple-element.121) | copy-start | bytes 884740
  1264.2 118.8 %copy-start.6 = (f32[384,256]{1,0:T(8,128)S(1)}, f32[384,256]{1,0:T(8,128)}, u32[]{:S(2)}) copy-start(f32[384,256]{1,0:T(8,128)} %get-tuple-element.146) | copy-start | bytes 1179652
  1384.9 15.2 %copy-start.4 = (f32[256,1536]{1,0:T(8,128)S(1)}, f32[256,1536]{1,0:T(8,128)}, u32[]{:S(2)}) copy-start(f32[256,1536]{1,0:T(8,128)} %get-tuple-element.194) | copy-start | bytes 4718596

commit v4 on v3

--- a/solution.py
+++ b/solution.py
@@ -689,7 +689,45 @@
         keep.wait()
 
 
-def moe_backward_kernel(dims, opening, *refs):
+class RowTotal:
+    def __init__(self, rows, blocks, landed, own, sems):
+        self.rows = rows
+        self.blocks = blocks
+        self.landed = landed
+        self.own = own
+        self.remote_sems = sems[:2]
+        self.local_sem = sems[2]
+
+    def out(self, step):
+        place = self.rows.ahead(step)
+        return send_to(
+            self.blocks.at[place],
+            self.landed.at[step - 1],
+            self.remote_sems,
+            step - 1,
+            self.rows.device_of(place),
+        )
+
+    def load(self):
+        return pltpu.make_async_copy(self.blocks.at[self.rows.place], self.own, self.local_sem)
+
+    def start(self):
+        self.load().start()
+        for step in range(1, self.rows.count):
+            self.out(step).start()
+
+    def finish(self, out):
+        self.load().wait()
+        total = self.own[...].astype(jnp.float32)
+        for step in range(1, self.rows.count):
+            self.out(step).wait_recv()
+            total = total + self.landed[step - 1].astype(jnp.float32)
+        out[...] = total
+        for step in range(1, self.rows.count):
+            self.out(step).wait_send()
+
+
+def moe_backward_kernel(dims, opening, dense_count, *refs):
     group_rows, col_count, copies, token_rows, slot_rows, chunks, width = dims
     own_ref, routes_ref, router_ref, gates_ref, normed_ref, slots_in, returned_in = refs[:7]
     weight_in = refs[7:10]
@@ -697,8 +735,18 @@
     opening_in = refs[: 1 if opening else 0]
     refs = refs[len(opening_in) :]
     block_count, slice_width = weight_in[0].shape[:2]
+    dense_in = refs[:dense_count]
+    refs = refs[dense_count:]
     sum_ref, router_grad_ref, *grads_out = refs[: 2 + block_count]
     refs = refs[2 + block_count :]
+    dense_out = refs[:dense_count]
+    refs = refs[dense_count:]
+    dense_scratch = refs[len(refs) - 5 * dense_count :]
+    refs = refs[: len(refs) - 5 * dense_count]
+    totals = [
+        RowTotal(all_rows(block_count), blocks, *dense_scratch[5 * n : 5 * n + 2], dense_scratch[5 * n + 2 : 5 * n + 5])
+        for n, blocks in enumerate(dense_in)
+    ]
     opening_out = refs[: len(opening_in)]
     refs = refs[len(opening_in) :]
     opening_scratch = ()
@@ -866,6 +914,8 @@
         received[slot_part(cols.place), chunk] = send[slot_part(cols.place), chunk]
 
     over_chunks(chunks, width, dispatch)
+    for total in totals:
+        total.start()
 
     def pairs(part):
         picked = slot_block((all_slots, pair_send.shape[1]), 0, slot_rows)
@@ -995,6 +1045,8 @@
 
     over_chunks(chunks, width, drain)
     pair.wait_send(0, None)
+    for total, out in zip(totals, dense_out):
+        total.finish(out)
 
 
 def moe_forward(
@@ -1056,12 +1108,12 @@
         compiler_params=pltpu.CompilerParams(
             collective_id=1 + 7 * layer, has_side_effects=True, vmem_limit_bytes=vmem_most
         ),
-        cost_estimate=long_cost,
+        cost_estimate=no_cost,
         name="moe_forward",
     )(own, routes, router, *weights, *next_blocks, *closing)
 
 
-def moe_backward(dims, own, routes, router, gates, normed, slots, returned, weights, opening):
+def moe_backward(dims, own, routes, router, gates, normed, slots, returned, weights, opening, dense):
     group_rows, col_count, copies, token_rows, slot_rows, chunks, width = dims
     all_tokens, all_slots = group_rows * token_rows, col_count * slot_rows
     model_width = own.shape[1]
@@ -1075,17 +1127,20 @@
     hidden_narrow = pltpu.VMEM((all_slots, hidden), jnp.bfloat16)
     weight_array = pltpu.VMEM((block_count, slice_width, model_width), jnp.bfloat16)
     return pl.pallas_call(
-        functools.partial(moe_backward_kernel, dims, bool(opening)),
+        functools.partial(moe_backward_kernel, dims, bool(opening), len(dense)),
         out_shape=(
             jax.ShapeDtypeStruct((token_rows, model_width), jnp.float32),
             jax.ShapeDtypeStruct((E, model_width), jnp.float32),
             *([grads] * block_count),
+            *(jax.ShapeDtypeStruct(block.shape[1:], jnp.float32) for block in dense),
             *([jax.ShapeDtypeStruct((token_rows, model_width), jnp.float32)] * opened),
         ),
         in_specs=[outside if opening else vmem]
         + [vmem] * 4
-        + [outside] * (5 + opened),
-        out_specs=(vmem, vmem) + (outside,) * block_count + (vmem,) * opened,
+        + [outside] * (5 + opened + len(dense)),
+        out_specs=(vmem, vmem)
+        + (outside,) * block_count
+        + (vmem,) * (len(dense) + opened),
         scratch_shapes=[
             pltpu.VMEM((all_slots, all_tokens), jnp.bfloat16),
             pltpu.VMEM((all_tokens, all_slots), jnp.bfloat16),
@@ -1124,13 +1179,22 @@
                 if opening
                 else ()
             ),
+            *(
+                item
+                for block in dense
+                for item in (
+                    pltpu.VMEM((max(block_count - 1, 1), *block.shape[1:]), jnp.bfloat16),
+                    pltpu.VMEM(block.shape[1:], jnp.bfloat16),
+                    *WeightMove.sems(block_count),
+                )
+            ),
         ],
         compiler_params=pltpu.CompilerParams(
-            collective_id=9 if opening else 2, has_side_effects=True, vmem_limit_bytes=vmem_most
+            collective_id=(9 if opening else 2) + (10 if dense else 0), has_side_effects=True, vmem_limit_bytes=vmem_most
         ),
-        cost_estimate=long_cost,
+        cost_estimate=no_cost,
         name="moe_backward",
-    )(own, routes, router, gates, normed, slots, returned, *weights, *opening)
+    )(own, routes, router, gates, normed, slots, returned, *weights, *opening, *dense)
 
 
 def col_pairs():
@@ -1154,12 +1218,11 @@
     grad_mid_ref,
     attended_ref,
     small_ref,
-    qkv_ref,
-    out_ref,
-    small_out_ref,
-    *scratch,
+    *refs,
 ):
-    row_count, pair_count = dims
+    row_count, pair_count, to_rows = dims
+    outputs = refs[:3]
+    scratch = refs[3:]
     kinds = 3
     buffers = [scratch[6 * kind : 6 * kind + 6] for kind in range(kinds)]
     sems = scratch[6 * kinds : 12 * kinds]
@@ -1190,8 +1253,7 @@
             return dot_nn(grad_mid_t[col], attended[row])
         return small_ref[col, row].astype(jnp.float32)
 
-    greet((rows, pairs, sides))
-    outputs = (qkv_ref, out_ref, small_out_ref)
+    greet((rows, pairs, sides) if to_rows else (pairs, sides))
 
     def side_copy(kind, pair):
         side_send, side_recv = buffers[kind][0], buffers[kind][1]
@@ -1262,6 +1324,10 @@
                 pair_copy(kind, ahead, row).wait_recv()
                 total = total + pair_recv[ahead - 1, row].astype(jnp.float32)
 
+            if not to_rows:
+                outputs[kind][row] = total.astype(jnp.bfloat16)
+                continue
+
             whole[row] = total.astype(jnp.bfloat16)
 
             @pl.when(step < row_count)
@@ -1271,7 +1337,7 @@
         return carry
 
     lax.fori_loop(1, row_count + 1, third, 0)
-    for kind in range(kinds):
+    for kind in range(kinds if to_rows else 0):
         whole, row_recv = buffers[kind][4], buffers[kind][5]
         total = whole[rows.place].astype(jnp.float32)
         for step in range(1, row_count):
@@ -1293,12 +1359,29 @@
         return carry
 
     lax.fori_loop(1, pair_count, drain_pairs, 0)
-    for kind in range(kinds):
+    for kind in range(kinds if to_rows else 0):
         for step in range(1, row_count):
             row_copy(kind, step).wait_send()
 
 
-def reduce_dense(row_count, col_count, normed, grad_projected, grad_mid_b, attended, small):
+def order_scratch(slice_width, model_width):
+    return [
+        pltpu.VMEM((4, slice_width, model_width), jnp.bfloat16),
+        pltpu.VMEM((4, slice_width, model_width), jnp.float32),
+        pltpu.SemaphoreType.DMA((4,)),
+        pltpu.SemaphoreType.DMA((4,)),
+    ]
+
+
+def ordered_shapes(layer_count, blocks):
+    _, slice_width, model_width = blocks[0].shape
+    shape = (layer_count, len(blocks), slice_width, model_width)
+    return (jax.ShapeDtypeStruct(shape, jnp.float32),) * 3
+
+
+def reduce_dense(
+    row_count, col_count, normed, grad_projected, grad_mid_b, attended, small, to_rows
+):
     token_rows, model_width = normed.shape
     qkv_width, out_rows = grad_projected.shape[1], attended.shape[1]
     pair_count = col_count // 2
@@ -1329,17 +1412,31 @@
         pltpu.VMEM((row_count, token_rows, shapes[1][1]), jnp.bfloat16),
     ]
     return pl.pallas_call(
-        functools.partial(reduce_dense_kernel, (row_count, pair_count)),
-        out_shape=tuple(jax.ShapeDtypeStruct(shape, jnp.float32) for shape in shapes),
+        functools.partial(
+            reduce_dense_kernel,
+            (row_count, pair_count, to_rows),
+        ),
+        out_shape=tuple(
+            jax.ShapeDtypeStruct(shape, jnp.float32)
+            if to_rows
+            else jax.ShapeDtypeStruct((row_count, *shape), jnp.bfloat16)
+            for shape in shapes
+        ),
         in_specs=[vmem] * 5,
         out_specs=(vmem,) * 3,
         scratch_shapes=scratch + sems + operands,
         compiler_params=pltpu.CompilerParams(
-            collective_id=3, has_side_effects=True, vmem_limit_bytes=vmem_most
+            collective_id=3 if to_rows else 11, has_side_effects=True, vmem_limit_bytes=vmem_most
         ),
         cost_estimate=no_cost,
         name="reduce_dense",
-    )(normed, grad_projected, grad_mid_b, attended, small)
+    )(
+        normed,
+        grad_projected,
+        grad_mid_b,
+        attended,
+        small,
+    )
 
 
 class DenseGather:
@@ -1561,34 +1658,22 @@
     )(qkv_block, out_block, routes, router, shards)
 
 
-def order_grads_kernel(layer_count, block_count, *refs):
-    blocks = refs[: layer_count * block_count]
-    outputs = refs[layer_count * block_count : layer_count * block_count + 3]
-    came, wide, in_sems, out_sems = refs[layer_count * block_count + 3 :]
+def order_layer(layer, blocks, outputs, came, wide, in_sems, out_sems):
+    block_count = len(blocks)
     row_index = lax.axis_index("row")
-    items = [
-        (layer, step, kind)
-        for layer in range(layer_count)
-        for step in range(block_count)
-        for kind in range(3)
-    ]
+    count = 3 * block_count
 
     def load(number):
-        layer, step, kind = items[number]
         return pltpu.make_async_copy(
-            blocks[layer * block_count + step].at[kind],
-            came.at[number % 4],
-            in_sems.at[number % 4],
+            blocks[number // 3].at[number % 3], came.at[number % 4], in_sems.at[number % 4]
         )
 
     def store(number):
-        layer, step, kind = items[number]
-        expert = lax.rem(row_index + step, block_count)
+        expert = lax.rem(row_index + number // 3, block_count)
         return pltpu.make_async_copy(
-            wide.at[number % 4], outputs[kind].at[layer, expert], out_sems.at[number % 4]
-        )
-
-    count = len(items)
+            wide.at[number % 4], outputs[number % 3].at[layer, expert], out_sems.at[number % 4]
+        )
+
     for number in range(min(3, count)):
         load(number).start()
     for number in range(count):
@@ -1603,26 +1688,30 @@
         store(number).wait()
 
 
-def order_grads(layers):
-    layer_count, block_count = len(layers), len(layers[0])
-    _, slice_width, model_width = layers[0][0].shape
+def order_grads_kernel(block_count, layers, early, *refs):
+    blocks = [refs[block_count * n : block_count * (n + 1)] for n in range(len(layers))]
+    refs = refs[block_count * len(layers) + (3 if early else 0) :]
+    for layer, group in zip(layers, blocks):
+        order_layer(layer, group, refs[:3], *refs[3:])
+
+
+def order_grads(layer_count, groups, early):
+    blocks = [block for _, group in groups for block in group]
+    block_count = len(groups[0][1])
     outside = pl.BlockSpec(memory_space=pl.ANY)
-    shape = jax.ShapeDtypeStruct((layer_count, block_count, slice_width, model_width), jnp.float32)
     return pl.pallas_call(
-        functools.partial(order_grads_kernel, layer_count, block_count),
-        out_shape=(shape,) * 3,
-        in_specs=[outside] * (layer_count * block_count),
+        functools.partial(
+            order_grads_kernel, block_count, tuple(layer for layer, _ in groups), bool(early)
+        ),
+        out_shape=ordered_shapes(layer_count, groups[0][1]),
+        in_specs=[outside] * (len(blocks) + len(early)),
         out_specs=(outside,) * 3,
-        scratch_shapes=[
-            pltpu.VMEM((4, slice_width, model_width), jnp.bfloat16),
-            pltpu.VMEM((4, slice_width, model_width), jnp.float32),
-            pltpu.SemaphoreType.DMA((4,)),
-            pltpu.SemaphoreType.DMA((4,)),
-        ],
+        scratch_shapes=order_scratch(*blocks[0].shape[1:]),
+        input_output_aliases={len(blocks) + n: n for n in range(len(early))},
         compiler_params=pltpu.CompilerParams(vmem_limit_bytes=vmem_most),
         cost_estimate=no_cost,
         name="order_grads",
-    )(*[block for blocks in layers for block in blocks])
+    )(*blocks, *early)
 
 
 def pieces_nt(left, weights_ref):
@@ -2121,8 +2210,9 @@
             hidden = mid + mixed
     incoming = cotangent.astype(wide_type)
     dense_results = [None] * layer_count
-    small_results = [None] * layer_count
     expert_results = [None] * layer_count
+    part_sums = ()
+    ordered = ()
     for layer_index in reversed(range(layer_count)):
         x, mid, normed, queries, key_value, attended, log_sums, normed_moe = saved[layer_index][:8]
         gates, slots, returned = saved[layer_index][8:]
@@ -2137,10 +2227,18 @@
             returned,
             experts[layer_index],
             closing[1:],
-        )
+            part_sums,
+        )
+        if part_sums:
+            dense_results[layer_index + 1] = rest[row_count : row_count + 3]
+            del rest[row_count : row_count + 3]
         if closing:
             hidden = mid + rest.pop()
             closing = ()
+        if layer_index + 1 < layer_count:
+            grad_moe, expert_results[layer_index + 1] = lax.optimization_barrier(
+                (grad_moe, expert_results[layer_index + 1])
+            )
         expert_results[layer_index] = move_grads(rest)
         incoming, grad_mid, grad_projected, grad_gain_attn, grad_gain_moe = attend_backward(
             col_count,
@@ -2171,20 +2269,34 @@
         small_rows = -(-small_size // 2048) * 16
         small = jnp.pad(small, ((0, 0), (0, small_rows * 128 - small_size)))
         small = small.reshape(row_count, col_count, small_rows, 128).transpose(1, 0, 2, 3)
-        grad_qkv_block, grad_out_block, small = reduce_dense(
-            row_count, col_count, normed, grad_projected, grad_mid, attended, small
-        )
-        dense_results[layer_index] = (grad_qkv_block, grad_out_block.T)
-        small_results[layer_index] = small.reshape(-1)[:small_size].reshape(E + 2, -1).T
+        if layer_index == 0 and copies == 1 and layer_count > 1:
+            groups = tuple((above, expert_results[above]) for above in range(1, layer_count))
+            grad_mid, ordered = lax.optimization_barrier(
+                (grad_mid, order_grads(layer_count, groups, ()))
+            )
+        part_sums = reduce_dense(
+            row_count,
+            col_count,
+            normed,
+            grad_projected,
+            grad_mid,
+            attended,
+            small,
+            layer_index == 0,
+        )
         if layer_index > 0:
-            incoming, dense_results[layer_index], expert_results[layer_index] = (
-                lax.optimization_barrier(
-                    (incoming, dense_results[layer_index], expert_results[layer_index])
-                )
-            )
+            incoming, part_sums = lax.optimization_barrier((incoming, part_sums))
+        else:
+            dense_results[0] = part_sums
+    small_results = [
+        small.reshape(-1)[:small_size].reshape(E + 2, -1).T for _, _, small in dense_results
+    ]
+    dense_results = [(qkv, out.T) for qkv, out, _ in dense_results]
     small = jnp.stack(small_results)
     if copies == 1:
-        grad_gate, grad_up, grad_down = order_grads(expert_results)
+        grad_gate, grad_up, grad_down = order_grads(
+            layer_count, ((0, expert_results[0]),), ordered
+        )
     else:
         ordered = jnp.stack([own_grads(blocks) for blocks in expert_results])
         grad_gate, grad_up, grad_down = (ordered[:, :, kind] for kind in range(3))

time: 1420 us -> 1380 us (0.972)
  Pallas kernels: 1340 us -> 1300 us
    pallas_call x2, Pallas kernels: 231 us -> 181 us  [reduce_dense(): pl.pallas_call(functools.partial(reduce_dense_kernel, (row_count, pair_co...]
  transfers between devices with their start and end apart: 6 -> 6, of which waited for: 0 -> 0; matrix products, arithmetic and copies ran while one was open for 1% -> 1% of each run, Pallas kernels for 24% -> 34%
where the time goes in v4:
time: 1380 us; the launch traced here: 1370 us
  Pallas kernels  1300 us (94%)
  starting transfers between devices  28.6 us (2%)
  other arithmetic  19.3 us (1%)
  local copies, waits for them, and re-layouts  17.9 us (1%)
    pallas_call x2, Pallas kernels, moe_forward(): pl.pallas_call(functools.partial(moe_forward_kernel, dims, row_count, lay...  457 us
    pallas_call x2, Pallas kernels, moe_backward(): pl.pallas_call(functools.partial(moe_backward_kernel, dims, bool(opening)...  351 us
    pallas_call x2, Pallas kernels, reduce_dense(): pl.pallas_call(functools.partial(reduce_dense_kernel, (row_count, pair_co...  181 us
    pallas_call x2, Pallas kernels, attend_forward(): pl.pallas_call(functools.partial(attend_forward_kernel, (col_count, row_c...  110 us
    pallas_call x2, Pallas kernels, attend_backward(): pl.pallas_call(functools.partial(attend_backward_kernel, (col_count, HEAD...  103 us
    pallas_call x1, Pallas kernels, gather_dense(): pl.pallas_call(functools.partial(gather_dense_kernel, dims, copies), out_...  84 us
    ppermute x6, starting transfers between devices, move_grads(): blocks.append(lax.ppermute(grads[step], 'row', pairs))  28.6 us
  transfers between devices with their start and end apart: 6, of which 0 were waited for; matrix products, arithmetic and copies ran while one was open for 1% of the time, Pallas kernels for 34%

profile of v4, /device:TPU:30, one launch (start us, length us, event | category | flops | bytes accessed | tf_op | source)
XLA Modules:
  0.0 1368.7 jit_solution(1991804125421343147)
XLA Ops:
  0.7 1.1 fusion.9
  1.7 0.8 copy.39
  2.6 1.7 slice_bitcast_fusion
  4.3 1.4 reshape.109.router_ref
  5.7 1.3 reshape.108.routes_ref
  7.0 84.0 %gather_dense.1 = (bf16[4,2048,384]{2,1,0:T(8,128)(2,1)}, bf16[4,1536,384]{2,1,0:T(8,128)(2,1)}, s32[4,16,128]{2,1,0:T(8,128)}, bf16[4,192,128]{2,1,0:T(8,128)(2,1)}, bf16[4,192,1536]{2,1,0:T(8,128)(2,1)}) custom-call(bf16[256,384]{1,0:T(8,128)(2,1)} %bitcast.99, bf16[192,384]{1,0:T(8,128)(2,1)} %get-tuple-element.187.out_ref, ...), custom_call_target="tpu_custom_call" | custom-call | tf_op jit(solution)/shard_map/gather_dense/pallas_call | solution.py:1642
  91.1 1.1 reshape_reshape.7
  92.2 0.2 copy.58
  92.6 0.4 fusion.5
  93.0 0.7 copy.60
  93.6 1.3 convert_element_type.29.x_ref
  95.0 0.6 slice_bitcast_fusion.2
  95.6 0.8 copy.41
  96.4 0.7 copy.59
  97.1 0.5 fusion.8
  97.6 0.6 fusion.11
  98.2 0.8 pad_maximum_fusion.2
  99.1 54.0 %attend_forward.2 = (f32[256,1536]{1,0:T(8,128)}, bf16[256,1536]{1,0:T(8,128)(2,1)}, bf16[256,1536]{1,0:T(8,128)(2,1)}, bf16[2048,512]{1,0:T(8,128)(2,1)}, bf16[...) custom-call(f32[256,1536]{1,0:T(8,128)} %convert_element_type.29.x_ref,, ...), custom_call_target="tpu_custom_call" | custom-call | tf_op jit(solution)/shard_map/attend_forward/pallas_call | solution.py:1862
  153.1 231.2 %moe_forward.2 = (f32[256,1536]{1,0:T(8,128)}, f32[1024,32]{1,0:T(8,128)}, bf16[1152,1536]{1,0:T(8,128)(2,1)}, bf16[1152,1536]{1,0:T(8,128)(2,1)}, bf16[4,192,15...) custom-call(bf16[256,1536]{1,0:T(8,128)(2,1)} %get-tuple-element.101.refs_0_.refs_4_, ...), custom_call_target="tpu_custom_call" | custom-call | tf_op jit(solution)/shard_map/moe_forward/pallas_call | solution.py:1068
  384.3 2.7 add.38.x_ref
  387.0 55.7 %attend_forward.3 = (f32[256,1536]{1,0:T(8,128)}, bf16[256,1536]{1,0:T(8,128)(2,1)}, bf16[256,1536]{1,0:T(8,128)(2,1)}, bf16[2048,512]{1,0:T(8,128)(2,1)}, bf16[...) custom-call(f32[256,1536]{1,0:T(8,128)} %add.38.x_ref, ...), custom_call_target="tpu_custom_call" | custom-call | tf_op jit(solution)/shard_map/attend_forward/pallas_call | solution.py:1862
  442.7 225.7 %moe_forward.3 = (bf16[1024,1536]{1,0:T(8,128)(2,1)}, f32[1024,32]{1,0:T(8,128)}, bf16[1152,1536]{1,0:T(8,128)(2,1)}, bf16[1152,1536]{1,0:T(8,128)(2,1)}, bf16[1...) custom-call(bf16[256,1536]{1,0:T(8,128)(2,1)} %get-tuple-element.110.refs_0_.refs_4_, ...), custom_call_target="tpu_custom_call" | custom-call | tf_op jit(solution)/shard_map/moe_forward/pallas_call | solution.py:1068
  668.5 177.5 %moe_backward.2 = (f32[256,1536]{1,0:T(8,128)}, f32[32,1536]{1,0:T(8,128)}, bf16[3,192,1536]{2,1,0:T(8,128)(2,1)}, bf16[3,192,1536]{2,1,0:T(8,128)(2,1)}, bf16[3...) custom-call(bf16[1024,1536]{1,0:T(8,128)(2,1)} %get-tuple-element.112.refs_0_, ...), custom_call_target="tpu_custom_call" | custom-call | tf_op jit(solution)/shard_map/moe_backward/pallas_call | solution.py:1129
  846.0 11.8 collective-permute-start
  857.8 2.4 collective-permute-start.2
  860.2 1.3 convert_element_type.33.incoming_ref
  861.6 49.8 %attend_backward.2 = (f32[256,1536]{1,0:T(8,128)}, bf16[256,1536]{1,0:T(8,128)(2,1)}, bf16[256,2048]{1,0:T(8,128)(2,1)}, f32[1,1536]{1,0:T(1,128)}, f32[1,1536]{1,0:T(1,128)}) custom-call(f32[256,1536]{1,0:T(8,128)} %convert_element_type.33.incoming_ref, f32[256,1536]{1,0:T(8,128)} %get-tuple-element.120.grad_moe_ref, ...), custom_call_target="tpu_custom_call" | custom-call | tf_op jit(solution)/shard_map/attend_backward/pallas_call | solution.py:2029
  911.4 0.7 convert_reduce_fusion.3
  912.1 0.1 concatenate.37
  912.2 0.7 convert_reduce_fusion.2
  912.9 0.1 concatenate.38
  913.0 0.1 copy.57
  913.2 0.2 fusion.3
  913.4 0.2 concatenate.36
  913.7 0.1 copy.34
  913.8 0.2 reshape.113
  914.1 0.7 copy_bitcast_fusion.6.small_ref
  914.7 75.6 %reduce_dense.2 = (bf16[4,384,256]{2,1,0:T(8,128)(2,1)}, bf16[4,192,384]{2,1,0:T(8,128)(2,1)}, bf16[4,16,128]{2,1,0:T(8,128)(2,1)}) custom-call(bf16[256,1536]{1,0:T(8,128)(2,1)} %get-tuple-element.126.normed_ref, bf16[256,2048]{1,0:T(8,128)(2,1)} %get-tuple-element.127.grad_proj_ref, bf16[256,1536]{1,0:T(8,128)(2,1)} %get-tuple-element.128.grad_mid_ref, ...), custom_call_target="tpu_custom_call" | custom-call | tf_op jit(solution)/shard_map/reduce_dense/pallas_call | solution.py:1414
  990.3 1.0 convert_element_type.34.refs_0_
  991.3 173.2 %moe_backward.3 = (f32[256,1536]{1,0:T(8,128)}, f32[32,1536]{1,0:T(8,128)}, bf16[3,192,1536]{2,1,0:T(8,128)(2,1)}, bf16[3,192,1536]{2,1,0:T(8,128)(2,1)}, bf16[3...) custom-call(bf16[256,1536]{1,0:T(8,128)(2,1)} %convert_element_type., ...), custom_call_target="tpu_custom_call" | custom-call | tf_op jit(solution)/shard_map/moe_backward/pallas_call | solution.py:1129
  1164.5 11.9 collective-permute-start.3
  1176.4 2.4 collective-permute-start.5
  1178.8 1.1 copy.56
  1179.9 0.2 fusion.1
  1180.1 0.2 concatenate.40
  1180.3 0.8 reshape.121
  1181.1 2.8 add.39
  1183.9 7.9 order_grads.2
  1191.9 53.2 %attend_backward.3 = (f32[256,1536]{1,0:T(8,128)}, bf16[256,1536]{1,0:T(8,128)(2,1)}, bf16[256,2048]{1,0:T(8,128)(2,1)}, f32[1,1536]{1,0:T(1,128)}, f32[1,1536]{1,0:T(1,128)}) custom-call(f32[256,1536]{1,0:T(8,128)} %get-tuple-element.135.incoming_ref, f32[256,1536]{1,0:T(8,128)} %get-tuple-element.148.grad_moe_ref, f32[256,1536]{1,0:T(8,128)} %get-tuple-element.100.mid_ref, ...), custom_call_target="tpu_custom_call" | custom-call | tf_op jit(solution)/shard_map/attend_backward/pallas_call | solution.py:2029
  1245.1 0.7 convert_reduce_fusion.1
  1245.8 0.1 concatenate.41
  1245.9 0.7 convert_reduce_fusion
  1246.6 0.1 concatenate.42
  1246.8 0.1 copy.37
  1246.9 0.2 reshape.116
  1247.1 0.7 copy_bitcast_fusion.5.small_ref
  1247.8 105.7 %reduce_dense.3 = (f32[384,256]{1,0:T(8,128)}, f32[192,384]{1,0:T(8,128)}, f32[16,128]{1,0:T(8,128)}) custom-call(bf16[256,1536]{1,0:T(8,128)(2,1)} %get-tuple-element.154.normed_ref, bf16[256,2048]{1,0:T(8,128)(2,1)} %get-tuple-element.155.grad_proj_ref, bf16[256,1536]{1,0:T(8,128)(2,1)} %get-tuple-element.164.grad_mid_ref, ...), custom_call_target="tpu_custom_call" | custom-call | tf_op jit(solution)/shard_map/reduce_dense/pallas_call | solution.py:1414
  1353.6 0.8 reshape.119
  1354.3 0.6 pad_maximum_fusion.5
  1354.9 0.6 pad_maximum_fusion.4
  1355.5 1.8 pad_maximum_fusion.1
  1357.3 1.9 pad_maximum_fusion
  1359.3 8.1 order_grads.3
  1367.4 1.1 copy.65
  (42 shorter events, 0.4 us)
Async XLA Ops:
  91.1 2.5 copy-start.5
  92.2 2.8 copy-start.9
  92.5 5.1 copy-start.10
  92.5 5.1 copy-start.11
  153.1 231.2 %copy-start = (f32[256,1536]{1,0:T(8,128)S(1)}, f32[256,1536]{1,0:T(8,128)}, u32[]{:S(2)}) copy-start(f32[256,1536]{1,0:T(8,128)} %get-tuple-element.100.mid_ref) | copy-start | bytes 4718596
  668.5 191.8 %copy-start.3 = (bf16[256,1536]{1,0:T(8,128)(2,1)S(1)}, bf16[256,1536]{1,0:T(8,128)(2,1)}, u32[]{:S(2)}) copy-start(bf16[256,1536]{1,0:T(8,128)(2,1)} %refs_6_.1) | copy-start | bytes 2359300
  846.0 330.4 %collective-permute-start = (bf16[3,192,1536]{2,1,0:T(8,128)(2,1)}, bf16[3,192,1536]{2,1,0:T(8,128)(2,1)}, u32[]{:S(2)}, u32[]{:S(2)}) collective-permute-start(bf16[3,192,1536]{2,1,0:T(8,128)(2,1)} %get-tuple-element.145), channel_id=1, source_target_pairs={{0,24},{8,0},{16,8},{24,16},{1,25},{9,1},{17,9},{25,17},{2,26},{10... | collective-permute-start | bytes 5308424 | tf_op jit(solution)/shard_map/ppermute | solution.py:2117
  857.8 326.1 %collective-permute-start.1 = (bf16[3,192,1536]{2,1,0:T(8,128)(2,1)}, bf16[3,192,1536]{2,1,0:T(8,128)(2,1)}, u32[]{:S(2)}, u32[]{:S(2)}) collective-permute-start(bf16[3,192,1536]{2,1,0:T(8,128)(2,1)} %get-tuple-element.146), channel_id=1, source_target_pairs={{0,16},{8,24},{16,0},{24,8},{1,17},{9,25},{17,1},{25,9},{2,18},{10... | collective-permute-start | bytes 5308424 | tf_op jit(solution)/shard_map/ppermute | solution.py:2117
  857.8 326.1 %collective-permute-start.2 = (bf16[3,192,1536]{2,1,0:T(8,128)(2,1)}, bf16[3,192,1536]{2,1,0:T(8,128)(2,1)}, u32[]{:S(2)}, u32[]{:S(2)}) collective-permute-start(bf16[3,192,1536]{2,1,0:T(8,128)(2,1)} %get-tuple-element.147), channel_id=1, source_target_pairs={{0,8},{8,16},{16,24},{24,0},{1,9},{9,17},{17,25},{25,1},{2,10},{10... | collective-permute-start | bytes 5308424 | tf_op jit(solution)/shard_map/ppermute | solution.py:2117
  861.6 51.5 %copy-start.8 = (f32[32,1536]{1,0:T(8,128)S(1)}, f32[32,1536]{1,0:T(8,128)}, u32[]{:S(2)}) copy-start(f32[32,1536]{1,0:T(8,128)} %get-tuple-element.129) | copy-start | bytes 589828
  914.0 76.3 %copy-start.2 = (f32[256,1536]{1,0:T(8,128)S(1)}, f32[256,1536]{1,0:T(8,128)}, u32[]{:S(2)}) copy-start(f32[256,1536]{1,0:T(8,128)} %get-tuple-element.135.incoming_ref) | copy-start | bytes 4718596
  991.3 189.8 %copy-start.1 = (f32[256,1536]{1,0:T(8,128)S(1)}, f32[256,1536]{1,0:T(8,128)}, u32[]{:S(2)}) copy-start(f32[256,1536]{1,0:T(8,128)} %get-tuple-element.109.mid_ref) | copy-start | bytes 4718596
  1164.5 194.8 %collective-permute-start.3 = (bf16[3,192,1536]{2,1,0:T(8,128)(2,1)}, bf16[3,192,1536]{2,1,0:T(8,128)(2,1)}, u32[]{:S(2)}, u32[]{:S(2)}) collective-permute-start(bf16[3,192,1536]{2,1,0:T(8,128)(2,1)} %get-tuple-element.175), channel_id=1, source_target_pairs={{0,24},{8,0},{16,8},{24,16},{1,25},{9,1},{17,9},{25,17},{2,26},{10... | collective-permute-start | bytes 5308424 | tf_op jit(solution)/shard_map/ppermute | solution.py:2117
  1176.4 182.9 %collective-permute-start.4 = (bf16[3,192,1536]{2,1,0:T(8,128)(2,1)}, bf16[3,192,1536]{2,1,0:T(8,128)(2,1)}, u32[]{:S(2)}, u32[]{:S(2)}) collective-permute-start(bf16[3,192,1536]{2,1,0:T(8,128)(2,1)} %get-tuple-element.176), channel_id=1, source_target_pairs={{0,16},{8,24},{16,0},{24,8},{1,17},{9,25},{17,1},{25,9},{2,18},{10... | collective-permute-start | bytes 5308424 | tf_op jit(solution)/shard_map/ppermute | solution.py:2117
  1176.4 182.9 %collective-permute-start.5 = (bf16[3,192,1536]{2,1,0:T(8,128)(2,1)}, bf16[3,192,1536]{2,1,0:T(8,128)(2,1)}, u32[]{:S(2)}, u32[]{:S(2)}) collective-permute-start(bf16[3,192,1536]{2,1,0:T(8,128)(2,1)} %get-tuple-element.177), channel_id=1, source_target_pairs={{0,8},{8,16},{16,24},{24,0},{1,9},{9,17},{17,25},{25,1},{2,10},{10... | collective-permute-start | bytes 5308424 | tf_op jit(solution)/shard_map/ppermute | solution.py:2117
  1247.1 108.4 %copy-start.7 = (f32[192,384]{1,0:T(8,128)S(1)}, f32[192,384]{1,0:T(8,128)}, u32[]{:S(2)}) copy-start(f32[192,384]{1,0:T(8,128)} %get-tuple-element.173) | copy-start | bytes 884740
  1247.8 109.5 %copy-start.6 = (f32[384,256]{1,0:T(8,128)S(1)}, f32[384,256]{1,0:T(8,128)}, u32[]{:S(2)}) copy-start(f32[384,256]{1,0:T(8,128)} %get-tuple-element.171) | copy-start | bytes 1179652
  1359.3 8.1 copy-start.4

commit v5 on v4

--- a/solution.py
+++ b/solution.py
@@ -351,7 +351,7 @@
 
 
 class WeightMove:
-    def __init__(self, rows, copies, layer, shards, target, sems):
+    def __init__(self, rows, copies, layer, shards, target, sems, parts=1):
         self.rows = rows
         self.copies = copies
         self.layer = layer
@@ -359,51 +359,71 @@
         self.target = target
         self.remote_sems = sems[:2]
         self.local_sem = sems[2]
+        self.parts = parts
+        self.width = target.shape[2] // parts
 
     @staticmethod
-    def sems(row_count):
-        return [pltpu.SemaphoreType.DMA((max(row_count - 1, 1),))] * 2 + [pltpu.SemaphoreType.DMA]
-
-    def shard(self, place):
-        return self.shards.at[self.layer, place // self.copies]
+    def sems(row_count, parts=1):
+        return [pltpu.SemaphoreType.DMA((parts, max(row_count - 1, 1)))] * 2 + [
+            pltpu.SemaphoreType.DMA
+        ]
 
     def own(self):
         return pltpu.make_async_copy(
-            self.shard(self.rows.place), self.target.at[0], self.local_sem
-        )
-
-    def out(self, step):
+            self.shards.at[self.layer, self.rows.place // self.copies],
+            self.target.at[0],
+            self.local_sem,
+        )
+
+    def lanes(self, part):
+        return pl.ds(pl.multiple_of(part * self.width, self.width), self.width)
+
+    def out(self, step, part):
         place = self.rows.ahead(step)
         return send_to(
-            self.shard(place),
-            self.target.at[step],
+            self.shards.at[self.layer, place // self.copies, :, self.lanes(part)],
+            self.target.at[step, :, self.lanes(part)],
             self.remote_sems,
-            step - 1,
+            (part, step - 1),
             self.rows.device_of(place),
         )
 
     def start(self):
-        for there, place in far_first(self.rows):
-            step = lax.rem(place - self.rows.place + self.rows.count, self.rows.count)
-
-            @pl.when(there)
-            def _():
-                self.out(step).start()
-
         self.own().start()
+
+        def one_part(part, carry):
+            for there, place in far_first(self.rows):
+                step = lax.rem(place - self.rows.place + self.rows.count, self.rows.count)
+
+                @pl.when(there)
+                def _():
+                    self.out(step, part).start()
+
+            return carry
+
+        lax.fori_loop(0, self.parts, one_part, 0)
+
+    def wait_part(self, part):
+        for step in range(1, self.rows.count):
+            landed = self.target.at[step, :, self.lanes(part)]
+            place = self.rows.behind(step)
+            send_to(
+                landed, landed, self.remote_sems, (part, step - 1), self.rows.device_of(place)
+            ).wait_recv()
 
     def wait_recv(self):
         self.own().wait()
-        for step in range(1, self.rows.count):
-            landed = self.target.at[step]
-            place = self.rows.behind(step)
-            send_to(
-                landed, landed, self.remote_sems, step - 1, self.rows.device_of(place)
-            ).wait_recv()
+        for part in range(self.parts):
+            self.wait_part(part)
 
     def wait_send(self):
-        for step in range(1, self.rows.count):
-            self.out(step).wait_send()
+        for part in range(self.parts):
+            for step in range(1, self.rows.count):
+                self.out(step, part).wait_send()
+
+
+def line_sems(row_count):
+    return [pltpu.SemaphoreType.DMA((max(row_count - 1, 1),))] * 2 + [pltpu.SemaphoreType.DMA]
 
 
 def all_rows(row_count):
@@ -426,12 +446,8 @@
     refs = refs[6:]
     next_blocks = refs[: 2 if gather_dims else 0]
     refs = refs[len(next_blocks) :]
-    closing_in = refs[: 1 if closing else 0]
-    refs = refs[len(closing_in) :]
     sum_ref, gates_ref, slots_out, returned_out = refs[:4]
     refs = refs[4:]
-    closing_out = refs[: len(closing_in)]
-    refs = refs[len(closing_in) :]
     moved_out = refs[: len(moving)]
     refs = refs[len(moving) :]
     next_full = refs[: len(next_blocks)]
@@ -441,10 +457,6 @@
         count = len(DenseGather.sems(gather_dims, 2))
         dense = DenseGather(gather_dims, next_blocks, next_full, refs[-count:])
         refs = refs[:-count]
-    closing_sems = ()
-    if closing:
-        closing_sems = refs[-4:]
-        refs = refs[:-4]
     move_sems = refs[len(refs) - 3 * len(moving) :]
     refs = refs[: len(refs) - 3 * len(moving)]
     (
@@ -500,12 +512,6 @@
         lambda place, step, chunk: returned.at[slot_part(place), chunk],
     )
     home = LineSum(rows, tokens, token_part, landed, (home_send, home_recv))
-    ahead = None
-    if closing:
-        ahead = LineGather(rows, *closing_in, *closing_out, token_part, closing_sems[:3])
-        ahead_own = pltpu.make_async_copy(
-            closing_in[0], closing_out[0].at[token_part(rows.place), :], closing_sems[3]
-        )
     weights = (gate, up, down)
     moves = {
         kind: WeightMove(
@@ -515,6 +521,7 @@
             weight_in[kind],
             weights[kind],
             move_sems[3 * number : 3 * number + 3],
+            chunks if kind == 2 else 1,
         )
         for number, kind in enumerate(moving)
     }
@@ -525,16 +532,21 @@
     }
     keeps = []
 
+    def keep_weight(kind):
+        keep = pltpu.make_async_copy(
+            weights[kind], moved_out[moving.index(kind)], local_sem.at[2 + kind]
+        )
+        keep.start()
+        keeps.append(keep)
+
     def weight_ready(kind):
         if kind in loads:
             loads[kind].wait()
+        elif kind == 2:
+            moves[kind].own().wait()
         else:
             moves[kind].wait_recv()
-            keep = pltpu.make_async_copy(
-                weights[kind], moved_out[moving.index(kind)], local_sem.at[2 + kind]
-            )
-            keep.start()
-            keeps.append(keep)
+            keep_weight(kind)
 
     def weight(kind, chunk):
         return weights[kind][:, :, chunk].reshape(-1, width)
@@ -616,11 +628,9 @@
         for kind in dense.kinds:
             dense.pass_rows(kind)
     weight_ready(2)
-    if ahead:
-        ahead_own.start()
-        over_chunks(chunks, width, ahead.start_own)
-
     def give_back(index, chunk):
+        if 2 in moves:
+            moves[2].wait_part(index)
         there.wait_send(index, chunk)
 
         def rows_of(part):
@@ -631,6 +641,8 @@
         returned[slot_part(cols.place), chunk] = send[slot_part(cols.place), chunk]
 
     over_chunks(chunks, width, give_back)
+    if 2 in moves:
+        keep_weight(2)
 
     over_chunks(chunks, width, gather.wait_send)
 
@@ -641,8 +653,7 @@
             tokens[part, chunk] = dot_nn(place_t[part, :], returned[:, chunk]).astype(jnp.bfloat16)
 
         over_blocks(all_tokens, token_rows, rows_of)
-        if ahead:
-            ahead.arrive(index, chunk)
+        if closing:
             return
         pl.when(~home.is_middle())(functools.partial(home.pass_on, index, chunk))
 
@@ -652,7 +663,7 @@
             home.pass_on(index - 1, before)
 
     over_chunks(chunks, width, combine)
-    if ahead:
+    if closing:
         keep_mixed = pltpu.make_async_copy(tokens, sum_ref, local_sem.at[5])
         keep_mixed.start()
     else:
@@ -667,12 +678,13 @@
     def finish(index, chunk):
         home.total(index, chunk, sum_ref)
 
-    if not ahead:
+    if not closing:
         over_chunks(chunks, width, finish)
 
     def drain(index, chunk):
         back.wait_send(index, chunk)
-        (ahead or home).wait_send(index, chunk)
+        if not closing:
+            home.wait_send(index, chunk)
 
     over_chunks(chunks, width, drain)
     if dense:
@@ -680,8 +692,7 @@
             dense.finish(kind)
     for kind in moving:
         moves[kind].wait_send()
-    if ahead:
-        ahead_own.wait()
+    if closing:
         keep_mixed.wait()
     keep_slots.wait()
     keep_returned.wait()
@@ -828,12 +839,8 @@
         lambda place, step, chunk: pair_landed.at[step - 1],
     )
     greet((all_rows(block_count), cols))
-    if before:
-        load_tokens = pltpu.make_async_copy(own_ref, tokens, local_sem.at[7])
-        load_tokens.start()
-    else:
-        for index in range(min(2, chunks)):
-            gather.start_own(index, pl.ds(index * width, width))
+    for index in range(min(2, chunks)):
+        gather.start_own(index, pl.ds(index * width, width))
     load_returned = pltpu.make_async_copy(returned_in, returned, local_sem.at[1])
     load_returned.start()
     load_slots = pltpu.make_async_copy(slots_in, slots, local_sem.at[0])
@@ -849,8 +856,7 @@
     def weight_part(kind, chunk):
         return weights[kind][:, :, chunk].reshape(block_count * slice_width, width)
 
-    if not before:
-        tokens[token_part(rows.place), :] = own_ref[...]
+    tokens[token_part(rows.place), :] = own_ref[...]
     build_places(dims, rows, routes_ref, place, place_t, None)
 
     def recompute(part):
@@ -878,20 +884,16 @@
         over_blocks(all_slots, slot_step, recompute)
 
     over_blocks(all_slots, slot_step, slot_gates)
-    if before:
-        load_tokens.wait()
-    else:
-        recompute_all()
+    recompute_all()
     load_returned.wait()
 
     def dispatch(index, chunk):
-        if not before:
-            gather.arrive(index, chunk)
-
-            @pl.when(index + 2 < chunks)
-            def _():
-                later = pl.ds(pl.multiple_of((index + 2) * width, width), width)
-                gather.start_own(index + 2, later)
+        gather.arrive(index, chunk)
+
+        @pl.when(index + 2 < chunks)
+        def _():
+            later = pl.ds(pl.multiple_of((index + 2) * width, width), width)
+            gather.start_own(index + 2, later)
 
 
         def rows_of(part):
@@ -924,6 +926,7 @@
         low = (spread - high.astype(jnp.float32)).astype(jnp.bfloat16)
         pair_send[part, :] = dot_nn(place_t[part, :], high) + dot_nn(place_t[part, :], low)
 
+    over_chunks(chunks, width, gather.wait_send)
     if before:
         load_mixed = pltpu.make_async_copy(opening_in[0], tokens, local_sem.at[7])
         load_mixed.start()
@@ -936,11 +939,8 @@
         def _():
             over_chunks(chunks, width, before.pass_on)
 
-        recompute_all()
 
     def project(index, chunk):
-        if before:
-            pl.when(before.is_middle())(functools.partial(before.pass_on, index, chunk))
         there.wait_recv(index, chunk)
 
         def rows_of(part):
@@ -981,13 +981,15 @@
 
     returned[slot_part(cols.place), :] = send[slot_part(cols.place), :]
     if before:
+
+        @pl.when(before.is_middle())
+        def _():
+            over_chunks(chunks, width, before.pass_on)
+
         over_chunks(
             chunks, width, lambda index, chunk: before.total(index, chunk, opening_out[0])
         )
         over_chunks(chunks, width, before.wait_send)
-
-    if not before:
-        over_chunks(chunks, width, gather.wait_send)
 
     def combine(index, chunk):
         back.wait_recv(index, chunk)
@@ -1067,20 +1069,19 @@
     weight_array = pltpu.VMEM((row_count, slice_width, model_width), jnp.bfloat16)
     return pl.pallas_call(
         functools.partial(
-            moe_forward_kernel, dims, row_count, layer, moving, gather_dims, bool(closing)
+            moe_forward_kernel, dims, row_count, layer, moving, gather_dims, closing
         ),
         out_shape=(
             every_row if closing else jax.ShapeDtypeStruct((token_rows, model_width), jnp.float32),
             jax.ShapeDtypeStruct((all_tokens, E), jnp.float32),
             jax.ShapeDtypeStruct((all_slots, model_width), jnp.bfloat16),
             jax.ShapeDtypeStruct((all_slots, model_width), jnp.bfloat16),
-            *([every_row] * len(closing)),
             *(moved_shape(row_count, weights[kind]) for kind in moving),
             *(gathered_shapes(gather_dims, next_blocks) if next_blocks else ()),
         ),
-        in_specs=[vmem] * 3 + [outside] * (3 + len(next_blocks) + len(closing)),
+        in_specs=[vmem] * 3 + [outside] * (3 + len(next_blocks)),
         out_specs=(outside if closing else vmem, vmem)
-        + (outside,) * (2 + len(closing) + len(moving) + len(next_blocks)),
+        + (outside,) * (2 + len(moving) + len(next_blocks)),
         scratch_shapes=[
             pltpu.VMEM((all_slots, all_tokens), jnp.bfloat16),
             pltpu.VMEM((all_tokens, all_slots), jnp.bfloat16),
@@ -1101,8 +1102,11 @@
             *exchange_sems(chunks, col_count),
             *LineSum.sems(chunks, group_rows),
             pltpu.SemaphoreType.DMA((6,)),
-            *(WeightMove.sems(row_count) * len(moving)),
-            *((*LineGather.sems(chunks, group_rows), pltpu.SemaphoreType.DMA) if closing else ()),
+            *(
+                sem
+                for kind in moving
+                for sem in WeightMove.sems(row_count, chunks if kind == 2 else 1)
+            ),
             *dense_sems,
         ],
         compiler_params=pltpu.CompilerParams(
@@ -1110,7 +1114,7 @@
         ),
         cost_estimate=no_cost,
         name="moe_forward",
-    )(own, routes, router, *weights, *next_blocks, *closing)
+    )(own, routes, router, *weights, *next_blocks)
 
 
 def moe_backward(dims, own, routes, router, gates, normed, slots, returned, weights, opening, dense):
@@ -1135,8 +1139,7 @@
             *(jax.ShapeDtypeStruct(block.shape[1:], jnp.float32) for block in dense),
             *([jax.ShapeDtypeStruct((token_rows, model_width), jnp.float32)] * opened),
         ),
-        in_specs=[outside if opening else vmem]
-        + [vmem] * 4
+        in_specs=[vmem] * 5
         + [outside] * (5 + opened + len(dense)),
         out_specs=(vmem, vmem)
         + (outside,) * block_count
@@ -1185,7 +1188,7 @@
                 for item in (
                     pltpu.VMEM((max(block_count - 1, 1), *block.shape[1:]), jnp.bfloat16),
                     pltpu.VMEM(block.shape[1:], jnp.bfloat16),
-                    *WeightMove.sems(block_count),
+                    *line_sems(block_count),
                 )
             ),
         ],
@@ -2182,7 +2185,7 @@
         next_blocks = ()
         if layer_index + 1 < layer_count:
             next_blocks = (w_qkv[layer_index + 1].T, w_out[layer_index + 1].T)
-        closing = (cotangent,) if layer_index + 1 == layer_count else ()
+        closing = layer_index + 1 == layer_count
         mixed, gates, slots, returned, *rest = moe_forward(
             dims,
             row_count,
@@ -2196,7 +2199,7 @@
             closing,
         )
         if closing:
-            closing = (rest.pop(0), mixed)
+            left_sum = (mixed,)
         for kind, moved in zip(moving, rest):
             weights[kind] = moved
         experts.append(weights)
@@ -2218,7 +2221,7 @@
         gates, slots, returned = saved[layer_index][8:]
         grad_moe, grad_router, *rest = moe_backward(
             dims,
-            closing[0] if closing else incoming.astype(narrow_type),
+            incoming.astype(narrow_type),
             routes_all[:, layer_index],
             routers[layer_index],
             gates,
@@ -2226,15 +2229,15 @@
             slots,
             returned,
             experts[layer_index],
-            closing[1:],
+            left_sum,
             part_sums,
         )
         if part_sums:
             dense_results[layer_index + 1] = rest[row_count : row_count + 3]
             del rest[row_count : row_count + 3]
-        if closing:
+        if left_sum:
             hidden = mid + rest.pop()
-            closing = ()
+            left_sum = ()
         if layer_index + 1 < layer_count:
             grad_moe, expert_results[layer_index + 1] = lax.optimization_barrier(
                 (grad_moe, expert_results[layer_index + 1])

time: 1380 us -> 1350 us (0.978)
  Pallas kernels: 1300 us -> 1280 us
    pallas_call x2, Pallas kernels: 457 us -> 396 us  [moe_forward(): pl.pallas_call(functools.partial(moe_forward_kernel, dims, row_count, lay...]
    pallas_call x2, Pallas kernels: 351 us -> 398 us  [moe_backward(): pl.pallas_call(functools.partial(moe_backward_kernel, dims, bool(opening)...]
where the time goes in v5:
time: 1350 us; the launch traced here: 1340 us
  Pallas kernels  1280 us (95%)
  other arithmetic  19.3 us (1%)
  starting transfers between devices  18.1 us (1%)
  local copies, waits for them, and re-layouts  16.4 us (1%)
    pallas_call x2, Pallas kernels, moe_backward(): pl.pallas_call(functools.partial(moe_backward_kernel, dims, bool(opening)...  398 us
    pallas_call x2, Pallas kernels, moe_forward(): pl.pallas_call(functools.partial(moe_forward_kernel, dims, row_count, lay...  396 us
    pallas_call x2, Pallas kernels, reduce_dense(): pl.pallas_call(functools.partial(reduce_dense_kernel, (row_count, pair_co...  179 us
    pallas_call x2, Pallas kernels, attend_forward(): pl.pallas_call(functools.partial(attend_forward_kernel, (col_count, row_c...  110 us
    pallas_call x2, Pallas kernels, attend_backward(): pl.pallas_call(functools.partial(attend_backward_kernel, (col_count, HEAD...  99.7 us
    pallas_call x1, Pallas kernels, gather_dense(): pl.pallas_call(functools.partial(gather_dense_kernel, dims, copies), out_...  84 us
  transfers between devices with their start and end apart: 6, of which 0 were waited for; matrix products, arithmetic and copies ran while one was open for 1% of the time, Pallas kernels for 34%

profile of v5, /device:TPU:30, one launch (start us, length us, event | category | flops | bytes accessed | tf_op | source)
XLA Modules:
  0.0 1336.8 jit_solution(14602599405576263161)
XLA Ops:
  0.7 1.1 fusion.9
  1.8 0.8 copy.39
  2.6 1.7 slice_bitcast_fusion
  4.3 0.7 reshape.109.router_ref
  5.0 0.6 reshape.108.routes_ref
  5.6 84.0 %gather_dense.1 = (bf16[4,2048,384]{2,1,0:T(8,128)(2,1)}, bf16[4,1536,384]{2,1,0:T(8,128)(2,1)}, s32[4,16,128]{2,1,0:T(8,128)}, bf16[4,192,128]{2,1,0:T(8,128)(2,1)}, bf16[4,192,1536]{2,1,0:T(8,128)(2,1)}) custom-call(bf16[256,384]{1,0:T(8,128)(2,1)} %bitcast.99, bf16[192,384]{1,0:T(8,128)(2,1)} %get-tuple-element.185.out_ref, ...), custom_call_target="tpu_custom_call" | custom-call | tf_op jit(solution)/shard_map/gather_dense/pallas_call | solution.py:1645
  89.6 1.1 reshape_reshape.7
  90.7 0.2 copy.58
  91.1 0.4 fusion.5
  91.5 0.7 copy.60
  92.1 1.3 convert_element_type.30.x_ref
  93.5 0.6 slice_bitcast_fusion.2
  94.1 0.8 copy.41
  94.9 0.7 copy.59
  95.6 0.5 fusion.8
  96.1 0.6 fusion.11
  96.8 0.8 pad_maximum_fusion.2
  97.6 54.0 %attend_forward.2 = (f32[256,1536]{1,0:T(8,128)}, bf16[256,1536]{1,0:T(8,128)(2,1)}, bf16[256,1536]{1,0:T(8,128)(2,1)}, bf16[2048,512]{1,0:T(8,128)(2,1)}, bf16[...) custom-call(f32[256,1536]{1,0:T(8,128)} %convert_element_type.30.x_ref,, ...), custom_call_target="tpu_custom_call" | custom-call | tf_op jit(solution)/shard_map/attend_forward/pallas_call | solution.py:1865
  151.6 222.3 %moe_forward.2 = (f32[256,1536]{1,0:T(8,128)}, f32[1024,32]{1,0:T(8,128)}, bf16[1152,1536]{1,0:T(8,128)(2,1)}, bf16[1152,1536]{1,0:T(8,128)(2,1)}, bf16[4,192,15...) custom-call(bf16[256,1536]{1,0:T(8,128)(2,1)} %get-tuple-element.100.refs_0_.refs_4_, ...), custom_call_target="tpu_custom_call" | custom-call | tf_op jit(solution)/shard_map/moe_forward/pallas_call | solution.py:1070
  373.9 2.7 add.38.x_ref
  376.6 55.6 %attend_forward.3 = (f32[256,1536]{1,0:T(8,128)}, bf16[256,1536]{1,0:T(8,128)(2,1)}, bf16[256,1536]{1,0:T(8,128)(2,1)}, bf16[2048,512]{1,0:T(8,128)(2,1)}, bf16[...) custom-call(f32[256,1536]{1,0:T(8,128)} %add.38.x_ref, ...), custom_call_target="tpu_custom_call" | custom-call | tf_op jit(solution)/shard_map/attend_forward/pallas_call | solution.py:1865
  432.3 173.3 %moe_forward.3 = (bf16[1024,1536]{1,0:T(8,128)(2,1)}, f32[1024,32]{1,0:T(8,128)}, bf16[1152,1536]{1,0:T(8,128)(2,1)}, bf16[1152,1536]{1,0:T(8,128)(2,1)}, bf16[4...) custom-call(bf16[256,1536]{1,0:T(8,128)(2,1)} %get-tuple-element.109.refs_0_.refs_4_, ...), custom_call_target="tpu_custom_call" | custom-call | tf_op jit(solution)/shard_map/moe_forward/pallas_call | solution.py:1070
  605.6 232.4 %moe_backward.2 = (f32[256,1536]{1,0:T(8,128)}, f32[32,1536]{1,0:T(8,128)}, bf16[3,192,1536]{2,1,0:T(8,128)(2,1)}, bf16[3,192,1536]{2,1,0:T(8,128)(2,1)}, bf16[3...) custom-call(bf16[256,1536]{1,0:T(8,128)(2,1)} %refs_0_, ...), custom_call_target="tpu_custom_call" | custom-call | tf_op jit(solution)/shard_map/moe_backward/pallas_call | solution.py:1133
  838.1 0.1 collective-permute-start.1
  838.1 3.7 collective-permute-start.2
  841.9 1.3 convert_element_type.34.incoming_ref
  843.2 49.8 %attend_backward.2 = (f32[256,1536]{1,0:T(8,128)}, bf16[256,1536]{1,0:T(8,128)(2,1)}, bf16[256,2048]{1,0:T(8,128)(2,1)}, f32[1,1536]{1,0:T(1,128)}, f32[1,1536]{1,0:T(1,128)}) custom-call(f32[256,1536]{1,0:T(8,128)} %convert_element_type.34.incoming_ref, f32[256,1536]{1,0:T(8,128)} %get-tuple-element.118.grad_moe_ref, ...), custom_call_target="tpu_custom_call" | custom-call | tf_op jit(solution)/shard_map/attend_backward/pallas_call | solution.py:2032
  893.0 0.7 convert_reduce_fusion.3
  893.7 0.1 concatenate.37
  893.8 0.7 convert_reduce_fusion.2
  894.5 0.1 concatenate.38
  894.6 0.1 copy.57
  894.8 0.2 fusion.3
  895.0 0.2 concatenate.36
  895.3 0.1 copy.34
  895.4 0.2 reshape.113
  895.6 0.7 copy_bitcast_fusion.6.small_ref
  896.3 75.8 %reduce_dense.2 = (bf16[4,384,256]{2,1,0:T(8,128)(2,1)}, bf16[4,192,384]{2,1,0:T(8,128)(2,1)}, bf16[4,16,128]{2,1,0:T(8,128)(2,1)}) custom-call(bf16[256,1536]{1,0:T(8,128)(2,1)} %get-tuple-element.124.normed_ref, bf16[256,2048]{1,0:T(8,128)(2,1)} %get-tuple-element.125.grad_proj_ref, bf16[256,1536]{1,0:T(8,128)(2,1)} %get-tuple-element.126.grad_mid_ref, ...), custom_call_target="tpu_custom_call" | custom-call | tf_op jit(solution)/shard_map/reduce_dense/pallas_call | solution.py:1417
  972.1 1.0 convert_element_type.35.refs_0_
  973.1 165.3 %moe_backward.3 = (f32[256,1536]{1,0:T(8,128)}, f32[32,1536]{1,0:T(8,128)}, bf16[3,192,1536]{2,1,0:T(8,128)(2,1)}, bf16[3,192,1536]{2,1,0:T(8,128)(2,1)}, bf16[3...) custom-call(bf16[256,1536]{1,0:T(8,128)(2,1)} %convert_element_type., ...), custom_call_target="tpu_custom_call" | custom-call | tf_op jit(solution)/shard_map/moe_backward/pallas_call | solution.py:1133
  1138.4 11.8 collective-permute-start.3
  1150.2 2.4 collective-permute-start.5
  1152.7 1.1 copy.56
  1153.7 0.2 fusion.1
  1153.9 0.2 concatenate.40
  1154.2 0.8 reshape.121
  1155.0 2.8 add.39
  1157.8 7.9 order_grads.2
  1165.7 49.9 %attend_backward.3 = (f32[256,1536]{1,0:T(8,128)}, bf16[256,1536]{1,0:T(8,128)(2,1)}, bf16[256,2048]{1,0:T(8,128)(2,1)}, f32[1,1536]{1,0:T(1,128)}, f32[1,1536]{1,0:T(1,128)}) custom-call(f32[256,1536]{1,0:T(8,128)} %get-tuple-element.133.incoming_ref, f32[256,1536]{1,0:T(8,128)} %get-tuple-element.146.grad_moe_ref, f32[256,1536]{1,0:T(8,128)} %get-tuple-element.99.mid_ref, ...), custom_call_target="tpu_custom_call" | custom-call | tf_op jit(solution)/shard_map/attend_backward/pallas_call | solution.py:2032
  1215.6 0.7 convert_reduce_fusion.1
  1216.3 0.1 concatenate.41
  1216.4 0.7 convert_reduce_fusion
  1217.1 0.1 concatenate.42
  1217.3 0.1 copy.37
  1217.4 0.2 reshape.116
  1217.6 0.7 copy_bitcast_fusion.5.small_ref
  1218.3 103.3 %reduce_dense.3 = (f32[384,256]{1,0:T(8,128)}, f32[192,384]{1,0:T(8,128)}, f32[16,128]{1,0:T(8,128)}) custom-call(bf16[256,1536]{1,0:T(8,128)(2,1)} %get-tuple-element.152.normed_ref, bf16[256,2048]{1,0:T(8,128)(2,1)} %get-tuple-element.153.grad_proj_ref, bf16[256,1536]{1,0:T(8,128)(2,1)} %get-tuple-element.162.grad_mid_ref, ...), custom_call_target="tpu_custom_call" | custom-call | tf_op jit(solution)/shard_map/reduce_dense/pallas_call | solution.py:1417
  1321.6 0.8 reshape.119
  1322.4 0.6 pad_maximum_fusion.5
  1323.0 0.6 pad_maximum_fusion.4
  1323.6 1.8 pad_maximum_fusion.1
  1325.4 1.9 pad_maximum_fusion
  1327.4 8.1 order_grads.3
  1335.5 1.1 copy.65
  (46 shorter events, 0.5 us)
Async XLA Ops:
  0.6 3.7 copy-start.9
  0.7 4.3 copy-start.13
  89.6 2.5 copy-start.5
  91.0 2.5 copy-start.10
  92.1 4.0 copy-start.11
  92.1 4.0 copy-start.12
  151.6 222.3 %copy-start = (f32[256,1536]{1,0:T(8,128)S(1)}, f32[256,1536]{1,0:T(8,128)}, u32[]{:S(2)}) copy-start(f32[256,1536]{1,0:T(8,128)} %get-tuple-element.99.mid_ref) | copy-start | bytes 4718596
  605.6 236.3 %copy-start.3 = (bf16[256,1536]{1,0:T(8,128)(2,1)S(1)}, bf16[256,1536]{1,0:T(8,128)(2,1)}, u32[]{:S(2)}) copy-start(bf16[256,1536]{1,0:T(8,128)(2,1)} %refs_0_) | copy-start | bytes 2359300
  838.0 312.2 %collective-permute-start = (bf16[3,192,1536]{2,1,0:T(8,128)(2,1)}, bf16[3,192,1536]{2,1,0:T(8,128)(2,1)}, u32[]{:S(2)}, u32[]{:S(2)}) collective-permute-start(bf16[3,192,1536]{2,1,0:T(8,128)(2,1)} %get-tuple-element.143), channel_id=1, source_target_pairs={{0,24},{8,0},{16,8},{24,16},{1,25},{9,1},{17,9},{25,17},{2,26},{10... | collective-permute-start | bytes 5308424 | tf_op jit(solution)/shard_map/ppermute | solution.py:2120
  838.1 319.7 %collective-permute-start.1 = (bf16[3,192,1536]{2,1,0:T(8,128)(2,1)}, bf16[3,192,1536]{2,1,0:T(8,128)(2,1)}, u32[]{:S(2)}, u32[]{:S(2)}) collective-permute-start(bf16[3,192,1536]{2,1,0:T(8,128)(2,1)} %get-tuple-element.144), channel_id=1, source_target_pairs={{0,16},{8,24},{16,0},{24,8},{1,17},{9,25},{17,1},{25,9},{2,18},{10... | collective-permute-start | bytes 5308424 | tf_op jit(solution)/shard_map/ppermute | solution.py:2120
  838.1 319.6 %collective-permute-start.2 = (bf16[3,192,1536]{2,1,0:T(8,128)(2,1)}, bf16[3,192,1536]{2,1,0:T(8,128)(2,1)}, u32[]{:S(2)}, u32[]{:S(2)}) collective-permute-start(bf16[3,192,1536]{2,1,0:T(8,128)(2,1)} %get-tuple-element.145), channel_id=1, source_target_pairs={{0,8},{8,16},{16,24},{24,0},{1,9},{9,17},{17,25},{25,1},{2,10},{10... | collective-permute-start | bytes 5308424 | tf_op jit(solution)/shard_map/ppermute | solution.py:2120
  843.2 51.4 %copy-start.8 = (f32[32,1536]{1,0:T(8,128)S(1)}, f32[32,1536]{1,0:T(8,128)}, u32[]{:S(2)}) copy-start(f32[32,1536]{1,0:T(8,128)} %get-tuple-element.127) | copy-start | bytes 589828
  896.3 75.8 %copy-start.2 = (f32[256,1536]{1,0:T(8,128)S(1)}, f32[256,1536]{1,0:T(8,128)}, u32[]{:S(2)}) copy-start(f32[256,1536]{1,0:T(8,128)} %get-tuple-element.133.incoming_ref) | copy-start | bytes 4718596
  973.1 181.9 %copy-start.1 = (f32[256,1536]{1,0:T(8,128)S(1)}, f32[256,1536]{1,0:T(8,128)}, u32[]{:S(2)}) copy-start(f32[256,1536]{1,0:T(8,128)} %get-tuple-element.108.mid_ref) | copy-start | bytes 4718596
  1138.4 189.0 %collective-permute-start.3 = (bf16[3,192,1536]{2,1,0:T(8,128)(2,1)}, bf16[3,192,1536]{2,1,0:T(8,128)(2,1)}, u32[]{:S(2)}, u32[]{:S(2)}) collective-permute-start(bf16[3,192,1536]{2,1,0:T(8,128)(2,1)} %get-tuple-element.173), channel_id=1, source_target_pairs={{0,24},{8,0},{16,8},{24,16},{1,25},{9,1},{17,9},{25,17},{2,26},{10... | collective-permute-start | bytes 5308424 | tf_op jit(solution)/shard_map/ppermute | solution.py:2120
  1150.2 177.1 %collective-permute-start.4 = (bf16[3,192,1536]{2,1,0:T(8,128)(2,1)}, bf16[3,192,1536]{2,1,0:T(8,128)(2,1)}, u32[]{:S(2)}, u32[]{:S(2)}) collective-permute-start(bf16[3,192,1536]{2,1,0:T(8,128)(2,1)} %get-tuple-element.174), channel_id=1, source_target_pairs={{0,16},{8,24},{16,0},{24,8},{1,17},{9,25},{17,1},{25,9},{2,18},{10... | collective-permute-start | bytes 5308424 | tf_op jit(solution)/shard_map/ppermute | solution.py:2120
  1150.2 177.1 %collective-permute-start.5 = (bf16[3,192,1536]{2,1,0:T(8,128)(2,1)}, bf16[3,192,1536]{2,1,0:T(8,128)(2,1)}, u32[]{:S(2)}, u32[]{:S(2)}) collective-permute-start(bf16[3,192,1536]{2,1,0:T(8,128)(2,1)} %get-tuple-element.175), channel_id=1, source_target_pairs={{0,8},{8,16},{16,24},{24,0},{1,9},{9,17},{17,25},{25,1},{2,10},{10... | collective-permute-start | bytes 5308424 | tf_op jit(solution)/shard_map/ppermute | solution.py:2120
  1218.3 105.3 %copy-start.7 = (f32[192,384]{1,0:T(8,128)S(1)}, f32[192,384]{1,0:T(8,128)}, u32[]{:S(2)}) copy-start(f32[192,384]{1,0:T(8,128)} %get-tuple-element.171) | copy-start | bytes 884740
  1218.3 107.1 %copy-start.6 = (f32[384,256]{1,0:T(8,128)S(1)}, f32[384,256]{1,0:T(8,128)}, u32[]{:S(2)}) copy-start(f32[384,256]{1,0:T(8,128)} %get-tuple-element.169) | copy-start | bytes 1179652
  1327.4 8.1 copy-start.4

commit v6 on v5

--- a/solution.py
+++ b/solution.py
@@ -444,6 +444,8 @@
     own_ref, routes_ref, router_ref = refs[:3]
     weight_in = refs[3:6]
     refs = refs[6:]
+    mid_in = refs[: 0 if closing else 1]
+    refs = refs[len(mid_in) :]
     next_blocks = refs[: 2 if gather_dims else 0]
     refs = refs[len(next_blocks) :]
     sum_ref, gates_ref, slots_out, returned_out = refs[:4]
@@ -677,6 +679,7 @@
 
     def finish(index, chunk):
         home.total(index, chunk, sum_ref)
+        sum_ref[:, chunk] += mid_in[0][:, chunk]
 
     if not closing:
         over_chunks(chunks, width, finish)
@@ -762,8 +765,8 @@
     refs = refs[len(opening_in) :]
     opening_scratch = ()
     if opening:
-        opening_scratch = refs[-3:]
-        refs = refs[:-3]
+        opening_scratch = refs[-4:]
+        refs = refs[:-4]
     (
         place,
         place_t,
@@ -772,7 +775,6 @@
         down,
         tokens,
         send,
-        slots,
         slope,
         silu,
         act,
@@ -830,7 +832,8 @@
     home = LineSum(rows, tokens, token_part, landed, (home_send, home_recv))
     before = None
     if opening:
-        before = LineSum(rows, tokens, token_part, opening_scratch[0], opening_scratch[1:])
+        before = LineSum(rows, opening_scratch[0], token_part, opening_scratch[1], opening_scratch[2:])
+        load_mixed = pltpu.make_async_copy(opening_in[0], opening_scratch[0], local_sem.at[7])
     pair = Exchange(
         rows,
         pair_send_sem,
@@ -843,8 +846,10 @@
         gather.start_own(index, pl.ds(index * width, width))
     load_returned = pltpu.make_async_copy(returned_in, returned, local_sem.at[1])
     load_returned.start()
-    load_slots = pltpu.make_async_copy(slots_in, slots, local_sem.at[0])
+    load_slots = pltpu.make_async_copy(slots_in, send, local_sem.at[0])
     load_slots.start()
+    if before:
+        load_mixed.start()
     weights = (gate, up, down)
     loads = [
         pltpu.make_async_copy(weight_in[kind], weights[kind], local_sem.at[4 + kind])
@@ -860,8 +865,8 @@
     build_places(dims, rows, routes_ref, place, place_t, None)
 
     def recompute(part):
-        gate_val = dot_nt(slots[part, :], gate[...].reshape(-1, gate.shape[2]))
-        up_val = dot_nt(slots[part, :], up[...].reshape(-1, up.shape[2]))
+        gate_val = dot_nt(send[part, :], gate[...].reshape(-1, gate.shape[2]))
+        up_val = dot_nt(send[part, :], up[...].reshape(-1, up.shape[2]))
         sigmoid = jax.nn.sigmoid(gate_val)
         value = gate_val * sigmoid
         act[part, :] = (value * up_val).astype(jnp.bfloat16)
@@ -927,9 +932,6 @@
         pair_send[part, :] = dot_nn(place_t[part, :], high) + dot_nn(place_t[part, :], low)
 
     over_chunks(chunks, width, gather.wait_send)
-    if before:
-        load_mixed = pltpu.make_async_copy(opening_in[0], tokens, local_sem.at[7])
-        load_mixed.start()
     over_blocks(all_tokens, token_rows, pairs)
     pair.start(0, None)
     if before:
@@ -980,16 +982,12 @@
     over_chunks(chunks, width, give_back)
 
     returned[slot_part(cols.place), :] = send[slot_part(cols.place), :]
+
     if before:
 
         @pl.when(before.is_middle())
         def _():
             over_chunks(chunks, width, before.pass_on)
-
-        over_chunks(
-            chunks, width, lambda index, chunk: before.total(index, chunk, opening_out[0])
-        )
-        over_chunks(chunks, width, before.wait_send)
 
     def combine(index, chunk):
         back.wait_recv(index, chunk)
@@ -1008,12 +1006,17 @@
     over_chunks(chunks, width, combine)
     last_chunk = pl.ds((chunks - 1) * width, width)
     pl.when(home.is_middle())(functools.partial(home.pass_on, chunks - 1, last_chunk))
+    over_chunks(chunks, width, back.wait_send)
+    load_slots = pltpu.make_async_copy(slots_in, send, local_sem.at[0])
+    load_slots.start()
+    load_slots.wait()
+
     def keep(kind, index):
         return pltpu.make_async_copy(
             staged.at[index % 2], grads_out[index].at[kind], local_sem.at[2 + index % 2]
         )
 
-    for kind, (left, right) in enumerate(((grad_gate, slots), (grad_up, slots), (act, received))):
+    for kind, (left, right) in enumerate(((grad_gate, send), (grad_up, send), (act, received))):
         turned[...] = left[...].T
         for index in range(block_count):
             if index >= 2:
@@ -1040,9 +1043,13 @@
         sum_ref[:, chunk] += dot_nn(grad_logits, router_ref[:, chunk])
 
     over_chunks(chunks, width, finish)
+    if before:
+        over_chunks(
+            chunks, width, lambda index, chunk: before.total(index, chunk, opening_out[0])
+        )
+        over_chunks(chunks, width, before.wait_send)
 
     def drain(index, chunk):
-        back.wait_send(index, chunk)
         home.wait_send(index, chunk)
 
     over_chunks(chunks, width, drain)
@@ -1052,7 +1059,7 @@
 
 
 def moe_forward(
-    dims, row_count, layer, own, routes, router, weights, moving, next_blocks, closing
+    dims, row_count, layer, own, routes, router, weights, moving, next_blocks, closing, mid
 ):
     group_rows, col_count, copies, token_rows, slot_rows, chunks, width = dims
     all_tokens, all_slots = group_rows * token_rows, col_count * slot_rows
@@ -1079,7 +1086,7 @@
             *(moved_shape(row_count, weights[kind]) for kind in moving),
             *(gathered_shapes(gather_dims, next_blocks) if next_blocks else ()),
         ),
-        in_specs=[vmem] * 3 + [outside] * (3 + len(next_blocks)),
+        in_specs=[vmem] * 3 + [outside] * 3 + [vmem] * len(mid) + [outside] * len(next_blocks),
         out_specs=(outside if closing else vmem, vmem)
         + (outside,) * (2 + len(moving) + len(next_blocks)),
         scratch_shapes=[
@@ -1114,7 +1121,7 @@
         ),
         cost_estimate=no_cost,
         name="moe_forward",
-    )(own, routes, router, *weights, *next_blocks)
+    )(own, routes, router, *weights, *mid, *next_blocks)
 
 
 def moe_backward(dims, own, routes, router, gates, normed, slots, returned, weights, opening, dense):
@@ -1152,7 +1159,6 @@
             weight_array,
             pltpu.VMEM((all_tokens, model_width), jnp.bfloat16),
             slot_array,
-            slot_array,
             hidden_narrow,
             hidden_narrow,
             hidden_narrow,
@@ -1176,6 +1182,7 @@
             pltpu.SemaphoreType.DMA((8,)),
             *(
                 (
+                    pltpu.VMEM((all_tokens, model_width), jnp.bfloat16),
                     pltpu.VMEM((group_rows + 1, token_rows, model_width), jnp.bfloat16),
                     *LineSum.sems(chunks, group_rows),
                 )
@@ -1792,7 +1799,7 @@
     move = WeightMove(all_rows(row_count), copies, layer, shards_ref, moved, move_sems)
     greet((cols, move.rows))
     move.start()
-    x = x_ref[...]
+    x = x_ref[...].astype(jnp.float32)
     inverse = lax.rsqrt(jnp.mean(x * x, axis=-1, keepdims=True) + eps_norm)
     normed_ref[...] = (x * inverse * gain_attn_ref[...]).astype(jnp.bfloat16)
     proj[...] = pieces_nt(normed_ref[...], qkv_ref)
@@ -1830,7 +1837,7 @@
         lax.fori_loop(0, group, head_step, 0)
     keep = pltpu.make_async_copy(kv_all, kv_out, local_sem)
     keep.start()
-    mid = x_ref[...] + pieces_nt(attended_ref[...], out_w_ref)
+    mid = x_ref[...].astype(jnp.float32) + pieces_nt(attended_ref[...], out_w_ref)
     mid_ref[...] = mid
     inverse = lax.rsqrt(jnp.mean(mid * mid, axis=-1, keepdims=True) + eps_norm)
     normed_moe_ref[...] = (mid * inverse * gain_moe_ref[...]).astype(jnp.bfloat16)
@@ -2000,7 +2007,9 @@
     pieces = qkv_ref.shape[0]
     grad_normed = [dot_nn(grad_proj_ref[...], qkv_ref[index]) for index in range(pieces)]
     grad_normed = jnp.concatenate(grad_normed, axis=1) if pieces > 1 else grad_normed[0]
-    grad, gain_sum = norm_backward(x_ref[...], gain_attn_ref[...], grad_normed)
+    grad, gain_sum = norm_backward(
+        x_ref[...].astype(jnp.float32), gain_attn_ref[...], grad_normed
+    )
     grad_gain_attn_ref[...] = gain_sum
     grad_x_ref[...] += grad
     for head in range(KEY_VALUE_HEADS):
@@ -2050,7 +2059,7 @@
             *exchange_sems(KEY_VALUE_HEADS, col_count),
         ],
         compiler_params=pltpu.CompilerParams(
-            collective_id=6, has_side_effects=True, vmem_limit_bytes=vmem_most
+            collective_id=6 if x.dtype == jnp.float32 else 14, has_side_effects=True, vmem_limit_bytes=vmem_most
         ),
         cost_estimate=no_cost,
         name="attend_backward",
@@ -2161,7 +2170,7 @@
     ]
     gains_attn = norm_attn.astype(wide_type)[:, None, :]
     gains_moe = norm_moe.astype(wide_type)[:, None, :]
-    hidden = hidden_in.astype(wide_type)
+    hidden = hidden_in
     saved = []
     for layer_index in range(layer_count):
         early = 0 if layer_index else 1
@@ -2197,6 +2206,7 @@
             moving,
             next_blocks,
             closing,
+            () if closing else (mid,),
         )
         if closing:
             left_sum = (mixed,)
@@ -2210,7 +2220,7 @@
             + (gates, slots, returned)
         )
         if not closing:
-            hidden = mid + mixed
+            hidden = mixed
     incoming = cotangent.astype(wide_type)
     dense_results = [None] * layer_count
     expert_results = [None] * layer_count

time: 1350 us -> 1340 us (level)
  Pallas kernels: 1280 us -> 1260 us
  starting transfers between devices: 18.1 us -> 33.3 us
    pallas_call x2, Pallas kernels: 398 us -> 367 us  [moe_backward(): pl.pallas_call(functools.partial(moe_backward_kernel, dims, bool(opening)...]
    ppermute x6, starting transfers between devices: 18.1 us -> 33.3 us  [move_grads(): blocks.append(lax.ppermute(grads[step], 'row', pairs))]
  transfers between devices with their start and end apart: 6 -> 6, of which waited for: 0 -> 0; matrix products, arithmetic and copies ran while one was open for 1% -> 1% of each run, Pallas kernels for 34% -> 35%
where the time goes in v6:
time: 1340 us; the launch traced here: 1320 us
  Pallas kernels  1260 us (94%)
  starting transfers between devices  33.3 us (2%)
  local copies, waits for them, and re-layouts  17.8 us (1%)
  other arithmetic  15.2 us (1%)
    pallas_call x2, Pallas kernels, moe_forward(): pl.pallas_call(functools.partial(moe_forward_kernel, dims, row_count, lay...  396 us
    pallas_call x2, Pallas kernels, moe_backward(): pl.pallas_call(functools.partial(moe_backward_kernel, dims, bool(opening)...  367 us
    pallas_call x2, Pallas kernels, reduce_dense(): pl.pallas_call(functools.partial(reduce_dense_kernel, (row_count, pair_co...  177 us
    pallas_call x2, Pallas kernels, attend_forward(): pl.pallas_call(functools.partial(attend_forward_kernel, (col_count, row_c...  109 us
    pallas_call x2, Pallas kernels, attend_backward(): pl.pallas_call(functools.partial(attend_backward_kernel, (col_count, HEAD...  106 us
    pallas_call x1, Pallas kernels, gather_dense(): pl.pallas_call(functools.partial(gather_dense_kernel, dims, copies), out_...  84 us
    ppermute x6, starting transfers between devices, move_grads(): blocks.append(lax.ppermute(grads[step], 'row', pairs))  33.3 us
  transfers between devices with their start and end apart: 6, of which 0 were waited for; matrix products, arithmetic and copies ran while one was open for 1% of the time, Pallas kernels for 35%

profile of v6, /device:TPU:30, one launch (start us, length us, event | category | flops | bytes accessed | tf_op | source)
XLA Modules:
  0.0 1323.1 jit_solution(17719180713624387377)
XLA Ops:
  0.7 1.1 fusion.9
  1.7 0.8 copy.39
  2.6 1.7 slice_bitcast_fusion
  4.3 1.4 reshape.109.router_ref
  5.7 1.3 reshape.108.routes_ref
  7.0 84.0 %gather_dense.1 = (bf16[4,2048,384]{2,1,0:T(8,128)(2,1)}, bf16[4,1536,384]{2,1,0:T(8,128)(2,1)}, s32[4,16,128]{2,1,0:T(8,128)}, bf16[4,192,128]{2,1,0:T(8,128)(2,1)}, bf16[4,192,1536]{2,1,0:T(8,128)(2,1)}) custom-call(bf16[256,384]{1,0:T(8,128)(2,1)} %bitcast.99, bf16[192,384]{1,0:T(8,128)(2,1)} %get-tuple-element.185.out_ref, ...), custom_call_target="tpu_custom_call" | custom-call | tf_op jit(solution)/shard_map/gather_dense/pallas_call | solution.py:1652
  91.1 1.0 reshape_reshape.7
  92.2 0.2 copy.58
  92.3 0.1 fusion.10
  92.5 0.4 fusion.5
  92.9 0.7 copy.60
  93.6 0.6 slice_bitcast_fusion.2
  94.2 0.8 copy.41
  95.0 0.7 copy.59
  95.7 0.5 fusion.8
  96.2 0.6 fusion.11
  96.8 0.9 pad_maximum_fusion.2
  97.7 53.8 %attend_forward.2 = (f32[256,1536]{1,0:T(8,128)}, bf16[256,1536]{1,0:T(8,128)(2,1)}, bf16[256,1536]{1,0:T(8,128)(2,1)}, bf16[2048,512]{1,0:T(8,128)(2,1)}, bf16[...) custom-call(bf16[256,1536]{1,0:T(8,128)(2,1)} %x_ref.3, ...), custom_call_target="tpu_custom_call" | custom-call | tf_op jit(solution)/shard_map/attend_forward/pallas_call | solution.py:1872
  151.5 222.7 %moe_forward.2 = (f32[256,1536]{1,0:T(8,128)}, f32[1024,32]{1,0:T(8,128)}, bf16[1152,1536]{1,0:T(8,128)(2,1)}, bf16[1152,1536]{1,0:T(8,128)(2,1)}, bf16[4,192,15...) custom-call(bf16[256,1536]{1,0:T(8,128)(2,1)} %get-tuple-element.99.refs_0_.refs_4_, ...), custom_call_target="tpu_custom_call" | custom-call | tf_op jit(solution)/shard_map/moe_forward/pallas_call | solution.py:1077
  374.2 55.6 %attend_forward.3 = (f32[256,1536]{1,0:T(8,128)}, bf16[256,1536]{1,0:T(8,128)(2,1)}, bf16[256,1536]{1,0:T(8,128)(2,1)}, bf16[2048,512]{1,0:T(8,128)(2,1)}, bf16[...) custom-call(f32[256,1536]{1,0:T(8,128)} %get-tuple-element.105.x_ref, ...), custom_call_target="tpu_custom_call" | custom-call | tf_op jit(solution)/shard_map/attend_forward/pallas_call | solution.py:1872
  429.8 173.4 %moe_forward.3 = (bf16[1024,1536]{1,0:T(8,128)(2,1)}, f32[1024,32]{1,0:T(8,128)}, bf16[1152,1536]{1,0:T(8,128)(2,1)}, bf16[1152,1536]{1,0:T(8,128)(2,1)}, bf16[4...) custom-call(bf16[256,1536]{1,0:T(8,128)(2,1)} %get-tuple-element.109.refs_0_.refs_4_, ...), custom_call_target="tpu_custom_call" | custom-call | tf_op jit(solution)/shard_map/moe_forward/pallas_call | solution.py:1077
  603.2 196.2 %moe_backward.2 = (f32[256,1536]{1,0:T(8,128)}, f32[32,1536]{1,0:T(8,128)}, bf16[3,192,1536]{2,1,0:T(8,128)(2,1)}, bf16[3,192,1536]{2,1,0:T(8,128)(2,1)}, bf16[3...) custom-call(bf16[256,1536]{1,0:T(8,128)(2,1)} %refs_0_, ...), custom_call_target="tpu_custom_call" | custom-call | tf_op jit(solution)/shard_map/moe_backward/pallas_call | solution.py:1140
  799.3 14.1 %collective-permute-start = (bf16[3,192,1536]{2,1,0:T(8,128)(2,1)}, bf16[3,192,1536]{2,1,0:T(8,128)(2,1)}, u32[]{:S(2)}, u32[]{:S(2)}) collective-permute-start(bf16[3,192,1536]{2,1,0:T(8,128)(2,1)} %get-tuple-element.143), channel_id=1, source_target_pairs={{0,24},{8,0},{16,8},{24,16},{1,25},{9,1},{17,9},{25,17},{2,26},{10... | collective-permute-start | bytes 5308424 | tf_op jit(solution)/shard_map/ppermute | solution.py:2129
  813.4 2.4 collective-permute-start.2
  815.9 1.3 convert_element_type.30.incoming_ref
  817.2 50.2 %attend_backward.2 = (f32[256,1536]{1,0:T(8,128)}, bf16[256,1536]{1,0:T(8,128)(2,1)}, bf16[256,2048]{1,0:T(8,128)(2,1)}, f32[1,1536]{1,0:T(1,128)}, f32[1,1536]{1,0:T(1,128)}) custom-call(f32[256,1536]{1,0:T(8,128)} %convert_element_type.30.incoming_ref, f32[256,1536]{1,0:T(8,128)} %get-tuple-element.118.grad_moe_ref, ...), custom_call_target="tpu_custom_call" | custom-call | tf_op jit(solution)/shard_map/attend_backward/pallas_call | solution.py:2041
  867.4 0.7 convert_reduce_fusion.3
  868.1 0.1 concatenate.37
  868.2 0.7 convert_reduce_fusion.2
  869.0 0.1 concatenate.38
  869.1 0.1 copy.57
  869.2 0.2 fusion.3
  869.4 0.2 concatenate.36
  869.7 0.1 copy.34
  869.9 0.2 reshape.113
  870.1 0.7 copy_bitcast_fusion.6.small_ref
  870.8 75.7 %reduce_dense.2 = (bf16[4,384,256]{2,1,0:T(8,128)(2,1)}, bf16[4,192,384]{2,1,0:T(8,128)(2,1)}, bf16[4,16,128]{2,1,0:T(8,128)(2,1)}) custom-call(bf16[256,1536]{1,0:T(8,128)(2,1)} %get-tuple-element.124.normed_ref, bf16[256,2048]{1,0:T(8,128)(2,1)} %get-tuple-element.125.grad_proj_ref, bf16[256,1536]{1,0:T(8,128)(2,1)} %get-tuple-element.126.grad_mid_ref, ...), custom_call_target="tpu_custom_call" | custom-call | tf_op jit(solution)/shard_map/reduce_dense/pallas_call | solution.py:1424
  946.5 1.0 convert_element_type.31.refs_0_
  947.4 171.3 %moe_backward.3 = (f32[256,1536]{1,0:T(8,128)}, f32[32,1536]{1,0:T(8,128)}, bf16[3,192,1536]{2,1,0:T(8,128)(2,1)}, bf16[3,192,1536]{2,1,0:T(8,128)(2,1)}, bf16[3...) custom-call(bf16[256,1536]{1,0:T(8,128)(2,1)} %convert_element_type., ...), custom_call_target="tpu_custom_call" | custom-call | tf_op jit(solution)/shard_map/moe_backward/pallas_call | solution.py:1140
  1118.8 14.0 %collective-permute-start.3 = (bf16[3,192,1536]{2,1,0:T(8,128)(2,1)}, bf16[3,192,1536]{2,1,0:T(8,128)(2,1)}, u32[]{:S(2)}, u32[]{:S(2)}) collective-permute-start(bf16[3,192,1536]{2,1,0:T(8,128)(2,1)} %get-tuple-element.173), channel_id=1, source_target_pairs={{0,24},{8,0},{16,8},{24,16},{1,25},{9,1},{17,9},{25,17},{2,26},{10... | collective-permute-start | bytes 5308424 | tf_op jit(solution)/shard_map/ppermute | solution.py:2129
  1132.7 2.8 collective-permute-start.5
  1135.5 1.1 copy.56
  1136.6 0.2 fusion.1
  1136.8 0.2 concatenate.40
  1137.0 0.8 reshape.121
  1137.8 2.8 add.35
  1140.6 7.9 order_grads.2
  1148.6 55.8 %attend_backward.3 = (f32[256,1536]{1,0:T(8,128)}, bf16[256,1536]{1,0:T(8,128)(2,1)}, bf16[256,2048]{1,0:T(8,128)(2,1)}, f32[1,1536]{1,0:T(1,128)}, f32[1,1536]{1,0:T(1,128)}) custom-call(f32[256,1536]{1,0:T(8,128)} %get-tuple-element.133.incoming_ref, f32[256,1536]{1,0:T(8,128)} %get-tuple-element.146.grad_moe_ref, ...), custom_call_target="tpu_custom_call" | custom-call | tf_op jit(solution)/shard_map/attend_backward/pallas_call | solution.py:2041
  1204.4 0.7 convert_reduce_fusion.1
  1205.1 0.1 concatenate.41
  1205.2 0.7 convert_reduce_fusion
  1205.9 0.1 concatenate.42
  1206.0 0.1 maximum_bitcast_fusion.1
  1206.1 0.1 copy.37
  1206.2 0.2 reshape.116
  1206.4 0.7 copy_bitcast_fusion.5.small_ref
  1207.1 100.9 %reduce_dense.3 = (f32[384,256]{1,0:T(8,128)}, f32[192,384]{1,0:T(8,128)}, f32[16,128]{1,0:T(8,128)}) custom-call(bf16[256,1536]{1,0:T(8,128)(2,1)} %get-tuple-element.152.normed_ref, bf16[256,2048]{1,0:T(8,128)(2,1)} %get-tuple-element.153.grad_proj_ref, bf16[256,1536]{1,0:T(8,128)(2,1)} %get-tuple-element.162.grad_mid_ref, ...), custom_call_target="tpu_custom_call" | custom-call | tf_op jit(solution)/shard_map/reduce_dense/pallas_call | solution.py:1424
  1308.0 0.8 reshape.119
  1308.7 0.6 pad_maximum_fusion.5
  1309.3 0.6 pad_maximum_fusion.4
  1309.9 1.8 pad_maximum_fusion.1
  1311.7 1.9 pad_maximum_fusion
  1313.7 8.1 order_grads.3
  1321.8 1.1 copy.65
  (36 shorter events, 0.3 us)
Async XLA Ops:
  91.1 2.5 copy-start.7
  91.1 5.1 copy-start.8
  91.1 5.1 copy-start.9
  603.2 212.7 %copy-start.2 = (bf16[256,1536]{1,0:T(8,128)(2,1)S(1)}, bf16[256,1536]{1,0:T(8,128)(2,1)}, u32[]{:S(2)}) copy-start(bf16[256,1536]{1,0:T(8,128)(2,1)} %refs_0_) | copy-start | bytes 2359300
  799.3 333.4 %collective-permute-start = (bf16[3,192,1536]{2,1,0:T(8,128)(2,1)}, bf16[3,192,1536]{2,1,0:T(8,128)(2,1)}, u32[]{:S(2)}, u32[]{:S(2)}) collective-permute-start(bf16[3,192,1536]{2,1,0:T(8,128)(2,1)} %get-tuple-element.143), channel_id=1, source_target_pairs={{0,24},{8,0},{16,8},{24,16},{1,25},{9,1},{17,9},{25,17},{2,26},{10... | collective-permute-start | bytes 5308424 | tf_op jit(solution)/shard_map/ppermute | solution.py:2129
  813.4 327.2 %collective-permute-start.1 = (bf16[3,192,1536]{2,1,0:T(8,128)(2,1)}, bf16[3,192,1536]{2,1,0:T(8,128)(2,1)}, u32[]{:S(2)}, u32[]{:S(2)}) collective-permute-start(bf16[3,192,1536]{2,1,0:T(8,128)(2,1)} %get-tuple-element.144), channel_id=1, source_target_pairs={{0,16},{8,24},{16,0},{24,8},{1,17},{9,25},{17,1},{25,9},{2,18},{10... | collective-permute-start | bytes 5308424 | tf_op jit(solution)/shard_map/ppermute | solution.py:2129
  813.4 327.2 %collective-permute-start.2 = (bf16[3,192,1536]{2,1,0:T(8,128)(2,1)}, bf16[3,192,1536]{2,1,0:T(8,128)(2,1)}, u32[]{:S(2)}, u32[]{:S(2)}) collective-permute-start(bf16[3,192,1536]{2,1,0:T(8,128)(2,1)} %get-tuple-element.145), channel_id=1, source_target_pairs={{0,8},{8,16},{16,24},{24,0},{1,9},{9,17},{17,25},{25,1},{2,10},{10... | collective-permute-start | bytes 5308424 | tf_op jit(solution)/shard_map/ppermute | solution.py:2129
  817.2 51.9 %copy-start.6 = (f32[32,1536]{1,0:T(8,128)S(1)}, f32[32,1536]{1,0:T(8,128)}, u32[]{:S(2)}) copy-start(f32[32,1536]{1,0:T(8,128)} %get-tuple-element.127) | copy-start | bytes 589828
  870.1 76.4 %copy-start.1 = (f32[256,1536]{1,0:T(8,128)S(1)}, f32[256,1536]{1,0:T(8,128)}, u32[]{:S(2)}) copy-start(f32[256,1536]{1,0:T(8,128)} %get-tuple-element.133.incoming_ref) | copy-start | bytes 4718596
  947.4 190.4 %copy-start = (f32[256,1536]{1,0:T(8,128)S(1)}, f32[256,1536]{1,0:T(8,128)}, u32[]{:S(2)}) copy-start(f32[256,1536]{1,0:T(8,128)} %get-tuple-element.108.mid_ref) | copy-start | bytes 4718596
  1118.8 194.9 %collective-permute-start.3 = (bf16[3,192,1536]{2,1,0:T(8,128)(2,1)}, bf16[3,192,1536]{2,1,0:T(8,128)(2,1)}, u32[]{:S(2)}, u32[]{:S(2)}) collective-permute-start(bf16[3,192,1536]{2,1,0:T(8,128)(2,1)} %get-tuple-element.173), channel_id=1, source_target_pairs={{0,24},{8,0},{16,8},{24,16},{1,25},{9,1},{17,9},{25,17},{2,26},{10... | collective-permute-start | bytes 5308424 | tf_op jit(solution)/shard_map/ppermute | solution.py:2129
  1132.7 181.0 %collective-permute-start.4 = (bf16[3,192,1536]{2,1,0:T(8,128)(2,1)}, bf16[3,192,1536]{2,1,0:T(8,128)(2,1)}, u32[]{:S(2)}, u32[]{:S(2)}) collective-permute-start(bf16[3,192,1536]{2,1,0:T(8,128)(2,1)} %get-tuple-element.174), channel_id=1, source_target_pairs={{0,16},{8,24},{16,0},{24,8},{1,17},{9,25},{17,1},{25,9},{2,18},{10... | collective-permute-start | bytes 5308424 | tf_op jit(solution)/shard_map/ppermute | solution.py:2129
  1132.7 181.0 %collective-permute-start.5 = (bf16[3,192,1536]{2,1,0:T(8,128)(2,1)}, bf16[3,192,1536]{2,1,0:T(8,128)(2,1)}, u32[]{:S(2)}, u32[]{:S(2)}) collective-permute-start(bf16[3,192,1536]{2,1,0:T(8,128)(2,1)} %get-tuple-element.175), channel_id=1, source_target_pairs={{0,8},{8,16},{16,24},{24,0},{1,9},{9,17},{17,25},{25,1},{2,10},{10... | collective-permute-start | bytes 5308424 | tf_op jit(solution)/shard_map/ppermute | solution.py:2129
  1206.4 103.5 %copy-start.5 = (f32[192,384]{1,0:T(8,128)S(1)}, f32[192,384]{1,0:T(8,128)}, u32[]{:S(2)}) copy-start(f32[192,384]{1,0:T(8,128)} %get-tuple-element.171) | copy-start | bytes 884740
  1207.1 104.7 %copy-start.4 = (f32[384,256]{1,0:T(8,128)S(1)}, f32[384,256]{1,0:T(8,128)}, u32[]{:S(2)}) copy-start(f32[384,256]{1,0:T(8,128)} %get-tuple-element.169) | copy-start | bytes 1179652
  1313.7 8.1 copy-start.3
